TPU v7x, 512 devices: a whole 4x4x16 slice. The times are simulated.
512 devices in a mesh: seq: 128 (over y, z, core), head: 4 (over x).
Axes of the slice: x: 4, y: 4, z: 16, core: 2. Of those that a mesh axis runs over, the one named last changes fastest.
Arguments:
- query_rows: bfloat16 [16384, 512], P('seq', 'head'), may hold values from -6 to 6
- key_rows: bfloat16 [16384, 512], P('seq', 'head'), may hold values from -6 to 6
- value_rows: bfloat16 [16384, 512], P('seq', 'head'), may hold values from -6 to 6
- gate_rows: bfloat16 [16384, 512], P('seq', 'head'), may hold values from -6 to 6
- cotangent: bfloat16 [16384, 512], P('seq', 'head'), may hold values from -6 to 6
- event_gaps: int32 [16384], P('seq'), may hold values from 0 to 7
- block_lists: int32 [128, 8], replicated, may hold values from -1 to 126, as said below
- bias_table: float32 [8, 16], P('head'), may hold values from -1 to 1
- norm_gain: float32 [512], P('head'), may hold values from 0.1 to 1.9
Outputs:
- layer_out: bfloat16 [16384, 512], P('seq', 'head')
- grad_query: bfloat16 [16384, 512], P('seq', 'head')
- grad_key: bfloat16 [16384, 512], P('seq', 'head')
- grad_value: bfloat16 [16384, 512], P('seq', 'head')
- grad_gate: bfloat16 [16384, 512], P('seq', 'head')
Inputs may be any that keep to these rules, and one draw needn't show every extreme that they name: `block_lists`: slot s of row c holds either c - 2**s or -1; it holds -1 wherever 2**s >= 128 or 2**s > c. The last row lists every group c - 2**s that exists.
All inputs are finite; a program needn't handle non-finite values.
Results may differ from a plain program's by a relative error of at most 0.01.
Values may be sent and summed in bfloat16 or wider, within the bound.
No kernel may reach another device: no remote copies, remote signals or barrier semaphores. Data moves between devices by JAX's collectives and lax.ppermute only.
A program may use at most 64 MiB of HBM per device.

v0:
```python
import jax
import jax.numpy as jnp
from jax import lax
from jax.sharding import PartitionSpec as P

norm_eps = 1e-05


def prefix(x, axis, combine, identity):
    length, index = (lax.axis_size(axis), lax.axis_index(axis))
    everything = lax.all_gather(x, axis)
    start = jnp.broadcast_to(jnp.asarray(identity, x.dtype), x.shape)

    def step(k, before):
        reached = k < index
        new = combine(before, everything[k])
        return jnp.where(reached, new, before)

    return lax.fori_loop(0, length, step, start)


def shifted(x, axis, by):
    length = lax.axis_size(axis)
    pairs = [(i, i + by) for i in range(length) if 0 <= i + by < length]
    return lax.ppermute(x, axis, pairs)


def bucket_bias(delta, table):
    bias = jnp.zeros((table.shape[0],) + delta.shape, jnp.float32) + table[:, 0][:, None, None]
    for bucket_id in range(1, table.shape[1]):
        increment = (table[:, bucket_id] - table[:, bucket_id - 1])[:, None, None]
        reached = (delta >= 2 ** (bucket_id - 1)).astype(jnp.float32)
        bias = bias + increment * reached[None]
    return bias


def causal_mask(length):
    later_ids = lax.broadcasted_iota(jnp.int32, (length, length), 1)
    early_ids = lax.broadcasted_iota(jnp.int32, (length, length), 0)
    return (later_ids <= early_ids).astype(jnp.float32)


def add_counts(earlier, later):
    return earlier + later


def block_scores(query_heads, key_heads, query_times, key_times, table, scaling):
    scores = (
        jnp.einsum("qhd,khd->hqk", query_heads, key_heads, preferred_element_type=jnp.float32)
        * scaling
    )
    return scores + bucket_bias(query_times[:, None] - key_times[None, :], table)


def attend_block(
    running, query_heads, key_heads, value_heads, query_times, key_times, table, scaling, keep_mask
):
    weights = jax.nn.silu(
        block_scores(query_heads, key_heads, query_times, key_times, table, scaling)
    )
    if keep_mask is not None:
        weights = weights * keep_mask[None]
    weights = weights.astype(jnp.bfloat16)
    return running + jnp.einsum(
        "hqk,khd->qhd", weights, value_heads, preferred_element_type=jnp.float32
    )


def block_slopes(
    query_heads,
    key_heads,
    value_heads,
    grad_heads,
    query_times,
    key_times,
    table,
    scaling,
    keep_mask,
):
    scores = block_scores(query_heads, key_heads, query_times, key_times, table, scaling)
    sigmoid_val = jax.nn.sigmoid(scores)
    weights = jax.nn.silu(scores)
    slope = sigmoid_val * (1.0 + scores * (1.0 - sigmoid_val))
    grad_weights = jnp.einsum(
        "qhd,khd->hqk", grad_heads, value_heads, preferred_element_type=jnp.float32
    )
    grad_scores = grad_weights * slope
    if keep_mask is not None:
        weights = weights * keep_mask[None]
        grad_scores = grad_scores * keep_mask[None]
    return (weights.astype(jnp.bfloat16), grad_scores.astype(jnp.bfloat16))


def skip_block(running):
    return running


def per_device(
    query_rows,
    key_rows,
    value_rows,
    gate_rows,
    cotangent,
    event_gaps,
    block_lists,
    bias_table,
    norm_gain,
):
    row_count = query_rows.shape[0]
    feature_dim = query_rows.shape[1]
    head_count = bias_table.shape[0]
    head_dim = feature_dim // head_count
    scaling = head_dim ** (-0.5)
    full_width = feature_dim * lax.axis_size("head")
    seq_count = lax.axis_size("seq")
    group_id = lax.axis_index("seq")

    def split_heads(flat_rows):
        return flat_rows.reshape(flat_rows.shape[0], head_count, head_dim)

    local_times = jnp.cumsum(event_gaps)
    before = prefix(local_times[-1], "seq", add_counts, jnp.int32(0))
    event_times = local_times + before
    query_heads = split_heads(query_rows)
    key_heads = split_heads(key_rows)
    value_heads = split_heads(value_rows)
    diagonal = causal_mask(row_count)
    my_entries = lax.dynamic_index_in_dim(block_lists, group_id, 0, keepdims=False)
    offsets = [
        (slot_id, 2**slot_id) for slot_id in range(block_lists.shape[1]) if 2**slot_id < seq_count
    ]
    attended = attend_block(
        jnp.zeros(query_heads.shape, jnp.float32),
        query_heads,
        key_heads,
        value_heads,
        event_times,
        event_times,
        bias_table,
        scaling,
        diagonal,
    )
    kept = []
    for slot_id, distance in offsets:
        fetched = shifted((key_rows, value_rows, event_times), "seq", distance)
        kept.append(fetched)

        def add_remote(running, fetched=fetched):
            return attend_block(
                running,
                query_heads,
                split_heads(fetched[0]),
                split_heads(fetched[1]),
                event_times,
                fetched[2],
                bias_table,
                scaling,
                None,
            )

        attended = lax.cond(my_entries[slot_id] >= 0, add_remote, skip_block, attended)
    flat = attended.reshape(row_count, feature_dim)
    norm_sums = lax.psum((jnp.sum(flat, axis=1), jnp.sum(flat * flat, axis=1)), "head")
    row_mean = norm_sums[0] / full_width
    row_var = norm_sums[1] / full_width - row_mean * row_mean
    inv_std = lax.rsqrt(row_var + norm_eps)
    centered = (flat - row_mean[:, None]) * inv_std[:, None]
    normed = centered * norm_gain[None, :]
    gates = gate_rows.astype(jnp.float32)
    upstream = cotangent.astype(jnp.float32)
    layer_out = (normed * gates).astype(jnp.bfloat16)
    grad_gate = (upstream * normed).astype(jnp.bfloat16)
    scaled = upstream * gates * norm_gain[None, :]
    grad_sums = lax.psum((jnp.sum(scaled, axis=1), jnp.sum(scaled * centered, axis=1)), "head")
    grad_attended = inv_std[:, None] * (
        scaled - grad_sums[0][:, None] / full_width - centered * grad_sums[1][:, None] / full_width
    )
    grad_flat = grad_attended.astype(jnp.bfloat16)
    grad_heads = split_heads(grad_flat)
    weights, grad_scores = block_slopes(
        query_heads,
        key_heads,
        value_heads,
        grad_heads,
        event_times,
        event_times,
        bias_table,
        scaling,
        diagonal,
    )
    grad_query = (
        jnp.einsum("hqk,khd->qhd", grad_scores, key_heads, preferred_element_type=jnp.float32)
        * scaling
    )
    key_grad = (
        jnp.einsum("hqk,qhd->khd", grad_scores, query_heads, preferred_element_type=jnp.float32)
        * scaling
    )
    value_grad = jnp.einsum("hqk,qhd->khd", weights, grad_heads, preferred_element_type=jnp.float32)
    empty_heads = jnp.zeros(query_heads.shape, jnp.float32)
    for position, (slot_id, distance) in enumerate(offsets):
        fetched = kept[position]
        listed = my_entries[slot_id] >= 0
        remote_keys = split_heads(fetched[0])
        remote_values = split_heads(fetched[1])
        remote_times = fetched[2]

        def remote_grads(
            unused, remote_keys=remote_keys, remote_values=remote_values, remote_times=remote_times
        ):
            block_weights, block_grads = block_slopes(
                query_heads,
                remote_keys,
                remote_values,
                grad_heads,
                event_times,
                remote_times,
                bias_table,
                scaling,
                None,
            )
            query_part = (
                jnp.einsum(
                    "hqk,khd->qhd", block_grads, remote_keys, preferred_element_type=jnp.float32
                )
                * scaling
            )
            key_part = (
                jnp.einsum(
                    "hqk,qhd->khd", block_grads, query_heads, preferred_element_type=jnp.float32
                )
                * scaling
            )
            value_part = jnp.einsum(
                "hqk,qhd->khd", block_weights, grad_heads, preferred_element_type=jnp.float32
            )
            return (query_part, key_part, value_part)

        def no_grads(unused):
            return (empty_heads, empty_heads, empty_heads)

        query_part, key_part, value_part = lax.cond(listed, remote_grads, no_grads, jnp.int32(0))
        grad_query = grad_query + query_part
        returned = (
            shifted(key_part.astype(jnp.bfloat16), "seq", -distance).astype(key_part.dtype),
            shifted(value_part.astype(jnp.bfloat16), "seq", -distance).astype(value_part.dtype),
        )
        key_grad = key_grad + returned[0]
        value_grad = value_grad + returned[1]
    grad_query_out = grad_query.reshape(row_count, feature_dim).astype(jnp.bfloat16)
    grad_key_out = key_grad.reshape(row_count, feature_dim).astype(jnp.bfloat16)
    grad_value_out = value_grad.reshape(row_count, feature_dim).astype(jnp.bfloat16)
    return (layer_out, grad_query_out, grad_key_out, grad_value_out, grad_gate)


def solution(mesh):
    placed = (
        P("seq", "head"),
        P("seq", "head"),
        P("seq", "head"),
        P("seq", "head"),
        P("seq", "head"),
        P("seq"),
        P(),
        P("head", None),
        P("head"),
    )
    return jax.shard_map(
        per_device,
        mesh=mesh,
        in_specs=placed,
        out_specs=(
            P("seq", "head"),
            P("seq", "head"),
            P("seq", "head"),
            P("seq", "head"),
            P("seq", "head"),
        ),
        check_vma=False,
    )
```

profile of v0, /device:TPU:58, one launch (start us, length us, event | category | flops | bytes accessed | tf_op | source)
XLA Modules:
  0.0 372.5 jit_solution(15131667518954767041)
XLA Ops:
  3.4 1.3 bitcast_dynamic-update-slice_fusion
  4.7 30.9 %all-reduce = s32[128]{0:T(128)S(1)} all-reduce(s32[128]{0:T(128)S(1)} %bitcast_dynamic-update-slice_fusion), channel_id=2, replica_groups=mesh['seq'=128,'head'=4] {'seq'}, use_global_device_ids=true, to_apply=%add | all-reduce | flops 128 | bytes 1024 | tf_op jit(solution)/shard_map/all_gather | solution.py:11
  35.6 162.1 %while.13 = (s32[]{:T(128)}, s32[]{:T(128)}, s32[]{:T(128)}, s32[128]{0:T(128)S(1)}, s32[]{:T(128)}) while((s32[]{:T(128)}, s32[]{:T(128)}, s32[]{:T(128)}, s32[128]{0:T(128)S(1)}, s32[]{:T(128)}) %tuple.614), condition=%wide.region_2.3_spmd, body=%wide.region_1.2_spmd.sunk | while | flops 5 | bytes 115 | solution.py:19
  197.8 1.3 collective-permute-start.16
  199.1 6.2 %collective-permute-start.13 = (s32[128]{0:T(128)S(1)}, s32[128]{0:T(128)S(1)}, u32[]{:S(2)}, u32[]{:S(2)}) collective-permute-start(s32[128]{0:T(128)S(1)} %add_reduce_fusion), channel_id=1, source_target_pairs={{0,64},{4,68},{8,72},{12,76},{16,80},{20,84},{24,88},{28,92},{32,9... | collective-permute-start | bytes 1544 | tf_op jit(solution)/shard_map/ppermute | solution.py:25
  205.3 1.9 collective-permute-start.10
  207.2 2.6 collective-permute-start.7
  209.9 1.9 collective-permute-start.4
  214.8 1.9 collective-permute-start.14
  216.7 2.9 collective-permute-start.11
  219.6 3.4 collective-permute-start.8
  223.0 1.9 collective-permute-start.5
  225.0 1.9 collective-permute-start.1
  227.0 2.8 collective-permute-done.1
  229.8 1.9 collective-permute-start.2
  231.7 1.9 collective-permute-start.9
  233.7 2.0 collective-permute-start.6
  235.7 4.1 %collective-permute-start.3 = (bf16[128,128]{0,1:T(8,128)(2,1)S(1)}, bf16[128,128]{0,1:T(8,128)(2,1)S(1)}, u32[]{:S(2)}, u32[]{:S(2)}) collective-permute-start(bf16[128,128]{0,1:T(8,128)(2,1)S(1)} %copy.62), channel_id=1, source_target_pairs={{0,8},{4,12},{8,16},{12,20},{16,24},{20,28},{24,32},{28,36},{32,40... | collective-permute-start | bytes 98312 | tf_op jit(solution)/shard_map/ppermute | solution.py:25
  239.9 1.9 collective-permute-start
  241.9 1.4 collective-permute-start.20
  243.3 1.3 collective-permute-start.17
  244.6 1.3 collective-permute-start.18
  245.9 1.3 collective-permute-start.15
  247.3 1.9 collective-permute-start.12
  257.5 8.9 %collective-permute-done.12 = bf16[128,128]{0,1:T(8,128)(2,1)S(1)} collective-permute-done((bf16[128,128]{0,1:T(8,128)(2,1)S(1)}, bf16[128,128]{0,1:T(8,128)(2,1)S(1)}, u32[]{:S(2)}, u32[]{:S(2)}) %collective-permute-start.12) | collective-permute-done | bytes 32800 | tf_op jit(solution)/shard_map/ppermute | solution.py:25
  266.4 1.3 collective-permute-start.19
  270.0 20.8 %collective-permute-done.19 = s32[128]{0:T(128)S(1)} collective-permute-done((s32[128]{0:T(128)S(1)}, s32[128]{0:T(128)S(1)}, u32[]{:S(2)}, u32[]{:S(2)}) %collective-permute-start.19) | collective-permute-done | bytes 544 | tf_op jit(solution)/shard_map/ppermute | solution.py:25
  291.6 8.6 %all-reduce.2 = (f32[128]{0:T(128)S(1)}, f32[128]{0:T(128)S(1)}) all-reduce(f32[128]{0:T(128)S(1)} %get-tuple-element.672, f32[128]{0:T(128)S(1)} %get-tuple-element.671), channel_id=1, replica_groups=mesh['seq'=128,'head'=4] {'head'}, use_global_device_ids=true, to_apply=%region_20.21 | all-reduce | flops 256 | bytes 2048 | tf_op jit(solution)/shard_map/psum | solution.py:163
  300.9 10.1 %all-reduce.1 = (f32[128]{0:T(128)S(1)}, f32[128]{0:T(128)S(1)}) all-reduce(f32[128]{0:T(128)S(1)} %get-tuple-element.670, f32[128]{0:T(128)S(1)} %get-tuple-element.669), channel_id=1, replica_groups=mesh['seq'=128,'head'=4] {'head'}, use_global_device_ids=true, to_apply=%region_24.25 | all-reduce | flops 256 | bytes 2048 | tf_op jit(solution)/shard_map/psum | solution.py:174
  311.6 1.3 conditional.21
  312.9 1.9 collective-permute-start.28
  314.8 1.9 collective-permute-start.21
  318.1 1.9 collective-permute-start.29
  320.0 2.8 collective-permute-start.22
  322.8 1.3 conditional.23
  324.1 3.5 collective-permute-start.30
  327.6 1.3 conditional.24
  330.2 1.3 conditional.26
  333.0 4.2 %collective-permute-start.31 = (bf16[128,2,64]{0,2,1:T(8,128)(2,1)S(1)}, bf16[128,2,64]{0,2,1:T(8,128)(2,1)S(1)}, u32[]{:S(2)}, u32[]{:S(2)}) collective-permute-start(bf16[128,2,64]{0,2,1:T(8,128)(2,1)S(1)} %convert_element_type.1895), channel_id=1, source_target_pairs={{32,0},{36,4},{40,8},{44,12},{48,16},{52,20},{56,24},{60,28},{64,3... | collective-permute-start | bytes 98312 | tf_op jit(solution)/shard_map/ppermute | solution.py:25
  337.2 5.6 %collective-permute-start.32 = (bf16[128,2,64]{0,2,1:T(8,128)(2,1)S(1)}, bf16[128,2,64]{0,2,1:T(8,128)(2,1)S(1)}, u32[]{:S(2)}, u32[]{:S(2)}) collective-permute-start(bf16[128,2,64]{0,2,1:T(8,128)(2,1)S(1)} %convert_element_type.1897), channel_id=1, source_target_pairs={{64,0},{68,4},{72,8},{76,12},{80,16},{84,20},{88,24},{92,28},{96,3... | collective-permute-start | bytes 98312 | tf_op jit(solution)/shard_map/ppermute | solution.py:25
  342.8 3.1 collective-permute-start.33
  345.9 1.3 collective-permute-start.34
  349.6 2.6 collective-permute-start.23
  352.2 5.0 %collective-permute-start.24 = (bf16[128,2,64]{0,2,1:T(8,128)(2,1)S(1)}, bf16[128,2,64]{0,2,1:T(8,128)(2,1)S(1)}, u32[]{:S(2)}, u32[]{:S(2)}) collective-permute-start(bf16[128,2,64]{0,2,1:T(8,128)(2,1)S(1)} %convert_element_type.1879), channel_id=1, source_target_pairs={{32,0},{36,4},{40,8},{44,12},{48,16},{52,20},{56,24},{60,28},{64,3... | collective-permute-start | bytes 98312 | tf_op jit(solution)/shard_map/ppermute | solution.py:25
  357.2 5.2 %collective-permute-start.25 = (bf16[128,2,64]{0,2,1:T(8,128)(2,1)S(1)}, bf16[128,2,64]{0,2,1:T(8,128)(2,1)S(1)}, u32[]{:S(2)}, u32[]{:S(2)}) collective-permute-start(bf16[128,2,64]{0,2,1:T(8,128)(2,1)S(1)} %convert_element_type.1881), channel_id=1, source_target_pairs={{64,0},{68,4},{72,8},{76,12},{80,16},{84,20},{88,24},{92,28},{96,3... | collective-permute-start | bytes 98312 | tf_op jit(solution)/shard_map/ppermute | solution.py:25
  362.4 1.9 collective-permute-start.26
  364.4 1.3 collective-permute-start.27
  366.4 5.3 %collective-permute-done.25 = bf16[128,2,64]{0,2,1:T(8,128)(2,1)S(1)} collective-permute-done((bf16[128,2,64]{0,2,1:T(8,128)(2,1)S(1)}, bf16[128,2,64]{0,2,1:T(8,128)(2,1)S(1)}, u32[]{:S(2)}, u32[]{:S(2)}) %collective-permute-start.25) | collective-permute-done | bytes 32800 | tf_op jit(solution)/shard_map/ppermute | solution.py:25
  (349 shorter events, 110.6 us)
Async XLA Ops:
  0.6 241.2 %copy-start = (s32[128,8]{0,1:T(8,128)S(1)}, s32[128,8]{0,1:T(8,128)}, u32[]{:S(2)}) copy-start(s32[128,8]{0,1:T(8,128)} %param.45) | copy-start | bytes 12292
  0.7 0.7 copy-start.8
  197.8 16.9 %collective-permute-start.16 = (s32[128]{0:T(128)S(1)}, s32[128]{0:T(128)S(1)}, u32[]{:S(2)}, u32[]{:S(2)}) collective-permute-start(s32[128]{0:T(128)S(1)} %add_reduce_fusion), channel_id=1, source_target_pairs={{0,128},{4,132},{8,136},{12,140},{16,144},{20,148},{24,152},{28,15... | collective-permute-start | bytes 1544 | tf_op jit(solution)/shard_map/ppermute | solution.py:25
  199.1 17.6 %collective-permute-start.13 = (s32[128]{0:T(128)S(1)}, s32[128]{0:T(128)S(1)}, u32[]{:S(2)}, u32[]{:S(2)}) collective-permute-start(s32[128]{0:T(128)S(1)} %add_reduce_fusion), channel_id=1, source_target_pairs={{0,64},{4,68},{8,72},{12,76},{16,80},{20,84},{24,88},{28,92},{32,9... | collective-permute-start | bytes 1544 | tf_op jit(solution)/shard_map/ppermute | solution.py:25
  205.3 14.3 %collective-permute-start.10 = (s32[128]{0:T(128)S(1)}, s32[128]{0:T(128)S(1)}, u32[]{:S(2)}, u32[]{:S(2)}) collective-permute-start(s32[128]{0:T(128)S(1)} %add_reduce_fusion), channel_id=1, source_target_pairs={{0,32},{4,36},{8,40},{12,44},{16,48},{20,52},{24,56},{28,60},{32,6... | collective-permute-start | bytes 1544 | tf_op jit(solution)/shard_map/ppermute | solution.py:25
  207.2 15.8 %collective-permute-start.7 = (s32[128]{0:T(128)S(1)}, s32[128]{0:T(128)S(1)}, u32[]{:S(2)}, u32[]{:S(2)}) collective-permute-start(s32[128]{0:T(128)S(1)} %add_reduce_fusion), channel_id=1, source_target_pairs={{0,16},{4,20},{8,24},{12,28},{16,32},{20,36},{24,40},{28,44},{32,4... | collective-permute-start | bytes 1544 | tf_op jit(solution)/shard_map/ppermute | solution.py:25
  209.9 15.1 %collective-permute-start.4 = (s32[128]{0:T(128)S(1)}, s32[128]{0:T(128)S(1)}, u32[]{:S(2)}, u32[]{:S(2)}) collective-permute-start(s32[128]{0:T(128)S(1)} %add_reduce_fusion), channel_id=1, source_target_pairs={{0,8},{4,12},{8,16},{12,20},{16,24},{20,28},{24,32},{28,36},{32,40... | collective-permute-start | bytes 1544 | tf_op jit(solution)/shard_map/ppermute | solution.py:25
  211.8 0.7 copy-start.1
  211.8 1.1 copy-start.2
  213.0 0.8 copy-start.3
  213.9 0.8 copy-start.4
  214.8 17.0 %collective-permute-start.14 = (bf16[128,128]{0,1:T(8,128)(2,1)S(1)}, bf16[128,128]{0,1:T(8,128)(2,1)S(1)}, u32[]{:S(2)}, u32[]{:S(2)}) collective-permute-start(bf16[128,128]{0,1:T(8,128)(2,1)S(1)} %copy.64), channel_id=1, source_target_pairs={{0,64},{4,68},{8,72},{12,76},{16,80},{20,84},{24,88},{28,92},{32,9... | collective-permute-start | bytes 98312 | tf_op jit(solution)/shard_map/ppermute | solution.py:25
  216.7 17.0 %collective-permute-start.11 = (bf16[128,128]{0,1:T(8,128)(2,1)S(1)}, bf16[128,128]{0,1:T(8,128)(2,1)S(1)}, u32[]{:S(2)}, u32[]{:S(2)}) collective-permute-start(bf16[128,128]{0,1:T(8,128)(2,1)S(1)} %copy.64), channel_id=1, source_target_pairs={{0,32},{4,36},{8,40},{12,44},{16,48},{20,52},{24,56},{28,60},{32,6... | collective-permute-start | bytes 98312 | tf_op jit(solution)/shard_map/ppermute | solution.py:25
  219.6 16.1 %collective-permute-start.8 = (bf16[128,128]{0,1:T(8,128)(2,1)S(1)}, bf16[128,128]{0,1:T(8,128)(2,1)S(1)}, u32[]{:S(2)}, u32[]{:S(2)}) collective-permute-start(bf16[128,128]{0,1:T(8,128)(2,1)S(1)} %copy.64), channel_id=1, source_target_pairs={{0,16},{4,20},{8,24},{12,28},{16,32},{20,36},{24,40},{28,44},{32,4... | collective-permute-start | bytes 98312 | tf_op jit(solution)/shard_map/ppermute | solution.py:25
  223.0 16.8 %collective-permute-start.5 = (bf16[128,128]{0,1:T(8,128)(2,1)S(1)}, bf16[128,128]{0,1:T(8,128)(2,1)S(1)}, u32[]{:S(2)}, u32[]{:S(2)}) collective-permute-start(bf16[128,128]{0,1:T(8,128)(2,1)S(1)} %copy.64), channel_id=1, source_target_pairs={{0,8},{4,12},{8,16},{12,20},{16,24},{20,28},{24,32},{28,36},{32,40... | collective-permute-start | bytes 98312 | tf_op jit(solution)/shard_map/ppermute | solution.py:25
  225.0 4.9 %collective-permute-start.1 = (s32[128]{0:T(128)S(1)}, s32[128]{0:T(128)S(1)}, u32[]{:S(2)}, u32[]{:S(2)}) collective-permute-start(s32[128]{0:T(128)S(1)} %add_reduce_fusion), channel_id=1, source_target_pairs={{0,4},{4,8},{8,12},{12,16},{16,20},{20,24},{24,28},{28,32},{32,36}... | collective-permute-start | bytes 1544 | tf_op jit(solution)/shard_map/ppermute | solution.py:25
  229.8 12.1 %collective-permute-start.2 = (bf16[128,128]{0,1:T(8,128)(2,1)S(1)}, bf16[128,128]{0,1:T(8,128)(2,1)S(1)}, u32[]{:S(2)}, u32[]{:S(2)}) collective-permute-start(bf16[128,128]{0,1:T(8,128)(2,1)S(1)} %copy.64), channel_id=1, source_target_pairs={{0,4},{4,8},{8,12},{12,16},{16,20},{20,24},{24,28},{28,32},{32,36}... | collective-permute-start | bytes 98312 | tf_op jit(solution)/shard_map/ppermute | solution.py:25
  231.7 11.6 %collective-permute-start.9 = (bf16[128,128]{0,1:T(8,128)(2,1)S(1)}, bf16[128,128]{0,1:T(8,128)(2,1)S(1)}, u32[]{:S(2)}, u32[]{:S(2)}) collective-permute-start(bf16[128,128]{0,1:T(8,128)(2,1)S(1)} %copy.62), channel_id=1, source_target_pairs={{0,32},{4,36},{8,40},{12,44},{16,48},{20,52},{24,56},{28,60},{32,6... | collective-permute-start | bytes 98312 | tf_op jit(solution)/shard_map/ppermute | solution.py:25
  233.7 10.9 %collective-permute-start.6 = (bf16[128,128]{0,1:T(8,128)(2,1)S(1)}, bf16[128,128]{0,1:T(8,128)(2,1)S(1)}, u32[]{:S(2)}, u32[]{:S(2)}) collective-permute-start(bf16[128,128]{0,1:T(8,128)(2,1)S(1)} %copy.62), channel_id=1, source_target_pairs={{0,16},{4,20},{8,24},{12,28},{16,32},{20,36},{24,40},{28,44},{32,4... | collective-permute-start | bytes 98312 | tf_op jit(solution)/shard_map/ppermute | solution.py:25
  235.7 10.2 %collective-permute-start.3 = (bf16[128,128]{0,1:T(8,128)(2,1)S(1)}, bf16[128,128]{0,1:T(8,128)(2,1)S(1)}, u32[]{:S(2)}, u32[]{:S(2)}) collective-permute-start(bf16[128,128]{0,1:T(8,128)(2,1)S(1)} %copy.62), channel_id=1, source_target_pairs={{0,8},{4,12},{8,16},{12,20},{16,24},{20,28},{24,32},{28,36},{32,40... | collective-permute-start | bytes 98312 | tf_op jit(solution)/shard_map/ppermute | solution.py:25
  239.9 7.4 %collective-permute-start = (bf16[128,128]{0,1:T(8,128)(2,1)S(1)}, bf16[128,128]{0,1:T(8,128)(2,1)S(1)}, u32[]{:S(2)}, u32[]{:S(2)}) collective-permute-start(bf16[128,128]{0,1:T(8,128)(2,1)S(1)} %copy.62), channel_id=1, source_target_pairs={{0,4},{4,8},{8,12},{12,16},{16,20},{20,24},{24,28},{28,32},{32,36}... | collective-permute-start | bytes 98312 | tf_op jit(solution)/shard_map/ppermute | solution.py:25
  241.9 12.4 %copy-start.5 = (bf16[128,128]{1,0:T(8,128)(2,1)S(1)}, bf16[128,128]{1,0:T(8,128)(2,1)}, u32[]{:S(2)}) copy-start(bf16[128,128]{1,0:T(8,128)(2,1)} %param.42) | copy-start | bytes 98308
  241.9 48.9 %collective-permute-start.20 = (bf16[128,128]{0,1:T(8,128)(2,1)S(1)}, bf16[128,128]{0,1:T(8,128)(2,1)S(1)}, u32[]{:S(2)}, u32[]{:S(2)}) collective-permute-start(bf16[128,128]{0,1:T(8,128)(2,1)S(1)} %copy.64), channel_id=1, source_target_pairs={{0,256},{4,260},{8,264},{12,268},{16,272},{20,276},{24,280},{28,28... | collective-permute-start | bytes 98312 | tf_op jit(solution)/shard_map/ppermute | solution.py:25
  243.3 25.9 %collective-permute-start.17 = (bf16[128,128]{0,1:T(8,128)(2,1)S(1)}, bf16[128,128]{0,1:T(8,128)(2,1)S(1)}, u32[]{:S(2)}, u32[]{:S(2)}) collective-permute-start(bf16[128,128]{0,1:T(8,128)(2,1)S(1)} %copy.64), channel_id=1, source_target_pairs={{0,128},{4,132},{8,136},{12,140},{16,144},{20,148},{24,152},{28,15... | collective-permute-start | bytes 98312 | tf_op jit(solution)/shard_map/ppermute | solution.py:25
  244.6 46.1 %collective-permute-start.18 = (bf16[128,128]{0,1:T(8,128)(2,1)S(1)}, bf16[128,128]{0,1:T(8,128)(2,1)S(1)}, u32[]{:S(2)}, u32[]{:S(2)}) collective-permute-start(bf16[128,128]{0,1:T(8,128)(2,1)S(1)} %copy.62), channel_id=1, source_target_pairs={{0,256},{4,260},{8,264},{12,268},{16,272},{20,276},{24,280},{28,28... | collective-permute-start | bytes 98312 | tf_op jit(solution)/shard_map/ppermute | solution.py:25
  245.9 23.2 %collective-permute-start.15 = (bf16[128,128]{0,1:T(8,128)(2,1)S(1)}, bf16[128,128]{0,1:T(8,128)(2,1)S(1)}, u32[]{:S(2)}, u32[]{:S(2)}) collective-permute-start(bf16[128,128]{0,1:T(8,128)(2,1)S(1)} %copy.62), channel_id=1, source_target_pairs={{0,128},{4,132},{8,136},{12,140},{16,144},{20,148},{24,152},{28,15... | collective-permute-start | bytes 98312 | tf_op jit(solution)/shard_map/ppermute | solution.py:25
  247.3 19.1 %collective-permute-start.12 = (bf16[128,128]{0,1:T(8,128)(2,1)S(1)}, bf16[128,128]{0,1:T(8,128)(2,1)S(1)}, u32[]{:S(2)}, u32[]{:S(2)}) collective-permute-start(bf16[128,128]{0,1:T(8,128)(2,1)S(1)} %copy.62), channel_id=1, source_target_pairs={{0,64},{4,68},{8,72},{12,76},{16,80},{20,84},{24,88},{28,92},{32,9... | collective-permute-start | bytes 98312 | tf_op jit(solution)/shard_map/ppermute | solution.py:25
  254.3 0.8 copy-start.6
  266.4 24.4 %collective-permute-start.19 = (s32[128]{0:T(128)S(1)}, s32[128]{0:T(128)S(1)}, u32[]{:S(2)}, u32[]{:S(2)}) collective-permute-start(s32[128]{0:T(128)S(1)} %add_reduce_fusion), channel_id=1, source_target_pairs={{0,256},{4,260},{8,264},{12,268},{16,272},{20,276},{24,280},{28,28... | collective-permute-start | bytes 1544 | tf_op jit(solution)/shard_map/ppermute | solution.py:25
  300.2 0.7 copy-start.7
  312.9 20.1 %collective-permute-start.28 = (bf16[128,2,64]{0,2,1:T(8,128)(2,1)S(1)}, bf16[128,2,64]{0,2,1:T(8,128)(2,1)S(1)}, u32[]{:S(2)}, u32[]{:S(2)}) collective-permute-start(bf16[128,2,64]{0,2,1:T(8,128)(2,1)S(1)} %convert_element_type.1889), channel_id=1, source_target_pairs={{4,0},{8,4},{12,8},{16,12},{20,16},{24,20},{28,24},{32,28},{36,32}... | collective-permute-start | bytes 98312 | tf_op jit(solution)/shard_map/ppermute | solution.py:25
  314.8 22.4 %collective-permute-start.21 = (bf16[128,2,64]{0,2,1:T(8,128)(2,1)S(1)}, bf16[128,2,64]{0,2,1:T(8,128)(2,1)S(1)}, u32[]{:S(2)}, u32[]{:S(2)}) collective-permute-start(bf16[128,2,64]{0,2,1:T(8,128)(2,1)S(1)} %convert_element_type.1873), channel_id=1, source_target_pairs={{4,0},{8,4},{12,8},{16,12},{20,16},{24,20},{28,24},{32,28},{36,32}... | collective-permute-start | bytes 98312 | tf_op jit(solution)/shard_map/ppermute | solution.py:25
  318.1 24.7 %collective-permute-start.29 = (bf16[128,2,64]{0,2,1:T(8,128)(2,1)S(1)}, bf16[128,2,64]{0,2,1:T(8,128)(2,1)S(1)}, u32[]{:S(2)}, u32[]{:S(2)}) collective-permute-start(bf16[128,2,64]{0,2,1:T(8,128)(2,1)S(1)} %convert_element_type.1891), channel_id=1, source_target_pairs={{8,0},{12,4},{16,8},{20,12},{24,16},{28,20},{32,24},{36,28},{40,32... | collective-permute-start | bytes 98312 | tf_op jit(solution)/shard_map/ppermute | solution.py:25
  320.0 25.9 %collective-permute-start.22 = (bf16[128,2,64]{0,2,1:T(8,128)(2,1)S(1)}, bf16[128,2,64]{0,2,1:T(8,128)(2,1)S(1)}, u32[]{:S(2)}, u32[]{:S(2)}) collective-permute-start(bf16[128,2,64]{0,2,1:T(8,128)(2,1)S(1)} %convert_element_type.1875), channel_id=1, source_target_pairs={{8,0},{12,4},{16,8},{20,12},{24,16},{28,20},{32,24},{36,28},{40,32... | collective-permute-start | bytes 98312 | tf_op jit(solution)/shard_map/ppermute | solution.py:25
  324.1 25.4 %collective-permute-start.30 = (bf16[128,2,64]{0,2,1:T(8,128)(2,1)S(1)}, bf16[128,2,64]{0,2,1:T(8,128)(2,1)S(1)}, u32[]{:S(2)}, u32[]{:S(2)}) collective-permute-start(bf16[128,2,64]{0,2,1:T(8,128)(2,1)S(1)} %convert_element_type.1893), channel_id=1, source_target_pairs={{16,0},{20,4},{24,8},{28,12},{32,16},{36,20},{40,24},{44,28},{48,3... | collective-permute-start | bytes 98312 | tf_op jit(solution)/shard_map/ppermute | solution.py:25
  333.0 19.2 %collective-permute-start.31 = (bf16[128,2,64]{0,2,1:T(8,128)(2,1)S(1)}, bf16[128,2,64]{0,2,1:T(8,128)(2,1)S(1)}, u32[]{:S(2)}, u32[]{:S(2)}) collective-permute-start(bf16[128,2,64]{0,2,1:T(8,128)(2,1)S(1)} %convert_element_type.1895), channel_id=1, source_target_pairs={{32,0},{36,4},{40,8},{44,12},{48,16},{52,20},{56,24},{60,28},{64,3... | collective-permute-start | bytes 98312 | tf_op jit(solution)/shard_map/ppermute | solution.py:25
  337.2 20.0 %collective-permute-start.32 = (bf16[128,2,64]{0,2,1:T(8,128)(2,1)S(1)}, bf16[128,2,64]{0,2,1:T(8,128)(2,1)S(1)}, u32[]{:S(2)}, u32[]{:S(2)}) collective-permute-start(bf16[128,2,64]{0,2,1:T(8,128)(2,1)S(1)} %convert_element_type.1897), channel_id=1, source_target_pairs={{64,0},{68,4},{72,8},{76,12},{80,16},{84,20},{88,24},{92,28},{96,3... | collective-permute-start | bytes 98312 | tf_op jit(solution)/shard_map/ppermute | solution.py:25
  342.8 19.6 %collective-permute-start.33 = (bf16[128,2,64]{0,2,1:T(8,128)(2,1)S(1)}, bf16[128,2,64]{0,2,1:T(8,128)(2,1)S(1)}, u32[]{:S(2)}, u32[]{:S(2)}) collective-permute-start(bf16[128,2,64]{0,2,1:T(8,128)(2,1)S(1)} %convert_element_type.1899), channel_id=1, source_target_pairs={{128,0},{132,4},{136,8},{140,12},{144,16},{148,20},{152,24},{156,2... | collective-permute-start | bytes 98312 | tf_op jit(solution)/shard_map/ppermute | solution.py:25
  345.9 18.5 %collective-permute-start.34 = (bf16[128,2,64]{0,2,1:T(8,128)(2,1)S(1)}, bf16[128,2,64]{0,2,1:T(8,128)(2,1)S(1)}, u32[]{:S(2)}, u32[]{:S(2)}) collective-permute-start(bf16[128,2,64]{0,2,1:T(8,128)(2,1)S(1)} %convert_element_type.1901), channel_id=1, source_target_pairs={{256,0},{260,4},{264,8},{268,12},{272,16},{276,20},{280,24},{284,2... | collective-permute-start | bytes 98312 | tf_op jit(solution)/shard_map/ppermute | solution.py:25
  349.6 16.9 %collective-permute-start.23 = (bf16[128,2,64]{0,2,1:T(8,128)(2,1)S(1)}, bf16[128,2,64]{0,2,1:T(8,128)(2,1)S(1)}, u32[]{:S(2)}, u32[]{:S(2)}) collective-permute-start(bf16[128,2,64]{0,2,1:T(8,128)(2,1)S(1)} %convert_element_type.1877), channel_id=1, source_target_pairs={{16,0},{20,4},{24,8},{28,12},{32,16},{36,20},{40,24},{44,28},{48,3... | collective-permute-start | bytes 98312 | tf_op jit(solution)/shard_map/ppermute | solution.py:25
  352.2 14.2 %collective-permute-start.24 = (bf16[128,2,64]{0,2,1:T(8,128)(2,1)S(1)}, bf16[128,2,64]{0,2,1:T(8,128)(2,1)S(1)}, u32[]{:S(2)}, u32[]{:S(2)}) collective-permute-start(bf16[128,2,64]{0,2,1:T(8,128)(2,1)S(1)} %convert_element_type.1879), channel_id=1, source_target_pairs={{32,0},{36,4},{40,8},{44,12},{48,16},{52,20},{56,24},{60,28},{64,3... | collective-permute-start | bytes 98312 | tf_op jit(solution)/shard_map/ppermute | solution.py:25
  357.2 14.5 %collective-permute-start.25 = (bf16[128,2,64]{0,2,1:T(8,128)(2,1)S(1)}, bf16[128,2,64]{0,2,1:T(8,128)(2,1)S(1)}, u32[]{:S(2)}, u32[]{:S(2)}) collective-permute-start(bf16[128,2,64]{0,2,1:T(8,128)(2,1)S(1)} %convert_element_type.1881), channel_id=1, source_target_pairs={{64,0},{68,4},{72,8},{76,12},{80,16},{84,20},{88,24},{92,28},{96,3... | collective-permute-start | bytes 98312 | tf_op jit(solution)/shard_map/ppermute | solution.py:25
  362.4 9.3 %collective-permute-start.26 = (bf16[128,2,64]{0,2,1:T(8,128)(2,1)S(1)}, bf16[128,2,64]{0,2,1:T(8,128)(2,1)S(1)}, u32[]{:S(2)}, u32[]{:S(2)}) collective-permute-start(bf16[128,2,64]{0,2,1:T(8,128)(2,1)S(1)} %convert_element_type.1883), channel_id=1, source_target_pairs={{128,0},{132,4},{136,8},{140,12},{144,16},{148,20},{152,24},{156,2... | collective-permute-start | bytes 98312 | tf_op jit(solution)/shard_map/ppermute | solution.py:25
  364.4 7.4 %collective-permute-start.27 = (bf16[128,2,64]{0,2,1:T(8,128)(2,1)S(1)}, bf16[128,2,64]{0,2,1:T(8,128)(2,1)S(1)}, u32[]{:S(2)}, u32[]{:S(2)}) collective-permute-start(bf16[128,2,64]{0,2,1:T(8,128)(2,1)S(1)} %convert_element_type.1885), channel_id=1, source_target_pairs={{256,0},{260,4},{264,8},{268,12},{272,16},{276,20},{280,24},{284,2... | collective-permute-start | bytes 98312 | tf_op jit(solution)/shard_map/ppermute | solution.py:25
where the time goes:
time: 377 us; the launch traced here: 372 us
  starting transfers between devices  88.6 us (24%)
  local copies, waits for them, and re-layouts  88.3 us (23%)
  loops' own time  87.6 us (23%)
  blocking collectives  49.7 us (13%)
  waiting for transfers between devices  37.9 us (10%)
  matrix products  11 us (3%)
  between operations  5.96 us (2%)
    ppermute x35, starting transfers between devices, shifted(): return lax.ppermute(x, axis, pairs)  88.6 us
    another operation x1, loops' own time, prefix(): return lax.fori_loop(0, length, step, start)  87 us
    dynamic_slice x128, local copies, waits for them, and re-layouts, step(): new = combine(before, everything[k])  75 us
    ppermute x35, waiting for transfers between devices, shifted(): return lax.ppermute(x, axis, pairs)  37.9 us
    all_gather x1, blocking collectives, prefix(): everything = lax.all_gather(x, axis)  30.9 us
    unnamed x31, local copies, waits for them, and re-layouts  10.3 us
    psum x1, blocking collectives, per_device(): lax.psum((jnp.sum(scaled, axis=1), jnp.sum(scaled * centered, axis=1)), '...  10.1 us
    psum x1, blocking collectives, per_device(): lax.psum((jnp.sum(flat, axis=1), jnp.sum(flat * flat, axis=1)), 'head')  8.61 us
  transfers between devices with their start and end apart: 35, of which 4 were waited for; matrix products, arithmetic and copies ran while one was open for 5% of the time, Pallas kernels for 0%

commit v1 on v0

v1 whole, which is shorter than its diff:
```python
import jax
import jax.numpy as jnp
from jax import lax
from jax.experimental import pallas as pl
from jax.experimental.pallas import tpu as pltpu
from jax.sharding import PartitionSpec as P

norm_eps = 1e-05
C = 128
F = 128
DH = 64
DISTANCES = (1, 2, 4, 8, 16, 32, 64)
ROW = 32
PAD = 16
WIDE = 512.0
f32, bf16, i32 = jnp.float32, jnp.bfloat16, jnp.int32
VMEM = pl.BlockSpec(memory_space=pltpu.VMEM)
PARAMS = pltpu.CompilerParams(vmem_limit_bytes=40 * 1024 * 1024)


def iota(shape, dim):
    return lax.broadcasted_iota(i32, shape, dim)


def by_head(rows):
    left = iota(rows.shape, 1) < DH
    zero = jnp.zeros_like(rows)
    return jnp.concatenate([jnp.where(left, rows, zero), jnp.where(left, zero, rows)], axis=0)


def from_heads(both):
    left = iota((C, F), 1) < DH
    return jnp.where(left, both[:C], both[C:])


def dot(a, b, dims, precision=None):
    return lax.dot_general(a, b, (dims, ((), ())), preferred_element_type=f32, precision=precision)


NN, NT, TN = ((1,), (0,)), ((1,), (1,)), ((0,), (0,))


def pack_kernel(key_ref, value_ref, gaps_ref, out_ref):
    out_ref[:C, :F] = key_ref[...]
    out_ref[:C, F:] = value_ref[...]
    gaps = jnp.broadcast_to(gaps_ref[...].astype(f32), (PAD, C))
    out_ref[C:, :F] = gaps.astype(bf16)
    out_ref[C:, F:] = gaps.astype(bf16)


def forward_kernel(
    group_ref,
    query_ref,
    gate_ref,
    cot_ref,
    gain_ref,
    lists_ref,
    table_ref,
    totals_ref,
    *refs,
):
    packets, (att_ref, sums_ref, weights_ref, slopes_ref) = refs[:8], refs[8:]
    group = group_ref[0]
    place = lax.rem(group, ROW)
    queries = by_head((query_ref[...].astype(f32) * 0.125).astype(bf16))
    gaps = jnp.concatenate([p[C : C + 1, :F] for p in packets], axis=0)
    upper = (iota((C, C), 0) <= iota((C, C), 1)).astype(bf16)
    key_times = dot(gaps, upper, NN)
    lower = (iota((C, C), 1) <= iota((C, C), 0)).astype(bf16)
    query_times = dot(lower, gaps, NT)[:, :1]
    totals = totals_ref[...].reshape(ROW, C)
    back = place - iota((ROW, C), 0) + ROW * iota((ROW, C), 1)
    sums = [jnp.zeros((1, C), f32)]
    for distance in DISTANCES:
        inside = (back >= 1) & (back <= distance)
        sums.append(jnp.sum(jnp.where(inside, totals, 0.0), axis=0, keepdims=True))
    between = jnp.sum(jnp.concatenate(sums, axis=0), axis=1, keepdims=True)
    shifts = between - key_times
    listed = lists_ref[pl.ds(group, 1), :]
    tables = [jnp.broadcast_to(jnp.pad(table_ref[h : h + 1, :], ((0, 0), (0, C - 16))), (C, C)) for h in range(2)]
    acc = jnp.zeros((2 * C, F), f32)
    for b, packet in enumerate(packets):
        scores = dot(queries, packet[:C, :F], NT)
        delta = (query_times + shifts[b : b + 1, :]).astype(i32)
        bucket = jnp.minimum(32 - lax.clz(delta), 15)
        bias = jnp.concatenate([jnp.take_along_axis(t, bucket, axis=1) for t in tables], axis=0)
        scores = scores + bias
        sig = 0.5 * jnp.tanh(0.5 * scores) + 0.5
        silu = scores * sig
        slope = sig + silu * (1.0 - sig)
        if b == 0:
            keep = (iota((C, C), 1) <= iota((C, C), 0)).astype(f32)
            keep = jnp.concatenate([keep, keep], axis=0)
        else:
            keep = (listed[:, b - 1 : b] >= 0).astype(f32)
        weights = (silu * keep).astype(bf16)
        weights_ref[:, b * C : (b + 1) * C] = weights
        slopes_ref[:, b * C : (b + 1) * C] = slope * keep
        acc = acc + dot(weights, packet[:C, F:], NN)
    att = from_heads(acc)
    att_ref[...] = att
    scaled = cot_ref[...].astype(f32) * gate_ref[...].astype(f32) * gain_ref[...]
    terms = jnp.concatenate([att, att * att, scaled, scaled * att], axis=0)
    rows = dot(jnp.ones((8, F), f32), terms, NT, lax.Precision.HIGHEST)
    for r in range(4):
        sums_ref[r : r + 1, :] = rows[0:1, r * C : (r + 1) * C]


def backward_kernel(
    query_ref,
    gate_ref,
    cot_ref,
    gain_ref,
    att_ref,
    sums_ref,
    weights_ref,
    slopes_ref,
    *refs,
):
    packets, (out_ref, dq_ref, dgate_ref, own_ref), sent = refs[:8], refs[8:12], refs[12:]
    sums = jnp.concatenate([sums_ref[...], jnp.zeros((4, C), f32)], axis=0)
    cols = jnp.transpose(sums) * (1.0 / WIDE)
    mean, square, mean_scaled, mean_cross = (cols[:, r : r + 1] for r in range(4))
    inv_std = lax.rsqrt(square - mean * mean + norm_eps)
    mean_cross = (mean_cross - mean * mean_scaled) * inv_std
    centered = (att_ref[...] - mean) * inv_std
    gain, gates, cot = gain_ref[...], gate_ref[...].astype(f32), cot_ref[...].astype(f32)
    normed = centered * gain
    out_ref[...] = (normed * gates).astype(bf16)
    dgate_ref[...] = (cot * normed).astype(bf16)
    scaled = cot * gates * gain
    grads = by_head((inv_std * (scaled - mean_scaled - centered * mean_cross)).astype(bf16))
    queries = by_head((query_ref[...].astype(f32) * 0.125).astype(bf16))
    acc = jnp.zeros((2 * C, F), f32)
    for b, packet in enumerate(packets):
        at = slice(b * C, (b + 1) * C)
        grad_weights = dot(grads, packet[:C, F:], NT)
        grad_scores = (grad_weights * slopes_ref[:, at]).astype(bf16)
        acc = acc + dot(grad_scores, packet[:C, :F], NN)
        dkey = dot(grad_scores, queries, TN)
        dvalue = dot(weights_ref[:, at], grads, TN)
        target = own_ref if b == 0 else sent[b - 1]
        target[:, :F] = dkey.astype(target.dtype)
        target[:, F:] = dvalue.astype(target.dtype)
    dq_ref[...] = (from_heads(acc) * 0.125).astype(bf16)


def total_kernel(own_ref, *refs):
    parts, (dk_ref, dv_ref) = refs[:7], refs[7:]
    total = own_ref[...]
    for part in parts:
        total = total + part[...].astype(f32)
    dk_ref[...] = total[:, :F].astype(bf16)
    dv_ref[...] = total[:, F:].astype(bf16)


def call(kernel, outs, smem=0):
    def run(*args):
        specs = [pl.BlockSpec(memory_space=pltpu.SMEM)] * smem + [VMEM] * (len(args) - smem)
        return pl.pallas_call(
            kernel,
            out_shape=[jax.ShapeDtypeStruct(s, t) for s, t in outs],
            in_specs=specs,
            out_specs=[VMEM] * len(outs),
            compiler_params=PARAMS,
        )(*args)

    return run


def shifted(x, by):
    count = lax.axis_size("seq")
    return lax.ppermute(x, "seq", [(i, i + by) for i in range(count) if 0 <= i + by < count])


def per_device(
    query_rows,
    key_rows,
    value_rows,
    gate_rows,
    cotangent,
    event_gaps,
    block_lists,
    bias_table,
    norm_gain,
):
    count = lax.axis_size("seq")
    group = lax.axis_index("seq").astype(i32).reshape(1)
    gain = norm_gain.reshape(1, F)
    (packet,) = call(pack_kernel, [((C + PAD, 2 * F), bf16)])(
        key_rows, value_rows, event_gaps.reshape(1, C)
    )
    fetched = {d: shifted(packet, d) for d in (64, 32)}
    fetched |= {d: shifted(packet, d) for d in (16, 8, 4, 2, 1)}
    three = [jnp.sum(p[C, :F].astype(f32)) for p in (packet, fetched[32], fetched[64])]
    lanes = lax.iota(i32, C)
    mine = sum(jnp.where(lanes == k, t, 0.0) for k, t in enumerate(three))
    rows = [[y * ROW + k for k in range(ROW)] for y in range(count // ROW)]
    totals = lax.all_to_all(
        jnp.broadcast_to(mine, (ROW, 1, C)), "seq", 0, 0, axis_index_groups=rows
    )
    packets = [packet] + [fetched[d] for d in DISTANCES]
    att, sums, weights, slopes = call(
        forward_kernel,
        [((C, F), f32), ((4, C), f32), ((2 * C, 8 * C), bf16), ((2 * C, 8 * C), f32)],
        1,
    )(
        group,
        query_rows,
        gate_rows,
        cotangent,
        gain,
        block_lists,
        bias_table,
        totals,
        *packets,
    )
    sums = lax.psum(sums, "head")
    layer_out, grad_query, grad_gate, own, *sent = call(
        backward_kernel,
        [((C, F), bf16)] * 3 + [((C, 2 * F), f32)] + [((C, 2 * F), bf16)] * 7,
    )(query_rows, gate_rows, cotangent, gain, att, sums, weights, slopes, *packets)
    order = (4, 3, 2, 1, 0, 6, 5)
    returned = [shifted(sent[s], -DISTANCES[s]) for s in order]
    grad_key, grad_value = call(total_kernel, [((C, F), bf16)] * 2)(own, *returned)
    return layer_out, grad_query, grad_key, grad_value, grad_gate


def solution(mesh):
    rows = P("seq", "head")
    return jax.shard_map(
        per_device,
        mesh=mesh,
        in_specs=(rows, rows, rows, rows, rows, P("seq"), P(), P("head", None), P("head")),
        out_specs=(rows, rows, rows, rows, rows),
        check_vma=False,
    )
```

time: 377 us -> 116 us (0.31)
  the two profiles are of different devices: /device:TPU:58 before, /device:TPU:9 now
where the time goes in v1:
time: 116 us; the launch traced here: 115 us
  starting transfers between devices  72.8 us (63%)
  waiting for transfers between devices  20.6 us (18%)
  blocking collectives  8.46 us (7%)
  Pallas kernels  4.53 us (4%)
  local copies, waits for them, and re-layouts  4.24 us (4%)
  other arithmetic  3.74 us (3%)
    ppermute x14, starting transfers between devices, shifted(): lax.ppermute(x, 'seq', [(i, i + by) for i in range(count) if 0 <= i + by...  63.5 us
    all_to_all x1, waiting for transfers between devices, per_device(): lax.all_to_all(jnp.broadcast_to(mine, (ROW, 1, C)), 'seq', 0, 0, axis_ind...  10.9 us
    ppermute x14, waiting for transfers between devices, shifted(): lax.ppermute(x, 'seq', [(i, i + by) for i in range(count) if 0 <= i + by...  9.73 us
    all_to_all x1, starting transfers between devices, per_device(): lax.all_to_all(jnp.broadcast_to(mine, (ROW, 1, C)), 'seq', 0, 0, axis_ind...  9.36 us
    psum x1, blocking collectives, per_device(): sums = lax.psum(sums, 'head')  8.46 us
    pallas_call x4, Pallas kernels, run(): pl.pallas_call(kernel, out_shape=[jax.ShapeDtypeStruct(s, t) for s, t in...  4.53 us
    unnamed x19, local copies, waits for them, and re-layouts  3.63 us
  transfers between devices with their start and end apart: 15, of which 5 were waited for; matrix products, arithmetic and copies ran while one was open for 4% of the time, Pallas kernels for 0%

profile of v1, /device:TPU:9, one launch (start us, length us, event | category | flops | bytes accessed | tf_op | source)
XLA Modules:
  0.0 115.3 jit_solution(4167934997229173420)
XLA Ops:
  0.6 0.6 copy-done.7
  1.3 0.8 copy-done.3
  2.0 0.8 copy-done.4
  2.8 15.4 %collective-permute-start.6 = (bf16[144,256]{1,0:T(8,128)(2,1)S(1)}, bf16[144,256]{1,0:T(8,128)(2,1)S(1)}, u32[]{:S(2)}, u32[]{:S(2)}) collective-permute-start(bf16[144,256]{1,0:T(8,128)(2,1)S(1)} %shard_map.128.refs_0_), channel_id=1, source_target_pairs={{0,64},{4,68},{8,72},{12,76},{16,80},{20,84},{24,88},{28,92},{32,9... | collective-permute-start | bytes 221192 | tf_op jit(solution)/shard_map/ppermute | solution.py:173
  18.3 4.0 %collective-permute-start.5 = (bf16[144,256]{1,0:T(8,128)(2,1)S(1)}, bf16[144,256]{1,0:T(8,128)(2,1)S(1)}, u32[]{:S(2)}, u32[]{:S(2)}) collective-permute-start(bf16[144,256]{1,0:T(8,128)(2,1)S(1)} %shard_map.128.refs_0_), channel_id=1, source_target_pairs={{0,32},{4,36},{8,40},{12,44},{16,48},{20,52},{24,56},{28,60},{32,6... | collective-permute-start | bytes 221192 | tf_op jit(solution)/shard_map/ppermute | solution.py:173
  22.3 3.1 %collective-permute-start.4 = (bf16[144,256]{1,0:T(8,128)(2,1)S(1)}, bf16[144,256]{1,0:T(8,128)(2,1)S(1)}, u32[]{:S(2)}, u32[]{:S(2)}) collective-permute-start(bf16[144,256]{1,0:T(8,128)(2,1)S(1)} %shard_map.128.refs_0_), channel_id=1, source_target_pairs={{0,16},{4,20},{8,24},{12,28},{16,32},{20,36},{24,40},{28,44},{32,4... | collective-permute-start | bytes 221192 | tf_op jit(solution)/shard_map/ppermute | solution.py:173
  25.4 2.6 %collective-permute-start.3 = (bf16[144,256]{1,0:T(8,128)(2,1)S(1)}, bf16[144,256]{1,0:T(8,128)(2,1)S(1)}, u32[]{:S(2)}, u32[]{:S(2)}) collective-permute-start(bf16[144,256]{1,0:T(8,128)(2,1)S(1)} %shard_map.128.refs_0_), channel_id=1, source_target_pairs={{0,8},{4,12},{8,16},{12,20},{16,24},{20,28},{24,32},{28,36},{32,40... | collective-permute-start | bytes 221192 | tf_op jit(solution)/shard_map/ppermute | solution.py:173
  28.1 3.9 %collective-permute-start.1 = (bf16[144,256]{1,0:T(8,128)(2,1)S(1)}, bf16[144,256]{1,0:T(8,128)(2,1)S(1)}, u32[]{:S(2)}, u32[]{:S(2)}) collective-permute-start(bf16[144,256]{1,0:T(8,128)(2,1)S(1)} %shard_map.128.refs_0_), channel_id=1, source_target_pairs={{0,256},{4,260},{8,264},{12,268},{16,272},{20,276},{24,280},{28,28... | collective-permute-start | bytes 221192 | tf_op jit(solution)/shard_map/ppermute | solution.py:173
  32.0 0.6 fusion.4
  32.6 0.8 collective-permute-done.1.refs_7_
  33.4 4.8 %collective-permute-start = (bf16[144,256]{1,0:T(8,128)(2,1)S(1)}, bf16[144,256]{1,0:T(8,128)(2,1)S(1)}, u32[]{:S(2)}, u32[]{:S(2)}) collective-permute-start(bf16[144,256]{1,0:T(8,128)(2,1)S(1)} %shard_map.128.refs_0_), channel_id=1, source_target_pairs={{0,128},{4,132},{8,136},{12,140},{16,144},{20,148},{24,152},{28,15... | collective-permute-start | bytes 221192 | tf_op jit(solution)/shard_map/ppermute | solution.py:173
  38.2 0.6 fusion.2
  38.8 0.8 collective-permute-done.refs_6_
  39.6 6.0 %collective-permute-start.2 = (bf16[144,256]{1,0:T(8,128)(2,1)S(1)}, bf16[144,256]{1,0:T(8,128)(2,1)S(1)}, u32[]{:S(2)}, u32[]{:S(2)}) collective-permute-start(bf16[144,256]{1,0:T(8,128)(2,1)S(1)} %shard_map.128.refs_0_), channel_id=1, source_target_pairs={{0,4},{4,8},{8,12},{12,16},{16,20},{20,24},{24,28},{28,32},{32,36}... | collective-permute-start | bytes 221192 | tf_op jit(solution)/shard_map/ppermute | solution.py:173
  45.6 0.6 fusion.3
  46.2 1.9 %fusion.1 = f32[128]{0:T(128)S(1)} fusion(f32[]{:T(128)} %fusion.2, f32[]{:T(128)} %fusion.3, f32[]{:T(128)} %fusion.4), kind=kLoop, calls=%fused_computation.4 | loop fusion | flops 1024 | bytes 524 | tf_op jit(solution)/shard_map/add | solution.py:197
  48.1 0.6 broadcast_in_dim.23
  48.8 9.4 %all-to-all-start = ((f32[32,1,128]{2,1,0:T(1,128)}), f32[32,1,128]{2,1,0:T(1,128)S(1)}, u32[]{:S(2)}, u32[]{:S(2)}) async-start(f32[32,1,128]{2,1,0:T(1,128)} %broadcast_in_dim.23), calls=%async_computation | async-start | bytes 32768 | tf_op jit(solution)/shard_map/all_to_all | solution.py:199
  58.1 0.0 copy-start.8
  58.1 0.7 copy-done.8
  58.8 0.1 copy.14.lists_ref
  58.9 0.0 collective-permute-done.6.refs_5_
  58.9 0.0 collective-permute-done.5.refs_4_
  58.9 0.0 collective-permute-done.4.refs_3_
  59.0 0.0 collective-permute-done.3.refs_2_
  59.0 0.0 collective-permute-done.2.refs_1_
  59.0 10.9 %all-to-all-done.totals_ref = f32[32,1,128]{2,1,0:T(1,128)S(1)} async-done(((f32[32,1,128]{2,1,0:T(1,128)}), f32[32,1,128]{2,1,0:T(1,128)S(1)}, u32[]{:S(2)}, u32[]{:S(2)}) %all-to-all-start) | async-done | bytes 16416 | tf_op jit(solution)/shard_map/all_to_all | solution.py:199
  69.9 0.0 copy-done.2
  69.9 0.6 copy-done.5
  70.5 0.0 copy-done.6
  70.5 1.5 %shard_map.129 = (f32[128,128]{1,0:T(8,128)S(1)}, f32[4,128]{1,0:T(4,128)S(1)}, bf16[256,1024]{1,0:T(8,128)(2,1)S(1)}, f32[256,1024]{1,0:T(8,128)S(1)}) custom-call(s32[1]{0:T(128)} %bitcast.1.group_ref, bf16[128,128]{1,0:T(8,128)(2,1)S(1)} %copy-done, bf16[128,128]{1,0:T(8,128)(2,1)S(1)} %copy-done.1, bf16[128,128]{1,0:T(8,128)(2,1)S(1)} %copy-done.2, ...), custom_call_target="tpu_custom_call" | custom-call | tf_op jit(solution)/shard_map/pallas_call | solution.py:160
  72.0 8.5 %psum.7.sums_ref = f32[4,128]{1,0:T(4,128)S(1)} all-reduce(f32[4,128]{1,0:T(4,128)S(1)} %get-tuple-element.23), channel_id=1, replica_groups=mesh['seq'=128,'head'=4] {'head'}, use_global_device_ids=true, to_apply=%region_3.4 | all-reduce | flops 512 | bytes 4096 | tf_op jit(solution)/shard_map/psum | solution.py:218
  80.5 2.4 %shard_map.130 = (bf16[128,128]{1,0:T(8,128)(2,1)}, bf16[128,128]{1,0:T(8,128)(2,1)}, bf16[128,128]{1,0:T(8,128)(2,1)}, f32[128,256]{1,0:T(8,128)S(1)}, bf16[128...) custom-call(bf16[128,128]{1,0:T(8,128)(2,1)S(1)} %copy-done, ...), custom_call_target="tpu_custom_call" | custom-call | tf_op jit(solution)/shard_map/pallas_call | solution.py:160
  82.8 1.9 %collective-permute-start.7 = (bf16[128,256]{1,0:T(8,128)(2,1)S(1)}, bf16[128,256]{1,0:T(8,128)(2,1)S(1)}, u32[]{:S(2)}, u32[]{:S(2)}) collective-permute-start(bf16[128,256]{1,0:T(8,128)(2,1)S(1)} %get-tuple-element.29), channel_id=1, source_target_pairs={{64,0},{68,4},{72,8},{76,12},{80,16},{84,20},{88,24},{92,28},{96,3... | collective-permute-start | bytes 196616 | tf_op jit(solution)/shard_map/ppermute | solution.py:173
  84.7 4.4 %collective-permute-start.8 = (bf16[128,256]{1,0:T(8,128)(2,1)S(1)}, bf16[128,256]{1,0:T(8,128)(2,1)S(1)}, u32[]{:S(2)}, u32[]{:S(2)}) collective-permute-start(bf16[128,256]{1,0:T(8,128)(2,1)S(1)} %get-tuple-element.30), channel_id=1, source_target_pairs={{32,0},{36,4},{40,8},{44,12},{48,16},{52,20},{56,24},{60,28},{64,3... | collective-permute-start | bytes 196616 | tf_op jit(solution)/shard_map/ppermute | solution.py:173
  89.1 5.1 %collective-permute-start.9 = (bf16[128,256]{1,0:T(8,128)(2,1)S(1)}, bf16[128,256]{1,0:T(8,128)(2,1)S(1)}, u32[]{:S(2)}, u32[]{:S(2)}) collective-permute-start(bf16[128,256]{1,0:T(8,128)(2,1)S(1)} %get-tuple-element.31), channel_id=1, source_target_pairs={{16,0},{20,4},{24,8},{28,12},{32,16},{36,20},{40,24},{44,28},{48,3... | collective-permute-start | bytes 196616 | tf_op jit(solution)/shard_map/ppermute | solution.py:173
  94.3 2.9 %collective-permute-start.10 = (bf16[128,256]{1,0:T(8,128)(2,1)S(1)}, bf16[128,256]{1,0:T(8,128)(2,1)S(1)}, u32[]{:S(2)}, u32[]{:S(2)}) collective-permute-start(bf16[128,256]{1,0:T(8,128)(2,1)S(1)} %get-tuple-element.32), channel_id=1, source_target_pairs={{8,0},{12,4},{16,8},{20,12},{24,16},{28,20},{32,24},{36,28},{40,32... | collective-permute-start | bytes 196616 | tf_op jit(solution)/shard_map/ppermute | solution.py:173
  97.2 6.0 %collective-permute-start.11 = (bf16[128,256]{1,0:T(8,128)(2,1)S(1)}, bf16[128,256]{1,0:T(8,128)(2,1)S(1)}, u32[]{:S(2)}, u32[]{:S(2)}) collective-permute-start(bf16[128,256]{1,0:T(8,128)(2,1)S(1)} %get-tuple-element.33), channel_id=1, source_target_pairs={{4,0},{8,4},{12,8},{16,12},{20,16},{24,20},{28,24},{32,28},{36,32}... | collective-permute-start | bytes 196616 | tf_op jit(solution)/shard_map/ppermute | solution.py:173
  103.2 0.0 collective-permute-done.7.refs_0_
  103.2 1.3 %collective-permute-start.12 = (bf16[128,256]{1,0:T(8,128)(2,1)S(1)}, bf16[128,256]{1,0:T(8,128)(2,1)S(1)}, u32[]{:S(2)}, u32[]{:S(2)}) collective-permute-start(bf16[128,256]{1,0:T(8,128)(2,1)S(1)} %get-tuple-element.34), channel_id=1, source_target_pairs={{256,0},{260,4},{264,8},{268,12},{272,16},{276,20},{280,24},{284,2... | collective-permute-start | bytes 196616 | tf_op jit(solution)/shard_map/ppermute | solution.py:173
  104.5 0.0 collective-permute-done.8.refs_1_
  104.5 1.9 %collective-permute-start.13 = (bf16[128,256]{1,0:T(8,128)(2,1)S(1)}, bf16[128,256]{1,0:T(8,128)(2,1)S(1)}, u32[]{:S(2)}, u32[]{:S(2)}) collective-permute-start(bf16[128,256]{1,0:T(8,128)(2,1)S(1)} %get-tuple-element.35), channel_id=1, source_target_pairs={{128,0},{132,4},{136,8},{140,12},{144,16},{148,20},{152,24},{156,2... | collective-permute-start | bytes 196616 | tf_op jit(solution)/shard_map/ppermute | solution.py:173
  106.5 0.0 collective-permute-done.9.refs_2_
  106.5 0.0 collective-permute-done.10.refs_3_
  106.5 0.0 collective-permute-done.11.refs_4_
  106.5 6.5 %collective-permute-done.12.refs_5_ = bf16[128,256]{1,0:T(8,128)(2,1)S(1)} collective-permute-done((bf16[128,256]{1,0:T(8,128)(2,1)S(1)}, bf16[128,256]{1,0:T(8,128)(2,1)S(1)}, u32[]{:S(2)}, u32[]{:S(2)}) %collective-permute-start.12) | collective-permute-done | bytes 65568 | tf_op jit(solution)/shard_map/ppermute | solution.py:173
  113.0 1.6 %collective-permute-done.13.refs_6_ = bf16[128,256]{1,0:T(8,128)(2,1)S(1)} collective-permute-done((bf16[128,256]{1,0:T(8,128)(2,1)S(1)}, bf16[128,256]{1,0:T(8,128)(2,1)S(1)}, u32[]{:S(2)}, u32[]{:S(2)}) %collective-permute-start.13) | collective-permute-done | bytes 65568 | tf_op jit(solution)/shard_map/ppermute | solution.py:173
  114.6 0.7 shard_map.131
  (11 shorter events, 0.0 us)
Async XLA Ops:
  0.6 0.7 copy-start.7
  1.3 0.8 copy-start.3
  2.0 0.8 copy-start.4
  2.8 56.1 %collective-permute-start.6 = (bf16[144,256]{1,0:T(8,128)(2,1)S(1)}, bf16[144,256]{1,0:T(8,128)(2,1)S(1)}, u32[]{:S(2)}, u32[]{:S(2)}) collective-permute-start(bf16[144,256]{1,0:T(8,128)(2,1)S(1)} %shard_map.128.refs_0_), channel_id=1, source_target_pairs={{0,64},{4,68},{8,72},{12,76},{16,80},{20,84},{24,88},{28,92},{32,9... | collective-permute-start | bytes 221192 | tf_op jit(solution)/shard_map/ppermute | solution.py:173
  18.3 40.7 %collective-permute-start.5 = (bf16[144,256]{1,0:T(8,128)(2,1)S(1)}, bf16[144,256]{1,0:T(8,128)(2,1)S(1)}, u32[]{:S(2)}, u32[]{:S(2)}) collective-permute-start(bf16[144,256]{1,0:T(8,128)(2,1)S(1)} %shard_map.128.refs_0_), channel_id=1, source_target_pairs={{0,32},{4,36},{8,40},{12,44},{16,48},{20,52},{24,56},{28,60},{32,6... | collective-permute-start | bytes 221192 | tf_op jit(solution)/shard_map/ppermute | solution.py:173
  22.3 36.7 %collective-permute-start.4 = (bf16[144,256]{1,0:T(8,128)(2,1)S(1)}, bf16[144,256]{1,0:T(8,128)(2,1)S(1)}, u32[]{:S(2)}, u32[]{:S(2)}) collective-permute-start(bf16[144,256]{1,0:T(8,128)(2,1)S(1)} %shard_map.128.refs_0_), channel_id=1, source_target_pairs={{0,16},{4,20},{8,24},{12,28},{16,32},{20,36},{24,40},{28,44},{32,4... | collective-permute-start | bytes 221192 | tf_op jit(solution)/shard_map/ppermute | solution.py:173
  25.4 33.6 %collective-permute-start.3 = (bf16[144,256]{1,0:T(8,128)(2,1)S(1)}, bf16[144,256]{1,0:T(8,128)(2,1)S(1)}, u32[]{:S(2)}, u32[]{:S(2)}) collective-permute-start(bf16[144,256]{1,0:T(8,128)(2,1)S(1)} %shard_map.128.refs_0_), channel_id=1, source_target_pairs={{0,8},{4,12},{8,16},{12,20},{16,24},{20,28},{24,32},{28,36},{32,40... | collective-permute-start | bytes 221192 | tf_op jit(solution)/shard_map/ppermute | solution.py:173
  28.1 5.3 %collective-permute-start.1 = (bf16[144,256]{1,0:T(8,128)(2,1)S(1)}, bf16[144,256]{1,0:T(8,128)(2,1)S(1)}, u32[]{:S(2)}, u32[]{:S(2)}) collective-permute-start(bf16[144,256]{1,0:T(8,128)(2,1)S(1)} %shard_map.128.refs_0_), channel_id=1, source_target_pairs={{0,256},{4,260},{8,264},{12,268},{16,272},{20,276},{24,280},{28,28... | collective-permute-start | bytes 221192 | tf_op jit(solution)/shard_map/ppermute | solution.py:173
  33.4 6.2 %collective-permute-start = (bf16[144,256]{1,0:T(8,128)(2,1)S(1)}, bf16[144,256]{1,0:T(8,128)(2,1)S(1)}, u32[]{:S(2)}, u32[]{:S(2)}) collective-permute-start(bf16[144,256]{1,0:T(8,128)(2,1)S(1)} %shard_map.128.refs_0_), channel_id=1, source_target_pairs={{0,128},{4,132},{8,136},{12,140},{16,144},{20,148},{24,152},{28,15... | collective-permute-start | bytes 221192 | tf_op jit(solution)/shard_map/ppermute | solution.py:173
  39.6 19.4 %collective-permute-start.2 = (bf16[144,256]{1,0:T(8,128)(2,1)S(1)}, bf16[144,256]{1,0:T(8,128)(2,1)S(1)}, u32[]{:S(2)}, u32[]{:S(2)}) collective-permute-start(bf16[144,256]{1,0:T(8,128)(2,1)S(1)} %shard_map.128.refs_0_), channel_id=1, source_target_pairs={{0,4},{4,8},{8,12},{12,16},{16,20},{20,24},{24,28},{28,32},{32,36}... | collective-permute-start | bytes 221192 | tf_op jit(solution)/shard_map/ppermute | solution.py:173
  48.8 21.1 %copy-start.2 = (bf16[128,128]{1,0:T(8,128)(2,1)S(1)}, bf16[128,128]{1,0:T(8,128)(2,1)}, u32[]{:S(2)}) copy-start(bf16[128,128]{1,0:T(8,128)(2,1)} %cot_ref.3) | copy-start | bytes 98308
  48.8 21.1 %all-to-all-start = ((f32[32,1,128]{2,1,0:T(1,128)}), f32[32,1,128]{2,1,0:T(1,128)S(1)}, u32[]{:S(2)}, u32[]{:S(2)}) async-start(f32[32,1,128]{2,1,0:T(1,128)} %broadcast_in_dim.23), calls=%async_computation | async-start | bytes 32768 | tf_op jit(solution)/shard_map/all_to_all | solution.py:199
  58.1 0.7 copy-start.8
  58.8 11.0 %copy-start = (bf16[128,128]{1,0:T(8,128)(2,1)S(1)}, bf16[128,128]{1,0:T(8,128)(2,1)}, u32[]{:S(2)}) copy-start(bf16[128,128]{1,0:T(8,128)(2,1)} %query_ref.3) | copy-start | bytes 98308
  58.8 11.0 %copy-start.1 = (bf16[128,128]{1,0:T(8,128)(2,1)S(1)}, bf16[128,128]{1,0:T(8,128)(2,1)}, u32[]{:S(2)}) copy-start(bf16[128,128]{1,0:T(8,128)(2,1)} %gate_ref.3) | copy-start | bytes 98308
  69.8 0.7 copy-start.5
  69.9 0.7 copy-start.6
  82.8 20.4 %collective-permute-start.7 = (bf16[128,256]{1,0:T(8,128)(2,1)S(1)}, bf16[128,256]{1,0:T(8,128)(2,1)S(1)}, u32[]{:S(2)}, u32[]{:S(2)}) collective-permute-start(bf16[128,256]{1,0:T(8,128)(2,1)S(1)} %get-tuple-element.29), channel_id=1, source_target_pairs={{64,0},{68,4},{72,8},{76,12},{80,16},{84,20},{88,24},{92,28},{96,3... | collective-permute-start | bytes 196616 | tf_op jit(solution)/shard_map/ppermute | solution.py:173
  84.7 19.8 %collective-permute-start.8 = (bf16[128,256]{1,0:T(8,128)(2,1)S(1)}, bf16[128,256]{1,0:T(8,128)(2,1)S(1)}, u32[]{:S(2)}, u32[]{:S(2)}) collective-permute-start(bf16[128,256]{1,0:T(8,128)(2,1)S(1)} %get-tuple-element.30), channel_id=1, source_target_pairs={{32,0},{36,4},{40,8},{44,12},{48,16},{52,20},{56,24},{60,28},{64,3... | collective-permute-start | bytes 196616 | tf_op jit(solution)/shard_map/ppermute | solution.py:173
  89.1 17.3 %collective-permute-start.9 = (bf16[128,256]{1,0:T(8,128)(2,1)S(1)}, bf16[128,256]{1,0:T(8,128)(2,1)S(1)}, u32[]{:S(2)}, u32[]{:S(2)}) collective-permute-start(bf16[128,256]{1,0:T(8,128)(2,1)S(1)} %get-tuple-element.31), channel_id=1, source_target_pairs={{16,0},{20,4},{24,8},{28,12},{32,16},{36,20},{40,24},{44,28},{48,3... | collective-permute-start | bytes 196616 | tf_op jit(solution)/shard_map/ppermute | solution.py:173
  94.3 12.2 %collective-permute-start.10 = (bf16[128,256]{1,0:T(8,128)(2,1)S(1)}, bf16[128,256]{1,0:T(8,128)(2,1)S(1)}, u32[]{:S(2)}, u32[]{:S(2)}) collective-permute-start(bf16[128,256]{1,0:T(8,128)(2,1)S(1)} %get-tuple-element.32), channel_id=1, source_target_pairs={{8,0},{12,4},{16,8},{20,12},{24,16},{28,20},{32,24},{36,28},{40,32... | collective-permute-start | bytes 196616 | tf_op jit(solution)/shard_map/ppermute | solution.py:173
  97.2 9.3 %collective-permute-start.11 = (bf16[128,256]{1,0:T(8,128)(2,1)S(1)}, bf16[128,256]{1,0:T(8,128)(2,1)S(1)}, u32[]{:S(2)}, u32[]{:S(2)}) collective-permute-start(bf16[128,256]{1,0:T(8,128)(2,1)S(1)} %get-tuple-element.33), channel_id=1, source_target_pairs={{4,0},{8,4},{12,8},{16,12},{20,16},{24,20},{28,24},{32,28},{36,32}... | collective-permute-start | bytes 196616 | tf_op jit(solution)/shard_map/ppermute | solution.py:173
  103.2 9.8 %collective-permute-start.12 = (bf16[128,256]{1,0:T(8,128)(2,1)S(1)}, bf16[128,256]{1,0:T(8,128)(2,1)S(1)}, u32[]{:S(2)}, u32[]{:S(2)}) collective-permute-start(bf16[128,256]{1,0:T(8,128)(2,1)S(1)} %get-tuple-element.34), channel_id=1, source_target_pairs={{256,0},{260,4},{264,8},{268,12},{272,16},{276,20},{280,24},{284,2... | collective-permute-start | bytes 196616 | tf_op jit(solution)/shard_map/ppermute | solution.py:173
  104.5 10.1 %collective-permute-start.13 = (bf16[128,256]{1,0:T(8,128)(2,1)S(1)}, bf16[128,256]{1,0:T(8,128)(2,1)S(1)}, u32[]{:S(2)}, u32[]{:S(2)}) collective-permute-start(bf16[128,256]{1,0:T(8,128)(2,1)S(1)} %get-tuple-element.35), channel_id=1, source_target_pairs={{128,0},{132,4},{136,8},{140,12},{144,16},{148,20},{152,24},{156,2... | collective-permute-start | bytes 196616 | tf_op jit(solution)/shard_map/ppermute | solution.py:173

commit v2 on v1

v2 whole, which is shorter than its diff:
```python
import functools

import jax
import jax.numpy as jnp
from jax import lax
from jax.experimental import pallas as pl
from jax.experimental.pallas import tpu as pltpu
from jax.sharding import PartitionSpec as P

norm_eps = 1e-05
C = 128
F = 128
DH = 64
DISTANCES = (1, 2, 4, 8, 16, 32, 64)
ROW = 32
PAD = 16
WIDE = 512.0
f32, bf16, i32 = jnp.float32, jnp.bfloat16, jnp.int32
VMEM = pl.BlockSpec(memory_space=pltpu.VMEM)
PARAMS = pltpu.CompilerParams(vmem_limit_bytes=40 * 1024 * 1024)


def iota(shape, dim):
    return lax.broadcasted_iota(i32, shape, dim)


def by_head(rows):
    left = iota(rows.shape, 1) < DH
    zero = jnp.zeros_like(rows)
    return jnp.concatenate([jnp.where(left, rows, zero), jnp.where(left, zero, rows)], axis=0)


def from_heads(both):
    left = iota((C, F), 1) < DH
    return jnp.where(left, both[:C], both[C:])


def dot(a, b, dims, precision=None):
    return lax.dot_general(a, b, (dims, ((), ())), preferred_element_type=f32, precision=precision)


NN, NT, TN = ((1,), (0,)), ((1,), (1,)), ((0,), (0,))


def pack_kernel(key_ref, value_ref, gaps_ref, out_ref, totals_ref, gaps_buf, sems):
    copies = [
        pltpu.make_async_copy(gaps_ref, gaps_buf, sems.at[0]),
        pltpu.make_async_copy(key_ref, out_ref.at[pl.ds(0, C), pl.ds(0, F)], sems.at[1]),
        pltpu.make_async_copy(value_ref, out_ref.at[pl.ds(0, C), pl.ds(F, F)], sems.at[2]),
    ]
    for copy in copies:
        copy.start()
    copies[0].wait()
    gaps = gaps_buf[...].astype(f32)
    total = jnp.sum(gaps, axis=1, keepdims=True)
    totals_ref[...] = jnp.broadcast_to(total.reshape(1, 1, 1), (ROW, 1, C))
    gaps = jnp.broadcast_to(gaps, (PAD, C)).astype(bf16)
    out_ref[C:, :F] = gaps
    out_ref[C:, F:] = gaps
    copies[1].wait()
    copies[2].wait()


def row_kernel(packet_ref, totals_ref, out_ref):
    out_ref[:C, :] = packet_ref[:C, :]
    totals = totals_ref[...].reshape(ROW, C)
    totals = jnp.where(iota((ROW, C), 0) == iota((ROW, C), 1), totals, 0.0)
    totals = jnp.sum(totals, axis=0, keepdims=True)
    high = jnp.floor(totals * 0.0625)
    low = totals - 16.0 * high
    line = iota((PAD, C), 0)
    gaps = packet_ref[C:, :F].astype(f32)
    out_ref[C:, :F] = jnp.where(line == 1, high, jnp.where(line == 2, low, gaps)).astype(bf16)
    out_ref[C:, F:] = packet_ref[C:, F:]


def prepare_kernel(query_ref, gate_ref, cot_ref, gain_ref, table_ref, lists_ref, *outs):
    heads_ref, scaled_ref, table_out_ref, lists_out_ref = outs
    heads_ref[...] = by_head((query_ref[...].astype(f32) * 0.125).astype(bf16))
    scaled_ref[...] = cot_ref[...].astype(f32) * gate_ref[...].astype(f32) * gain_ref[...]
    table_out_ref[...] = jnp.pad(table_ref[...], ((0, 0), (0, C - 16)))
    lists_out_ref[...] = lists_ref[...]


def forward_kernel(group_ref, heads_ref, scaled_ref, lists_ref, table_ref, totals_ref, *refs):
    packets, (att_ref, sums_ref, weights_ref, slopes_ref) = refs[:8], refs[8:]
    group = group_ref[0]
    place = lax.rem(group, ROW)
    queries = heads_ref[...]
    gaps = jnp.concatenate([p[C : C + 1, :F] for p in packets], axis=0)
    upper = (iota((C, C), 0) <= iota((C, C), 1)).astype(bf16)
    key_times = dot(gaps, upper, NN)
    lower = (iota((C, C), 1) <= iota((C, C), 0)).astype(bf16)
    query_times = dot(lower, gaps, NT)[:, :1]
    own = totals_ref[...].reshape(ROW, C)
    own = jnp.where(iota((ROW, C), 0) == iota((ROW, C), 1), own, 0.0)
    totals = [jnp.sum(own, axis=0, keepdims=True)]
    for packet in packets[6:]:
        part = packet[C:, :F].astype(f32)
        totals.append(part[1:2, :] * 16.0 + part[2:3, :])
    lane = iota((8, C), 1)
    distance = jnp.left_shift(1, iota((8, C), 0)) >> 1
    between = jnp.zeros((8, C), f32)
    for r, total in enumerate(totals):
        back = place - lane + ROW * r
        inside = (back >= 1) & (back <= distance) & (lane < ROW)
        between = between + jnp.where(inside, total, 0.0)
    shifts = jnp.sum(between, axis=1, keepdims=True) - key_times
    listed = jnp.where(lane == group, lists_ref[...], 0)
    listed = jnp.sum(listed.astype(f32), axis=1, keepdims=True) >= 0.0
    listed = listed.astype(f32)
    tables = [jnp.broadcast_to(table_ref[h : h + 1, :], (C, C)) for h in range(2)]
    acc = jnp.zeros((2 * C, F), f32)
    for b, packet in enumerate(packets):
        scores = dot(queries, packet[:C, :F], NT)
        delta = (query_times + shifts[b : b + 1, :]).astype(i32)
        bucket = jnp.minimum(32 - lax.clz(delta), 15)
        bias = jnp.concatenate([jnp.take_along_axis(t, bucket, axis=1) for t in tables], axis=0)
        scores = scores + bias
        sig = 0.5 * jnp.tanh(0.5 * scores) + 0.5
        silu = scores * sig
        slope = sig + silu * (1.0 - sig)
        if b == 0:
            keep = (iota((C, C), 1) <= iota((C, C), 0)).astype(f32)
            keep = jnp.concatenate([keep, keep], axis=0)
        else:
            keep = listed[b - 1 : b, :]
        weights = (silu * keep).astype(bf16)
        weights_ref[:, b * C : (b + 1) * C] = weights
        slopes_ref[:, b * C : (b + 1) * C] = slope * keep
        acc = acc + dot(weights, packet[:C, F:], NN)
    att = from_heads(acc)
    att_ref[...] = att
    scaled = scaled_ref[...]
    terms = jnp.concatenate([att, att * att, scaled, scaled * att], axis=0)
    rows = dot(jnp.ones((8, F), f32), terms, NT, lax.Precision.HIGHEST)
    for r in range(4):
        sums_ref[r : r + 1, :] = rows[0:1, r * C : (r + 1) * C]


def norm_terms(sums_ref, att_ref):
    sums = jnp.concatenate([sums_ref[...], jnp.zeros((4, C), f32)], axis=0)
    cols = jnp.transpose(sums) * (1.0 / WIDE)
    mean, square, mean_scaled, mean_cross = (cols[:, r : r + 1] for r in range(4))
    inv_std = lax.rsqrt(square - mean * mean + norm_eps)
    mean_cross = (mean_cross - mean * mean_scaled) * inv_std
    return inv_std, (att_ref[...] - mean) * inv_std, mean_scaled, mean_cross


def block_grads(b, queries, grads, weights_ref, slopes_ref, packet, out_ref):
    at = slice(b * C, (b + 1) * C)
    grad_weights = dot(grads, packet[:C, F:], NT)
    grad_scores = (grad_weights * slopes_ref[:, at]).astype(bf16)
    out_ref[:, :F] = dot(grad_scores, queries, TN).astype(out_ref.dtype)
    out_ref[:, F:] = dot(weights_ref[:, at], grads, TN).astype(out_ref.dtype)
    return dot(grad_scores, packet[:C, :F], NN)


def first_backward(blocks, att_ref, sums_ref, heads_ref, scaled_ref, weights_ref, slopes_ref, *refs):
    n = len(blocks)
    packets, grads_ref, acc_ref, sent = refs[:n], refs[n], refs[n + 1], refs[n + 2 :]
    inv_std, centered, mean_scaled, mean_cross = norm_terms(sums_ref, att_ref)
    grads = inv_std * (scaled_ref[...] - mean_scaled - centered * mean_cross)
    grads = by_head(grads.astype(bf16))
    grads_ref[...] = grads
    queries = heads_ref[...]
    acc = jnp.zeros((2 * C, F), f32)
    for b, packet, out in zip(blocks, packets, sent):
        acc = acc + block_grads(b, queries, grads, weights_ref, slopes_ref, packet, out)
    acc_ref[...] = acc


def next_backward(blocks, grads_ref, before_ref, heads_ref, weights_ref, slopes_ref, *refs):
    n = len(blocks)
    packets, acc_ref, sent = refs[:n], refs[n], refs[n + 1 :]
    grads, queries, acc = grads_ref[...], heads_ref[...], before_ref[...]
    for b, packet, out in zip(blocks, packets, sent):
        acc = acc + block_grads(b, queries, grads, weights_ref, slopes_ref, packet, out)
    acc_ref[...] = acc


def last_backward(
    grads_ref, before_ref, heads_ref, weights_ref, slopes_ref, packet, att_ref, sums_ref, gate_ref, cot_ref, gain_ref, *outs
):
    out_ref, dq_ref, dgate_ref, own_ref = outs
    acc = before_ref[...] + block_grads(
        0, heads_ref[...], grads_ref[...], weights_ref, slopes_ref, packet, own_ref
    )
    dq_ref[...] = (from_heads(acc) * 0.125).astype(bf16)
    centered = norm_terms(sums_ref, att_ref)[1]
    normed = centered * gain_ref[...]
    out_ref[...] = (normed * gate_ref[...].astype(f32)).astype(bf16)
    dgate_ref[...] = (cot_ref[...].astype(f32) * normed).astype(bf16)


def total_kernel(own_ref, *refs):
    parts, (dk_ref, dv_ref) = refs[:7], refs[7:]
    total = own_ref[...]
    for part in parts:
        total = total + part[...].astype(f32)
    dk_ref[...] = total[:, :F].astype(bf16)
    dv_ref[...] = total[:, F:].astype(bf16)


def call(kernel, outs, smem=0):
    def run(*args):
        specs = [pl.BlockSpec(memory_space=pltpu.SMEM)] * smem + [VMEM] * (len(args) - smem)
        return pl.pallas_call(
            kernel,
            out_shape=[jax.ShapeDtypeStruct(s, t) for s, t in outs],
            in_specs=specs,
            out_specs=[VMEM] * len(outs),
            compiler_params=PARAMS,
        )(*args)

    return run


def shifted(x, by):
    count = lax.axis_size("seq")
    return lax.ppermute(x, "seq", [(i, i + by) for i in range(count) if 0 <= i + by < count])


def per_device(
    query_rows,
    key_rows,
    value_rows,
    gate_rows,
    cotangent,
    event_gaps,
    block_lists,
    bias_table,
    norm_gain,
):
    count = lax.axis_size("seq")
    group = lax.axis_index("seq").astype(i32).reshape(1)
    gain = norm_gain.reshape(1, F)
    packet, totals = pl.pallas_call(
        pack_kernel,
        out_shape=[
            jax.ShapeDtypeStruct((C + PAD, 2 * F), bf16),
            jax.ShapeDtypeStruct((ROW, 1, C), f32),
        ],
        in_specs=[pl.BlockSpec(memory_space=pltpu.HBM)] * 3,
        out_specs=[VMEM] * 2,
        scratch_shapes=[pltpu.VMEM((1, C), i32), pltpu.SemaphoreType.DMA((3,))],
        compiler_params=pltpu.CompilerParams(vmem_limit_bytes=60 * 1024 * 1024),
    )(key_rows, value_rows, event_gaps.reshape(1, C))
    rows = [[y * ROW + k for k in range(ROW)] for y in range(count // ROW)]
    totals = lax.all_to_all(totals, "seq", 0, 0, axis_index_groups=rows)
    fetched = {d: shifted(packet, d) for d in (16, 8, 4, 2, 1)}
    (row_packet,) = call(row_kernel, [((C + PAD, 2 * F), bf16)])(packet, totals)
    fetched |= {d: shifted(row_packet, d) for d in (64, 32)}
    heads, scaled, table, lists = call(
        prepare_kernel,
        [((2 * C, F), bf16), ((C, F), f32), ((2, C), f32), ((8, C), i32)],
    )(query_rows, gate_rows, cotangent, gain, bias_table, block_lists.T)
    packets = [packet] + [fetched[d] for d in DISTANCES]
    att, sums, weights, slopes = call(
        forward_kernel,
        [((C, F), f32), ((4, C), f32), ((2 * C, 8 * C), bf16), ((2 * C, 8 * C), f32)],
        1,
    )(group, heads, scaled, lists, table, totals, *packets)
    sums = lax.psum(sums, "head")
    kept = (heads, weights, slopes)
    sent = {}
    blocks = (5,)
    grads, acc, *parts = call(
        functools.partial(first_backward, blocks),
        [((2 * C, F), bf16), ((2 * C, F), f32)] + [((C, 2 * F), bf16)] * len(blocks),
    )(att, sums, heads, scaled, weights, slopes, *(packets[b] for b in blocks))
    sent |= dict(zip(blocks, parts))
    for blocks in ((4, 3), (7, 2, 6), (1,)):
        acc, *parts = call(
            functools.partial(next_backward, blocks),
            [((2 * C, F), f32)] + [((C, 2 * F), bf16)] * len(blocks),
        )(grads, acc, *kept, *(packets[b] for b in blocks))
        sent |= dict(zip(blocks, parts))
    returned = [shifted(part, -DISTANCES[b - 1]) for b, part in sent.items()]
    layer_out, grad_query, grad_gate, own = call(
        last_backward, [((C, F), bf16)] * 3 + [((C, 2 * F), f32)]
    )(grads, acc, *kept, packet, att, sums, gate_rows, cotangent, gain)
    grad_key, grad_value = call(total_kernel, [((C, F), bf16)] * 2)(own, *returned)
    return layer_out, grad_query, grad_key, grad_value, grad_gate


def solution(mesh):
    rows = P("seq", "head")
    return jax.shard_map(
        per_device,
        mesh=mesh,
        in_specs=(rows, rows, rows, rows, rows, P("seq"), P(), P("head", None), P("head")),
        out_specs=(rows, rows, rows, rows, rows),
        check_vma=False,
    )
```

time: 116 us -> 101 us (0.87)
  the two profiles are of different devices: /device:TPU:9 before, /device:TPU:56 now
where the time goes in v2:
time: 101 us
  starting transfers between devices  65.3 us (65%)
  waiting for transfers between devices  15.7 us (16%)
  blocking collectives  10.5 us (10%)
  Pallas kernels  7.3 us (7%)
    ppermute x14, starting transfers between devices, shifted(): lax.ppermute(x, 'seq', [(i, i + by) for i in range(count) if 0 <= i + by...  60.8 us
    ppermute x14, waiting for transfers between devices, shifted(): lax.ppermute(x, 'seq', [(i, i + by) for i in range(count) if 0 <= i + by...  15.3 us
    psum x1, blocking collectives, per_device(): sums = lax.psum(sums, 'head')  10.5 us
    pallas_call x9, Pallas kernels, run(): pl.pallas_call(kernel, out_shape=[jax.ShapeDtypeStruct(s, t) for s, t in...  5.86 us
    all_to_all x1, starting transfers between devices, per_device(): totals = lax.all_to_all(totals, 'seq', 0, 0, axis_index_groups=rows)  4.51 us
  transfers between devices with their start and end apart: 15, of which 4 were waited for; matrix products, arithmetic and copies ran while one was open for 0% of the time, Pallas kernels for 1%

profile of v2, /device:TPU:56, one launch (start us, length us, event | category | flops | bytes accessed | tf_op | source)
XLA Modules:
  0.0 100.7 jit_solution(3368301309268590705)
XLA Ops:
  0.6 1.4 %shard_map.129 = (bf16[144,256]{1,0:T(8,128)(2,1)}, f32[32,1,128]{2,1,0:T(1,128)}) custom-call(bf16[128,128]{1,0:T(8,128)(2,1)} %key_ref.1, bf16[128,128]{1,0:T(8,128)(2,1)} %value_ref.1, s32[1,128]{1,0:T(1,128)} %bitcast.7), custom_call_target="tpu_custom_call" | custom-call | tf_op jit(solution)/shard_map/pallas_call | solution.py:238
  2.1 14.8 %collective-permute-start.4 = (bf16[144,256]{1,0:T(8,128)(2,1)}, bf16[144,256]{1,0:T(8,128)(2,1)S(1)}, u32[]{:S(2)}, u32[]{:S(2)}) collective-permute-start(bf16[144,256]{1,0:T(8,128)(2,1)} %get-tuple-element.38.packet_ref.refs_0_.packet), channel_id=1, source_target_pairs={{0,64},{4,68},{8,72},{12,76},{16,80},{20,84},{24,88},{28,92},{32,9... | collective-permute-start | bytes 221192 | tf_op jit(solution)/shard_map/ppermute | solution.py:221
  16.9 4.3 %collective-permute-start.3 = (bf16[144,256]{1,0:T(8,128)(2,1)}, bf16[144,256]{1,0:T(8,128)(2,1)S(1)}, u32[]{:S(2)}, u32[]{:S(2)}) collective-permute-start(bf16[144,256]{1,0:T(8,128)(2,1)} %get-tuple-element.38.packet_ref.refs_0_.packet), channel_id=1, source_target_pairs={{0,32},{4,36},{8,40},{12,44},{16,48},{20,52},{24,56},{28,60},{32,6... | collective-permute-start | bytes 221192 | tf_op jit(solution)/shard_map/ppermute | solution.py:221
  21.2 4.5 %all-to-all-start = ((f32[32,1,128]{2,1,0:T(1,128)}), f32[32,1,128]{2,1,0:T(1,128)S(1)}, u32[]{:S(2)}, u32[]{:S(2)}) async-start(f32[32,1,128]{2,1,0:T(1,128)} %get-tuple-element.37), calls=%async_computation | async-start | bytes 32768 | tf_op jit(solution)/shard_map/all_to_all | solution.py:250
  25.7 4.3 %collective-permute-start.2 = (bf16[144,256]{1,0:T(8,128)(2,1)}, bf16[144,256]{1,0:T(8,128)(2,1)S(1)}, u32[]{:S(2)}, u32[]{:S(2)}) collective-permute-start(bf16[144,256]{1,0:T(8,128)(2,1)} %get-tuple-element.38.packet_ref.refs_0_.packet), channel_id=1, source_target_pairs={{0,16},{4,20},{8,24},{12,28},{16,32},{20,36},{24,40},{28,44},{32,4... | collective-permute-start | bytes 221192 | tf_op jit(solution)/shard_map/ppermute | solution.py:221
  30.0 4.6 %collective-permute-start.1 = (bf16[144,256]{1,0:T(8,128)(2,1)}, bf16[144,256]{1,0:T(8,128)(2,1)S(1)}, u32[]{:S(2)}, u32[]{:S(2)}) collective-permute-start(bf16[144,256]{1,0:T(8,128)(2,1)} %get-tuple-element.38.packet_ref.refs_0_.packet), channel_id=1, source_target_pairs={{0,8},{4,12},{8,16},{12,20},{16,24},{20,28},{24,32},{28,36},{32,40... | collective-permute-start | bytes 221192 | tf_op jit(solution)/shard_map/ppermute | solution.py:221
  34.6 1.9 %collective-permute-start = (bf16[144,256]{1,0:T(8,128)(2,1)}, bf16[144,256]{1,0:T(8,128)(2,1)S(1)}, u32[]{:S(2)}, u32[]{:S(2)}) collective-permute-start(bf16[144,256]{1,0:T(8,128)(2,1)} %get-tuple-element.38.packet_ref.refs_0_.packet), channel_id=1, source_target_pairs={{0,4},{4,8},{8,12},{12,16},{16,20},{20,24},{24,28},{28,32},{32,36}... | collective-permute-start | bytes 221192 | tf_op jit(solution)/shard_map/ppermute | solution.py:221
  36.6 0.4 all-to-all-done.totals_ref
  37.0 0.9 copy-done
  37.9 0.0 copy-start.6
  37.9 0.0 copy-start.7
  37.9 0.0 copy-start.1
  37.9 0.0 collective-permute-done.4.refs_5_.refs_0_
  37.9 1.4 %collective-permute-start.6 = (bf16[144,256]{1,0:T(8,128)(2,1)S(1)}, bf16[144,256]{1,0:T(8,128)(2,1)S(1)}, u32[]{:S(2)}, u32[]{:S(2)}) collective-permute-start(bf16[144,256]{1,0:T(8,128)(2,1)S(1)} %shard_map.130), channel_id=1, source_target_pairs={{0,256},{4,260},{8,264},{12,268},{16,272},{20,276},{24,280},{28,28... | collective-permute-start | bytes 221192 | tf_op jit(solution)/shard_map/ppermute | solution.py:221
  39.4 0.0 collective-permute-done.3.refs_4_.refs_0_
  39.4 1.3 %collective-permute-start.5 = (bf16[144,256]{1,0:T(8,128)(2,1)S(1)}, bf16[144,256]{1,0:T(8,128)(2,1)S(1)}, u32[]{:S(2)}, u32[]{:S(2)}) collective-permute-start(bf16[144,256]{1,0:T(8,128)(2,1)S(1)} %shard_map.130), channel_id=1, source_target_pairs={{0,128},{4,132},{8,136},{12,140},{16,144},{20,148},{24,152},{28,15... | collective-permute-start | bytes 221192 | tf_op jit(solution)/shard_map/ppermute | solution.py:221
  40.7 0.0 copy-done.2
  40.7 0.0 copy-done.3
  40.7 0.0 copy-done.4
  40.7 0.0 copy-done.5
  40.7 0.0 copy-done.6
  40.8 0.0 collective-permute-done.2.refs_3_.refs_1_
  40.8 0.0 collective-permute-done.1.refs_2_.refs_1_
  40.8 0.0 collective-permute-done.refs_1_.refs_0_
  40.8 5.6 %collective-permute-done.6.refs_7_.refs_0_ = bf16[144,256]{1,0:T(8,128)(2,1)S(1)} collective-permute-done((bf16[144,256]{1,0:T(8,128)(2,1)S(1)}, bf16[144,256]{1,0:T(8,128)(2,1)S(1)}, u32[]{:S(2)}, u32[]{:S(2)}) %collective-permute-start.6) | collective-permute-done | bytes 73760 | tf_op jit(solution)/shard_map/ppermute | solution.py:221
  46.4 0.4 collective-permute-done.5.refs_6_.refs_2_
  46.8 1.4 %shard_map.131 = (f32[128,128]{1,0:T(8,128)S(1)}, f32[4,128]{1,0:T(4,128)S(1)}, bf16[256,1024]{1,0:T(8,128)(2,1)S(1)}, f32[256,1024]{1,0:T(8,128)S(1)}) custom-call(s32[1]{0:T(128)} %bitcast.group_ref, bf16[256,128]{1,0:T(8,128)(2,1)S(1)} %get-tuple-element.33.heads_ref, f32[128,128]{1,0:T(8,128)S(1)} %get-tuple-element.34.scaled_ref, ...), custom_call_target="tpu_custom_call" | custom-call | tf_op jit(solution)/shard_map/pallas_call | solution.py:208
  48.3 10.5 %psum.7.sums_ref = f32[4,128]{1,0:T(4,128)S(1)} all-reduce(f32[4,128]{1,0:T(4,128)S(1)} %get-tuple-element.40), channel_id=1, replica_groups=mesh['seq'=128,'head'=4] {'head'}, use_global_device_ids=true, to_apply=%region_0.0 | all-reduce | flops 512 | bytes 4096 | tf_op jit(solution)/shard_map/psum | solution.py:264
  58.8 0.7 shard_map.132
  59.5 0.7 shard_map.133
  60.2 0.7 shard_map.134
  60.9 0.4 shard_map.135
  61.3 1.9 %collective-permute-start.13 = (bf16[128,256]{1,0:T(8,128)(2,1)S(1)}, bf16[128,256]{1,0:T(8,128)(2,1)S(1)}, u32[]{:S(2)}, u32[]{:S(2)}) collective-permute-start(bf16[128,256]{1,0:T(8,128)(2,1)S(1)} %get-tuple-element.57), channel_id=1, source_target_pairs={{4,0},{8,4},{12,8},{16,12},{20,16},{24,20},{28,24},{32,28},{36,32}... | collective-permute-start | bytes 196616 | tf_op jit(solution)/shard_map/ppermute | solution.py:221
  63.3 6.6 %collective-permute-start.10 = (bf16[128,256]{1,0:T(8,128)(2,1)S(1)}, bf16[128,256]{1,0:T(8,128)(2,1)S(1)}, u32[]{:S(2)}, u32[]{:S(2)}) collective-permute-start(bf16[128,256]{1,0:T(8,128)(2,1)S(1)} %get-tuple-element.54), channel_id=1, source_target_pairs={{256,0},{260,4},{264,8},{268,12},{272,16},{276,20},{280,24},{284,2... | collective-permute-start | bytes 196616 | tf_op jit(solution)/shard_map/ppermute | solution.py:221
  69.8 3.0 %collective-permute-start.11 = (bf16[128,256]{1,0:T(8,128)(2,1)S(1)}, bf16[128,256]{1,0:T(8,128)(2,1)S(1)}, u32[]{:S(2)}, u32[]{:S(2)}) collective-permute-start(bf16[128,256]{1,0:T(8,128)(2,1)S(1)} %get-tuple-element.55), channel_id=1, source_target_pairs={{8,0},{12,4},{16,8},{20,12},{24,16},{28,20},{32,24},{36,28},{40,32... | collective-permute-start | bytes 196616 | tf_op jit(solution)/shard_map/ppermute | solution.py:221
  72.8 1.3 %collective-permute-start.12 = (bf16[128,256]{1,0:T(8,128)(2,1)S(1)}, bf16[128,256]{1,0:T(8,128)(2,1)S(1)}, u32[]{:S(2)}, u32[]{:S(2)}) collective-permute-start(bf16[128,256]{1,0:T(8,128)(2,1)S(1)} %get-tuple-element.56), channel_id=1, source_target_pairs={{128,0},{132,4},{136,8},{140,12},{144,16},{148,20},{152,24},{156,2... | collective-permute-start | bytes 196616 | tf_op jit(solution)/shard_map/ppermute | solution.py:221
  74.1 2.2 %collective-permute-start.8 = (bf16[128,256]{1,0:T(8,128)(2,1)S(1)}, bf16[128,256]{1,0:T(8,128)(2,1)S(1)}, u32[]{:S(2)}, u32[]{:S(2)}) collective-permute-start(bf16[128,256]{1,0:T(8,128)(2,1)S(1)} %get-tuple-element.52), channel_id=1, source_target_pairs={{32,0},{36,4},{40,8},{44,12},{48,16},{52,20},{56,24},{60,28},{64,3... | collective-permute-start | bytes 196616 | tf_op jit(solution)/shard_map/ppermute | solution.py:221
  76.3 0.0 collective-permute-done.13.refs_6_
  76.3 5.2 %collective-permute-start.9 = (bf16[128,256]{1,0:T(8,128)(2,1)S(1)}, bf16[128,256]{1,0:T(8,128)(2,1)S(1)}, u32[]{:S(2)}, u32[]{:S(2)}) collective-permute-start(bf16[128,256]{1,0:T(8,128)(2,1)S(1)} %get-tuple-element.53), channel_id=1, source_target_pairs={{16,0},{20,4},{24,8},{28,12},{32,16},{36,20},{40,24},{44,28},{48,3... | collective-permute-start | bytes 196616 | tf_op jit(solution)/shard_map/ppermute | solution.py:221
  81.5 0.0 collective-permute-done.10.refs_3_
  81.6 8.0 %collective-permute-start.7 = (bf16[128,256]{1,0:T(8,128)(2,1)S(1)}, bf16[128,256]{1,0:T(8,128)(2,1)S(1)}, u32[]{:S(2)}, u32[]{:S(2)}) collective-permute-start(bf16[128,256]{1,0:T(8,128)(2,1)S(1)} %get-tuple-element.51), channel_id=1, source_target_pairs={{64,0},{68,4},{72,8},{76,12},{80,16},{84,20},{88,24},{92,28},{96,3... | collective-permute-start | bytes 196616 | tf_op jit(solution)/shard_map/ppermute | solution.py:221
  89.6 1.1 %shard_map.136 = (bf16[128,128]{1,0:T(8,128)(2,1)}, bf16[128,128]{1,0:T(8,128)(2,1)}, bf16[128,128]{1,0:T(8,128)(2,1)}, f32[128,256]{1,0:T(8,128)S(1)}) custom-call(bf16[256,128]{1,0:T(8,128)(2,1)S(1)} %get-tuple-element.43.grads_ref, f32[256,128]{1,0:T(8,128)S(1)} %get-tuple-element.47.before_ref, bf16[256,128]{1,0:T(8,128)(2,1)S(1)} %get-tuple-element.33.heads_ref, ...), custom_call_target="tpu_custom_call" | custom-call | tf_op jit(solution)/shard_map/pallas_call | solution.py:208
  90.7 0.0 collective-permute-done.11.refs_4_
  90.7 0.0 collective-permute-done.12.refs_5_
  90.7 0.0 collective-permute-done.8.refs_1_
  90.7 0.0 collective-permute-done.9.refs_2_
  90.8 9.2 %collective-permute-done.7.refs_0_ = bf16[128,256]{1,0:T(8,128)(2,1)S(1)} collective-permute-done((bf16[128,256]{1,0:T(8,128)(2,1)S(1)}, bf16[128,256]{1,0:T(8,128)(2,1)S(1)}, u32[]{:S(2)}, u32[]{:S(2)}) %collective-permute-start.7) | collective-permute-done | bytes 65568 | tf_op jit(solution)/shard_map/ppermute | solution.py:221
  100.0 0.7 shard_map.137
  (9 shorter events, 0.1 us)
Async XLA Ops:
  2.1 35.9 %collective-permute-start.4 = (bf16[144,256]{1,0:T(8,128)(2,1)}, bf16[144,256]{1,0:T(8,128)(2,1)S(1)}, u32[]{:S(2)}, u32[]{:S(2)}) collective-permute-start(bf16[144,256]{1,0:T(8,128)(2,1)} %get-tuple-element.38.packet_ref.refs_0_.packet), channel_id=1, source_target_pairs={{0,64},{4,68},{8,72},{12,76},{16,80},{20,84},{24,88},{28,92},{32,9... | collective-permute-start | bytes 221192 | tf_op jit(solution)/shard_map/ppermute | solution.py:221
  16.9 22.5 %collective-permute-start.3 = (bf16[144,256]{1,0:T(8,128)(2,1)}, bf16[144,256]{1,0:T(8,128)(2,1)S(1)}, u32[]{:S(2)}, u32[]{:S(2)}) collective-permute-start(bf16[144,256]{1,0:T(8,128)(2,1)} %get-tuple-element.38.packet_ref.refs_0_.packet), channel_id=1, source_target_pairs={{0,32},{4,36},{8,40},{12,44},{16,48},{20,52},{24,56},{28,60},{32,6... | collective-permute-start | bytes 221192 | tf_op jit(solution)/shard_map/ppermute | solution.py:221
  21.2 15.8 %all-to-all-start = ((f32[32,1,128]{2,1,0:T(1,128)}), f32[32,1,128]{2,1,0:T(1,128)S(1)}, u32[]{:S(2)}, u32[]{:S(2)}) async-start(f32[32,1,128]{2,1,0:T(1,128)} %get-tuple-element.37), calls=%async_computation | async-start | bytes 32768 | tf_op jit(solution)/shard_map/all_to_all | solution.py:250
  25.7 15.1 %collective-permute-start.2 = (bf16[144,256]{1,0:T(8,128)(2,1)}, bf16[144,256]{1,0:T(8,128)(2,1)S(1)}, u32[]{:S(2)}, u32[]{:S(2)}) collective-permute-start(bf16[144,256]{1,0:T(8,128)(2,1)} %get-tuple-element.38.packet_ref.refs_0_.packet), channel_id=1, source_target_pairs={{0,16},{4,20},{8,24},{12,28},{16,32},{20,36},{24,40},{28,44},{32,4... | collective-permute-start | bytes 221192 | tf_op jit(solution)/shard_map/ppermute | solution.py:221
  30.0 10.8 %collective-permute-start.1 = (bf16[144,256]{1,0:T(8,128)(2,1)}, bf16[144,256]{1,0:T(8,128)(2,1)S(1)}, u32[]{:S(2)}, u32[]{:S(2)}) collective-permute-start(bf16[144,256]{1,0:T(8,128)(2,1)} %get-tuple-element.38.packet_ref.refs_0_.packet), channel_id=1, source_target_pairs={{0,8},{4,12},{8,16},{12,20},{16,24},{20,28},{24,32},{28,36},{32,40... | collective-permute-start | bytes 221192 | tf_op jit(solution)/shard_map/ppermute | solution.py:221
  34.6 6.2 %collective-permute-start = (bf16[144,256]{1,0:T(8,128)(2,1)}, bf16[144,256]{1,0:T(8,128)(2,1)S(1)}, u32[]{:S(2)}, u32[]{:S(2)}) collective-permute-start(bf16[144,256]{1,0:T(8,128)(2,1)} %get-tuple-element.38.packet_ref.refs_0_.packet), channel_id=1, source_target_pairs={{0,4},{4,8},{8,12},{12,16},{16,20},{20,24},{24,28},{28,32},{32,36}... | collective-permute-start | bytes 221192 | tf_op jit(solution)/shard_map/ppermute | solution.py:221
  37.0 0.9 copy-start
  37.9 2.8 %copy-start.2 = (bf16[128,128]{1,0:T(8,128)(2,1)S(1)}, bf16[128,128]{1,0:T(8,128)(2,1)}, u32[]{:S(2)}) copy-start(bf16[128,128]{1,0:T(8,128)(2,1)} %gate_ref.3) | copy-start | bytes 98308
  37.9 2.8 %copy-start.3 = (bf16[128,128]{1,0:T(8,128)(2,1)S(1)}, bf16[128,128]{1,0:T(8,128)(2,1)}, u32[]{:S(2)}) copy-start(bf16[128,128]{1,0:T(8,128)(2,1)} %cot_ref.3) | copy-start | bytes 98308
  37.9 2.9 %copy-start.4 = (bf16[128,128]{1,0:T(8,128)(2,1)S(1)}, bf16[128,128]{1,0:T(8,128)(2,1)}, u32[]{:S(2)}) copy-start(bf16[128,128]{1,0:T(8,128)(2,1)} %query_ref.1) | copy-start | bytes 98308
  37.9 2.9 %copy-start.5 = (s32[128,8]{0,1:T(8,128)S(1)}, s32[128,8]{0,1:T(8,128)}, u32[]{:S(2)}) copy-start(s32[128,8]{0,1:T(8,128)} %param.15) | copy-start | bytes 12292
  37.9 2.9 %copy-start.6 = (f32[128]{0:T(128)S(1)}, f32[128]{0:T(128)}, u32[]{:S(2)}) copy-start(f32[128]{0:T(128)} %param.17) | copy-start | bytes 1540
  37.9 2.9 %copy-start.7 = (f32[2,16]{1,0:T(2,128)S(1)}, f32[2,16]{1,0:T(2,128)}, u32[]{:S(2)}) copy-start(f32[2,16]{1,0:T(2,128)} %table_ref.1) | copy-start | bytes 388
  37.9 8.9 %copy-start.1 = (bf16[144,256]{1,0:T(8,128)(2,1)S(1)}, bf16[144,256]{1,0:T(8,128)(2,1)}, u32[]{:S(2)}) copy-start(bf16[144,256]{1,0:T(8,128)(2,1)} %get-tuple-element.38.packet_ref.refs_0_.packet) | copy-start | bytes 221188
  37.9 8.5 %collective-permute-start.6 = (bf16[144,256]{1,0:T(8,128)(2,1)S(1)}, bf16[144,256]{1,0:T(8,128)(2,1)S(1)}, u32[]{:S(2)}, u32[]{:S(2)}) collective-permute-start(bf16[144,256]{1,0:T(8,128)(2,1)S(1)} %shard_map.130), channel_id=1, source_target_pairs={{0,256},{4,260},{8,264},{12,268},{16,272},{20,276},{24,280},{28,28... | collective-permute-start | bytes 221192 | tf_op jit(solution)/shard_map/ppermute | solution.py:221
  39.4 7.5 %collective-permute-start.5 = (bf16[144,256]{1,0:T(8,128)(2,1)S(1)}, bf16[144,256]{1,0:T(8,128)(2,1)S(1)}, u32[]{:S(2)}, u32[]{:S(2)}) collective-permute-start(bf16[144,256]{1,0:T(8,128)(2,1)S(1)} %shard_map.130), channel_id=1, source_target_pairs={{0,128},{4,132},{8,136},{12,140},{16,144},{20,148},{24,152},{28,15... | collective-permute-start | bytes 221192 | tf_op jit(solution)/shard_map/ppermute | solution.py:221
  61.3 15.0 %collective-permute-start.13 = (bf16[128,256]{1,0:T(8,128)(2,1)S(1)}, bf16[128,256]{1,0:T(8,128)(2,1)S(1)}, u32[]{:S(2)}, u32[]{:S(2)}) collective-permute-start(bf16[128,256]{1,0:T(8,128)(2,1)S(1)} %get-tuple-element.57), channel_id=1, source_target_pairs={{4,0},{8,4},{12,8},{16,12},{20,16},{24,20},{28,24},{32,28},{36,32}... | collective-permute-start | bytes 196616 | tf_op jit(solution)/shard_map/ppermute | solution.py:221
  63.3 18.3 %collective-permute-start.10 = (bf16[128,256]{1,0:T(8,128)(2,1)S(1)}, bf16[128,256]{1,0:T(8,128)(2,1)S(1)}, u32[]{:S(2)}, u32[]{:S(2)}) collective-permute-start(bf16[128,256]{1,0:T(8,128)(2,1)S(1)} %get-tuple-element.54), channel_id=1, source_target_pairs={{256,0},{260,4},{264,8},{268,12},{272,16},{276,20},{280,24},{284,2... | collective-permute-start | bytes 196616 | tf_op jit(solution)/shard_map/ppermute | solution.py:221
  69.8 20.9 %collective-permute-start.11 = (bf16[128,256]{1,0:T(8,128)(2,1)S(1)}, bf16[128,256]{1,0:T(8,128)(2,1)S(1)}, u32[]{:S(2)}, u32[]{:S(2)}) collective-permute-start(bf16[128,256]{1,0:T(8,128)(2,1)S(1)} %get-tuple-element.55), channel_id=1, source_target_pairs={{8,0},{12,4},{16,8},{20,12},{24,16},{28,20},{32,24},{36,28},{40,32... | collective-permute-start | bytes 196616 | tf_op jit(solution)/shard_map/ppermute | solution.py:221
  72.8 17.9 %collective-permute-start.12 = (bf16[128,256]{1,0:T(8,128)(2,1)S(1)}, bf16[128,256]{1,0:T(8,128)(2,1)S(1)}, u32[]{:S(2)}, u32[]{:S(2)}) collective-permute-start(bf16[128,256]{1,0:T(8,128)(2,1)S(1)} %get-tuple-element.56), channel_id=1, source_target_pairs={{128,0},{132,4},{136,8},{140,12},{144,16},{148,20},{152,24},{156,2... | collective-permute-start | bytes 196616 | tf_op jit(solution)/shard_map/ppermute | solution.py:221
  74.1 16.6 %collective-permute-start.8 = (bf16[128,256]{1,0:T(8,128)(2,1)S(1)}, bf16[128,256]{1,0:T(8,128)(2,1)S(1)}, u32[]{:S(2)}, u32[]{:S(2)}) collective-permute-start(bf16[128,256]{1,0:T(8,128)(2,1)S(1)} %get-tuple-element.52), channel_id=1, source_target_pairs={{32,0},{36,4},{40,8},{44,12},{48,16},{52,20},{56,24},{60,28},{64,3... | collective-permute-start | bytes 196616 | tf_op jit(solution)/shard_map/ppermute | solution.py:221
  76.3 14.4 %collective-permute-start.9 = (bf16[128,256]{1,0:T(8,128)(2,1)S(1)}, bf16[128,256]{1,0:T(8,128)(2,1)S(1)}, u32[]{:S(2)}, u32[]{:S(2)}) collective-permute-start(bf16[128,256]{1,0:T(8,128)(2,1)S(1)} %get-tuple-element.53), channel_id=1, source_target_pairs={{16,0},{20,4},{24,8},{28,12},{32,16},{36,20},{40,24},{44,28},{48,3... | collective-permute-start | bytes 196616 | tf_op jit(solution)/shard_map/ppermute | solution.py:221
  81.6 18.4 %collective-permute-start.7 = (bf16[128,256]{1,0:T(8,128)(2,1)S(1)}, bf16[128,256]{1,0:T(8,128)(2,1)S(1)}, u32[]{:S(2)}, u32[]{:S(2)}) collective-permute-start(bf16[128,256]{1,0:T(8,128)(2,1)S(1)} %get-tuple-element.51), channel_id=1, source_target_pairs={{64,0},{68,4},{72,8},{76,12},{80,16},{84,20},{88,24},{92,28},{96,3... | collective-permute-start | bytes 196616 | tf_op jit(solution)/shard_map/ppermute | solution.py:221

commit v3 on v2

--- a/solution.py
+++ b/solution.py
@@ -17,6 +17,7 @@
 WIDE = 512.0
 f32, bf16, i32 = jnp.float32, jnp.bfloat16, jnp.int32
 VMEM = pl.BlockSpec(memory_space=pltpu.VMEM)
+COST = pl.CostEstimate(flops=8 * 10**8, bytes_accessed=2**20, transcendentals=0)
 PARAMS = pltpu.CompilerParams(vmem_limit_bytes=40 * 1024 * 1024)
 
 
@@ -147,6 +148,10 @@
     return inv_std, (att_ref[...] - mean) * inv_std, mean_scaled, mean_cross
 
 
+def add_kernel(part_ref, received_ref, out_ref):
+    out_ref[...] = (part_ref[...] + received_ref[...].astype(f32)).astype(bf16)
+
+
 def block_grads(b, queries, grads, weights_ref, slopes_ref, packet, out_ref):
     at = slice(b * C, (b + 1) * C)
     grad_weights = dot(grads, packet[:C, F:], NT)
@@ -194,7 +199,7 @@
 
 
 def total_kernel(own_ref, *refs):
-    parts, (dk_ref, dv_ref) = refs[:7], refs[7:]
+    parts, (dk_ref, dv_ref) = refs[:-2], refs[-2:]
     total = own_ref[...]
     for part in parts:
         total = total + part[...].astype(f32)
@@ -202,7 +207,7 @@
     dv_ref[...] = total[:, F:].astype(bf16)
 
 
-def call(kernel, outs, smem=0):
+def call(kernel, outs, smem=0, cost=None):
     def run(*args):
         specs = [pl.BlockSpec(memory_space=pltpu.SMEM)] * smem + [VMEM] * (len(args) - smem)
         return pl.pallas_call(
@@ -211,6 +216,7 @@
             in_specs=specs,
             out_specs=[VMEM] * len(outs),
             compiler_params=PARAMS,
+            cost_estimate=cost,
         )(*args)
 
     return run
@@ -263,20 +269,30 @@
     )(group, heads, scaled, lists, table, totals, *packets)
     sums = lax.psum(sums, "head")
     kept = (heads, weights, slopes)
-    sent = {}
-    blocks = (5,)
-    grads, acc, *parts = call(
+    narrow, wide = ((C, 2 * F), bf16), ((C, 2 * F), f32)
+    blocks = (5, 4)
+    grads, acc, part16, part8 = call(
         functools.partial(first_backward, blocks),
-        [((2 * C, F), bf16), ((2 * C, F), f32)] + [((C, 2 * F), bf16)] * len(blocks),
+        [((2 * C, F), bf16), ((2 * C, F), f32), narrow, narrow],
     )(att, sums, heads, scaled, weights, slopes, *(packets[b] for b in blocks))
-    sent |= dict(zip(blocks, parts))
-    for blocks in ((4, 3), (7, 2, 6), (1,)):
-        acc, *parts = call(
-            functools.partial(next_backward, blocks),
-            [((2 * C, F), f32)] + [((C, 2 * F), bf16)] * len(blocks),
-        )(grads, acc, *kept, *(packets[b] for b in blocks))
-        sent |= dict(zip(blocks, parts))
-    returned = [shifted(part, -DISTANCES[b - 1]) for b, part in sent.items()]
+
+    def more(blocks, acc, outs):
+        return call(functools.partial(next_backward, blocks), [((2 * C, F), f32)] + outs, cost=COST)(
+            grads, acc, *kept, *(packets[b] for b in blocks)
+        )
+
+    relayed = shifted(part8, -4)
+    acc, part64, part32, part2, part1, part4 = more((7, 6, 2, 1, 3), acc, [narrow] * 4 + [wide])
+    returned = [
+        shifted(part16, -16),
+        shifted(part64, -64),
+        shifted(part32, -32),
+        shifted(part2, -2),
+        shifted(part1, -1),
+    ]
+    part4, relayed, returned[0] = lax.optimization_barrier((part4, relayed, returned[0]))
+    (both,) = call(add_kernel, [narrow])(part4, relayed)
+    returned.append(shifted(both, -4))
     layer_out, grad_query, grad_gate, own = call(
         last_backward, [((C, F), bf16)] * 3 + [((C, 2 * F), f32)]
     )(grads, acc, *kept, packet, att, sums, gate_rows, cotangent, gain)

time: 101 us -> 97 us (0.960)
  the two profiles are of different devices: /device:TPU:56 before, /device:TPU:25 now
where the time goes in v3:
time: 97 us; the launch traced here: 96.4 us
  starting transfers between devices  69 us (71%)
  waiting for transfers between devices  10.6 us (11%)
  blocking collectives  8.47 us (9%)
  Pallas kernels  6.49 us (7%)
    ppermute x14, starting transfers between devices, shifted(): lax.ppermute(x, 'seq', [(i, i + by) for i in range(count) if 0 <= i + by...  64.2 us
    ppermute x14, waiting for transfers between devices, shifted(): lax.ppermute(x, 'seq', [(i, i + by) for i in range(count) if 0 <= i + by...  10.6 us
    psum x1, blocking collectives, per_device(): sums = lax.psum(sums, 'head')  8.47 us
    pallas_call x8, Pallas kernels, run(): pl.pallas_call(kernel, out_shape=[jax.ShapeDtypeStruct(s, t) for s, t in...  5.04 us
    all_to_all x1, starting transfers between devices, per_device(): totals = lax.all_to_all(totals, 'seq', 0, 0, axis_index_groups=rows)  4.73 us
  transfers between devices with their start and end apart: 15, of which 3 were waited for; matrix products, arithmetic and copies ran while one was open for 0% of the time, Pallas kernels for 2%

profile of v3, /device:TPU:25, one launch (start us, length us, event | category | flops | bytes accessed | tf_op | source)
XLA Modules:
  0.0 96.4 jit_solution(9616140019962846054)
XLA Ops:
  0.6 1.4 %shard_map.129 = (bf16[144,256]{1,0:T(8,128)(2,1)}, f32[32,1,128]{2,1,0:T(1,128)}) custom-call(bf16[128,128]{1,0:T(8,128)(2,1)} %key_ref.1, bf16[128,128]{1,0:T(8,128)(2,1)} %value_ref.1, s32[1,128]{1,0:T(1,128)} %bitcast.7), custom_call_target="tpu_custom_call" | custom-call | tf_op jit(solution)/shard_map/pallas_call | solution.py:244
  2.1 15.4 %collective-permute-start.4 = (bf16[144,256]{1,0:T(8,128)(2,1)}, bf16[144,256]{1,0:T(8,128)(2,1)S(1)}, u32[]{:S(2)}, u32[]{:S(2)}) collective-permute-start(bf16[144,256]{1,0:T(8,128)(2,1)} %get-tuple-element.39.packet_ref.refs_0_.packet), channel_id=1, source_target_pairs={{0,64},{4,68},{8,72},{12,76},{16,80},{20,84},{24,88},{28,92},{32,9... | collective-permute-start | bytes 221192 | tf_op jit(solution)/shard_map/ppermute | solution.py:227
  17.5 4.0 %collective-permute-start.3 = (bf16[144,256]{1,0:T(8,128)(2,1)}, bf16[144,256]{1,0:T(8,128)(2,1)S(1)}, u32[]{:S(2)}, u32[]{:S(2)}) collective-permute-start(bf16[144,256]{1,0:T(8,128)(2,1)} %get-tuple-element.39.packet_ref.refs_0_.packet), channel_id=1, source_target_pairs={{0,32},{4,36},{8,40},{12,44},{16,48},{20,52},{24,56},{28,60},{32,6... | collective-permute-start | bytes 221192 | tf_op jit(solution)/shard_map/ppermute | solution.py:227
  21.6 4.7 %all-to-all-start = ((f32[32,1,128]{2,1,0:T(1,128)}), f32[32,1,128]{2,1,0:T(1,128)S(1)}, u32[]{:S(2)}, u32[]{:S(2)}) async-start(f32[32,1,128]{2,1,0:T(1,128)} %get-tuple-element.38), calls=%async_computation | async-start | bytes 32768 | tf_op jit(solution)/shard_map/all_to_all | solution.py:256
  26.3 4.2 %collective-permute-start.2 = (bf16[144,256]{1,0:T(8,128)(2,1)}, bf16[144,256]{1,0:T(8,128)(2,1)S(1)}, u32[]{:S(2)}, u32[]{:S(2)}) collective-permute-start(bf16[144,256]{1,0:T(8,128)(2,1)} %get-tuple-element.39.packet_ref.refs_0_.packet), channel_id=1, source_target_pairs={{0,16},{4,20},{8,24},{12,28},{16,32},{20,36},{24,40},{28,44},{32,4... | collective-permute-start | bytes 221192 | tf_op jit(solution)/shard_map/ppermute | solution.py:227
  30.5 3.1 %collective-permute-start.1 = (bf16[144,256]{1,0:T(8,128)(2,1)}, bf16[144,256]{1,0:T(8,128)(2,1)S(1)}, u32[]{:S(2)}, u32[]{:S(2)}) collective-permute-start(bf16[144,256]{1,0:T(8,128)(2,1)} %get-tuple-element.39.packet_ref.refs_0_.packet), channel_id=1, source_target_pairs={{0,8},{4,12},{8,16},{12,20},{16,24},{20,28},{24,32},{28,36},{32,40... | collective-permute-start | bytes 221192 | tf_op jit(solution)/shard_map/ppermute | solution.py:227
  33.6 5.1 %collective-permute-start = (bf16[144,256]{1,0:T(8,128)(2,1)}, bf16[144,256]{1,0:T(8,128)(2,1)S(1)}, u32[]{:S(2)}, u32[]{:S(2)}) collective-permute-start(bf16[144,256]{1,0:T(8,128)(2,1)} %get-tuple-element.39.packet_ref.refs_0_.packet), channel_id=1, source_target_pairs={{0,4},{4,8},{8,12},{12,16},{16,20},{20,24},{24,28},{28,32},{32,36}... | collective-permute-start | bytes 221192 | tf_op jit(solution)/shard_map/ppermute | solution.py:227
  38.7 0.0 all-to-all-done.totals_ref
  38.8 0.0 copy-start
  38.8 0.9 copy-done
  39.7 0.0 copy-start.6
  39.7 0.0 copy-start.7
  39.7 0.0 copy-start.1
  39.7 0.0 collective-permute-done.4.refs_5_.refs_0_
  39.7 1.4 %collective-permute-start.6 = (bf16[144,256]{1,0:T(8,128)(2,1)S(1)}, bf16[144,256]{1,0:T(8,128)(2,1)S(1)}, u32[]{:S(2)}, u32[]{:S(2)}) collective-permute-start(bf16[144,256]{1,0:T(8,128)(2,1)S(1)} %shard_map.130), channel_id=1, source_target_pairs={{0,256},{4,260},{8,264},{12,268},{16,272},{20,276},{24,280},{28,28... | collective-permute-start | bytes 221192 | tf_op jit(solution)/shard_map/ppermute | solution.py:227
  41.2 0.0 collective-permute-done.3.refs_4_.refs_1_
  41.2 1.3 %collective-permute-start.5 = (bf16[144,256]{1,0:T(8,128)(2,1)S(1)}, bf16[144,256]{1,0:T(8,128)(2,1)S(1)}, u32[]{:S(2)}, u32[]{:S(2)}) collective-permute-start(bf16[144,256]{1,0:T(8,128)(2,1)S(1)} %shard_map.130), channel_id=1, source_target_pairs={{0,128},{4,132},{8,136},{12,140},{16,144},{20,148},{24,152},{28,15... | collective-permute-start | bytes 221192 | tf_op jit(solution)/shard_map/ppermute | solution.py:227
  42.5 0.0 copy-done.2
  42.5 0.0 copy-done.3
  42.5 0.0 copy-done.4
  42.5 0.0 copy-done.5
  42.5 0.0 copy-done.6
  42.5 0.0 copy-done.7
  42.6 0.0 collective-permute-done.2.refs_3_.refs_4_
  42.6 0.0 collective-permute-done.1.refs_2_
  42.6 0.0 collective-permute-done.refs_1_.refs_3_
  42.6 4.2 %collective-permute-done.6.refs_7_.refs_0_ = bf16[144,256]{1,0:T(8,128)(2,1)S(1)} collective-permute-done((bf16[144,256]{1,0:T(8,128)(2,1)S(1)}, bf16[144,256]{1,0:T(8,128)(2,1)S(1)}, u32[]{:S(2)}, u32[]{:S(2)}) %collective-permute-start.6) | collective-permute-done | bytes 73760 | tf_op jit(solution)/shard_map/ppermute | solution.py:227
  46.8 1.4 %collective-permute-done.5.refs_6_.refs_1_ = bf16[144,256]{1,0:T(8,128)(2,1)S(1)} collective-permute-done((bf16[144,256]{1,0:T(8,128)(2,1)S(1)}, bf16[144,256]{1,0:T(8,128)(2,1)S(1)}, u32[]{:S(2)}, u32[]{:S(2)}) %collective-permute-start.5) | collective-permute-done | bytes 73760 | tf_op jit(solution)/shard_map/ppermute | solution.py:227
  48.2 1.4 %shard_map.131 = (f32[128,128]{1,0:T(8,128)S(1)}, f32[4,128]{1,0:T(4,128)S(1)}, bf16[256,1024]{1,0:T(8,128)(2,1)S(1)}, f32[256,1024]{1,0:T(8,128)S(1)}) custom-call(s32[1]{0:T(128)} %bitcast.group_ref, bf16[256,128]{1,0:T(8,128)(2,1)S(1)} %get-tuple-element.34.heads_ref, f32[128,128]{1,0:T(8,128)S(1)} %get-tuple-element.35.scaled_ref, ...), custom_call_target="tpu_custom_call" | custom-call | tf_op jit(solution)/shard_map/pallas_call | solution.py:213
  49.7 8.5 %psum.7.sums_ref = f32[4,128]{1,0:T(4,128)S(1)} all-reduce(f32[4,128]{1,0:T(4,128)S(1)} %get-tuple-element.41), channel_id=1, replica_groups=mesh['seq'=128,'head'=4] {'head'}, use_global_device_ids=true, to_apply=%region_0.0 | all-reduce | flops 512 | bytes 4096 | tf_op jit(solution)/shard_map/psum | solution.py:270
  58.1 0.8 shard_map.132
  58.9 3.7 %collective-permute-start.7 = (bf16[128,256]{1,0:T(8,128)(2,1)S(1)}, bf16[128,256]{1,0:T(8,128)(2,1)S(1)}, u32[]{:S(2)}, u32[]{:S(2)}) collective-permute-start(bf16[128,256]{1,0:T(8,128)(2,1)S(1)} %get-tuple-element.51), channel_id=1, source_target_pairs={{16,0},{20,4},{24,8},{28,12},{32,16},{36,20},{40,24},{44,28},{48,3... | collective-permute-start | bytes 196616 | tf_op jit(solution)/shard_map/ppermute | solution.py:227
  62.6 11.3 %collective-permute-start.8 = (bf16[128,256]{1,0:T(8,128)(2,1)S(1)}, bf16[128,256]{1,0:T(8,128)(2,1)S(1)}, u32[]{:S(2)}, u32[]{:S(2)}) collective-permute-start(bf16[128,256]{1,0:T(8,128)(2,1)S(1)} %get-tuple-element.52), channel_id=1, source_target_pairs={{64,0},{68,4},{72,8},{76,12},{80,16},{84,20},{88,24},{92,28},{96,3... | collective-permute-start | bytes 196616 | tf_op jit(solution)/shard_map/ppermute | solution.py:227
  73.9 0.9 shard_map.133
  74.9 2.0 %collective-permute-start.9 = (bf16[128,256]{1,0:T(8,128)(2,1)S(1)}, bf16[128,256]{1,0:T(8,128)(2,1)S(1)}, u32[]{:S(2)}, u32[]{:S(2)}) collective-permute-start(bf16[128,256]{1,0:T(8,128)(2,1)S(1)} %get-tuple-element.54), channel_id=1, source_target_pairs={{256,0},{260,4},{264,8},{268,12},{272,16},{276,20},{280,24},{284,2... | collective-permute-start | bytes 196616 | tf_op jit(solution)/shard_map/ppermute | solution.py:227
  76.9 1.7 %collective-permute-start.10 = (bf16[128,256]{1,0:T(8,128)(2,1)S(1)}, bf16[128,256]{1,0:T(8,128)(2,1)S(1)}, u32[]{:S(2)}, u32[]{:S(2)}) collective-permute-start(bf16[128,256]{1,0:T(8,128)(2,1)S(1)} %get-tuple-element.55), channel_id=1, source_target_pairs={{128,0},{132,4},{136,8},{140,12},{144,16},{148,20},{152,24},{156,2... | collective-permute-start | bytes 196616 | tf_op jit(solution)/shard_map/ppermute | solution.py:227
  78.6 3.1 %collective-permute-start.11 = (bf16[128,256]{1,0:T(8,128)(2,1)S(1)}, bf16[128,256]{1,0:T(8,128)(2,1)S(1)}, u32[]{:S(2)}, u32[]{:S(2)}) collective-permute-start(bf16[128,256]{1,0:T(8,128)(2,1)S(1)} %get-tuple-element.56), channel_id=1, source_target_pairs={{8,0},{12,4},{16,8},{20,12},{24,16},{28,20},{32,24},{36,28},{40,32... | collective-permute-start | bytes 196616 | tf_op jit(solution)/shard_map/ppermute | solution.py:227
  81.7 0.0 collective-permute-done.7.received_ref
  81.7 5.8 %collective-permute-start.12 = (bf16[128,256]{1,0:T(8,128)(2,1)S(1)}, bf16[128,256]{1,0:T(8,128)(2,1)S(1)}, u32[]{:S(2)}, u32[]{:S(2)}) collective-permute-start(bf16[128,256]{1,0:T(8,128)(2,1)S(1)} %get-tuple-element.57), channel_id=1, source_target_pairs={{4,0},{8,4},{12,8},{16,12},{20,16},{24,20},{28,24},{32,28},{36,32}... | collective-permute-start | bytes 196616 | tf_op jit(solution)/shard_map/ppermute | solution.py:227
  87.4 0.0 collective-permute-done.8.refs_0_
  87.5 2.1 %collective-permute-start.13 = (bf16[128,256]{1,0:T(8,128)(2,1)S(1)}, bf16[128,256]{1,0:T(8,128)(2,1)S(1)}, u32[]{:S(2)}, u32[]{:S(2)}) collective-permute-start(bf16[128,256]{1,0:T(8,128)(2,1)S(1)} %shard_map.135), channel_id=1, source_target_pairs={{16,0},{20,4},{24,8},{28,12},{32,16},{36,20},{40,24},{44,28},{48,3... | collective-permute-start | bytes 196616 | tf_op jit(solution)/shard_map/ppermute | solution.py:227
  89.6 1.1 %shard_map.134 = (bf16[128,128]{1,0:T(8,128)(2,1)}, bf16[128,128]{1,0:T(8,128)(2,1)}, bf16[128,128]{1,0:T(8,128)(2,1)}, f32[128,256]{1,0:T(8,128)S(1)}) custom-call(bf16[256,128]{1,0:T(8,128)(2,1)S(1)} %get-tuple-element.44.grads_ref, f32[256,128]{1,0:T(8,128)S(1)} %get-tuple-element.46.before_ref, bf16[256,128]{1,0:T(8,128)(2,1)S(1)} %get-tuple-element.34.heads_ref, ...), custom_call_target="tpu_custom_call" | custom-call | tf_op jit(solution)/shard_map/pallas_call | solution.py:213
  90.7 0.0 collective-permute-done.9.refs_1_
  90.7 0.0 collective-permute-done.10.refs_2_
  90.7 0.0 collective-permute-done.11.refs_3_
  90.8 0.0 collective-permute-done.12.refs_4_
  90.8 4.9 %collective-permute-done.13.refs_5_ = bf16[128,256]{1,0:T(8,128)(2,1)S(1)} collective-permute-done((bf16[128,256]{1,0:T(8,128)(2,1)S(1)}, bf16[128,256]{1,0:T(8,128)(2,1)S(1)}, u32[]{:S(2)}, u32[]{:S(2)}) %collective-permute-start.13) | collective-permute-done | bytes 65568 | tf_op jit(solution)/shard_map/ppermute | solution.py:227
  95.7 0.7 shard_map.136
  (8 shorter events, 0.1 us)
Async XLA Ops:
  2.1 37.6 %collective-permute-start.4 = (bf16[144,256]{1,0:T(8,128)(2,1)}, bf16[144,256]{1,0:T(8,128)(2,1)S(1)}, u32[]{:S(2)}, u32[]{:S(2)}) collective-permute-start(bf16[144,256]{1,0:T(8,128)(2,1)} %get-tuple-element.39.packet_ref.refs_0_.packet), channel_id=1, source_target_pairs={{0,64},{4,68},{8,72},{12,76},{16,80},{20,84},{24,88},{28,92},{32,9... | collective-permute-start | bytes 221192 | tf_op jit(solution)/shard_map/ppermute | solution.py:227
  17.5 23.6 %collective-permute-start.3 = (bf16[144,256]{1,0:T(8,128)(2,1)}, bf16[144,256]{1,0:T(8,128)(2,1)S(1)}, u32[]{:S(2)}, u32[]{:S(2)}) collective-permute-start(bf16[144,256]{1,0:T(8,128)(2,1)} %get-tuple-element.39.packet_ref.refs_0_.packet), channel_id=1, source_target_pairs={{0,32},{4,36},{8,40},{12,44},{16,48},{20,52},{24,56},{28,60},{32,6... | collective-permute-start | bytes 221192 | tf_op jit(solution)/shard_map/ppermute | solution.py:227
  21.6 17.2 %all-to-all-start = ((f32[32,1,128]{2,1,0:T(1,128)}), f32[32,1,128]{2,1,0:T(1,128)S(1)}, u32[]{:S(2)}, u32[]{:S(2)}) async-start(f32[32,1,128]{2,1,0:T(1,128)} %get-tuple-element.38), calls=%async_computation | async-start | bytes 32768 | tf_op jit(solution)/shard_map/all_to_all | solution.py:256
  26.3 16.3 %collective-permute-start.2 = (bf16[144,256]{1,0:T(8,128)(2,1)}, bf16[144,256]{1,0:T(8,128)(2,1)S(1)}, u32[]{:S(2)}, u32[]{:S(2)}) collective-permute-start(bf16[144,256]{1,0:T(8,128)(2,1)} %get-tuple-element.39.packet_ref.refs_0_.packet), channel_id=1, source_target_pairs={{0,16},{4,20},{8,24},{12,28},{16,32},{20,36},{24,40},{28,44},{32,4... | collective-permute-start | bytes 221192 | tf_op jit(solution)/shard_map/ppermute | solution.py:227
  30.5 12.1 %collective-permute-start.1 = (bf16[144,256]{1,0:T(8,128)(2,1)}, bf16[144,256]{1,0:T(8,128)(2,1)S(1)}, u32[]{:S(2)}, u32[]{:S(2)}) collective-permute-start(bf16[144,256]{1,0:T(8,128)(2,1)} %get-tuple-element.39.packet_ref.refs_0_.packet), channel_id=1, source_target_pairs={{0,8},{4,12},{8,16},{12,20},{16,24},{20,28},{24,32},{28,36},{32,40... | collective-permute-start | bytes 221192 | tf_op jit(solution)/shard_map/ppermute | solution.py:227
  33.6 9.0 %collective-permute-start = (bf16[144,256]{1,0:T(8,128)(2,1)}, bf16[144,256]{1,0:T(8,128)(2,1)S(1)}, u32[]{:S(2)}, u32[]{:S(2)}) collective-permute-start(bf16[144,256]{1,0:T(8,128)(2,1)} %get-tuple-element.39.packet_ref.refs_0_.packet), channel_id=1, source_target_pairs={{0,4},{4,8},{8,12},{12,16},{16,20},{20,24},{24,28},{28,32},{32,36}... | collective-permute-start | bytes 221192 | tf_op jit(solution)/shard_map/ppermute | solution.py:227
  38.8 0.9 copy-start
  39.6 2.8 %copy-start.2 = (bf16[128,128]{1,0:T(8,128)(2,1)S(1)}, bf16[128,128]{1,0:T(8,128)(2,1)}, u32[]{:S(2)}) copy-start(bf16[128,128]{1,0:T(8,128)(2,1)} %gate_ref.3) | copy-start | bytes 98308
  39.6 2.8 %copy-start.3 = (bf16[128,128]{1,0:T(8,128)(2,1)S(1)}, bf16[128,128]{1,0:T(8,128)(2,1)}, u32[]{:S(2)}) copy-start(bf16[128,128]{1,0:T(8,128)(2,1)} %cot_ref.3) | copy-start | bytes 98308
  39.6 2.9 %copy-start.4 = (bf16[128,128]{1,0:T(8,128)(2,1)S(1)}, bf16[128,128]{1,0:T(8,128)(2,1)}, u32[]{:S(2)}) copy-start(bf16[128,128]{1,0:T(8,128)(2,1)} %query_ref.1) | copy-start | bytes 98308
  39.7 2.9 %copy-start.5 = (s32[128,8]{0,1:T(8,128)S(1)}, s32[128,8]{0,1:T(8,128)}, u32[]{:S(2)}) copy-start(s32[128,8]{0,1:T(8,128)} %param.15) | copy-start | bytes 12292
  39.7 2.9 %copy-start.6 = (f32[128]{0:T(128)S(1)}, f32[128]{0:T(128)}, u32[]{:S(2)}) copy-start(f32[128]{0:T(128)} %param.17) | copy-start | bytes 1540
  39.7 2.9 %copy-start.7 = (f32[2,16]{1,0:T(2,128)S(1)}, f32[2,16]{1,0:T(2,128)}, u32[]{:S(2)}) copy-start(f32[2,16]{1,0:T(2,128)} %table_ref.1) | copy-start | bytes 388
  39.7 8.5 %copy-start.1 = (bf16[144,256]{1,0:T(8,128)(2,1)S(1)}, bf16[144,256]{1,0:T(8,128)(2,1)}, u32[]{:S(2)}) copy-start(bf16[144,256]{1,0:T(8,128)(2,1)} %get-tuple-element.39.packet_ref.refs_0_.packet) | copy-start | bytes 221188
  39.7 7.1 %collective-permute-start.6 = (bf16[144,256]{1,0:T(8,128)(2,1)S(1)}, bf16[144,256]{1,0:T(8,128)(2,1)S(1)}, u32[]{:S(2)}, u32[]{:S(2)}) collective-permute-start(bf16[144,256]{1,0:T(8,128)(2,1)S(1)} %shard_map.130), channel_id=1, source_target_pairs={{0,256},{4,260},{8,264},{12,268},{16,272},{20,276},{24,280},{28,28... | collective-permute-start | bytes 221192 | tf_op jit(solution)/shard_map/ppermute | solution.py:227
  41.2 7.1 %collective-permute-start.5 = (bf16[144,256]{1,0:T(8,128)(2,1)S(1)}, bf16[144,256]{1,0:T(8,128)(2,1)S(1)}, u32[]{:S(2)}, u32[]{:S(2)}) collective-permute-start(bf16[144,256]{1,0:T(8,128)(2,1)S(1)} %shard_map.130), channel_id=1, source_target_pairs={{0,128},{4,132},{8,136},{12,140},{16,144},{20,148},{24,152},{28,15... | collective-permute-start | bytes 221192 | tf_op jit(solution)/shard_map/ppermute | solution.py:227
  58.9 22.7 %collective-permute-start.7 = (bf16[128,256]{1,0:T(8,128)(2,1)S(1)}, bf16[128,256]{1,0:T(8,128)(2,1)S(1)}, u32[]{:S(2)}, u32[]{:S(2)}) collective-permute-start(bf16[128,256]{1,0:T(8,128)(2,1)S(1)} %get-tuple-element.51), channel_id=1, source_target_pairs={{16,0},{20,4},{24,8},{28,12},{32,16},{36,20},{40,24},{44,28},{48,3... | collective-permute-start | bytes 196616 | tf_op jit(solution)/shard_map/ppermute | solution.py:227
  62.6 24.8 %collective-permute-start.8 = (bf16[128,256]{1,0:T(8,128)(2,1)S(1)}, bf16[128,256]{1,0:T(8,128)(2,1)S(1)}, u32[]{:S(2)}, u32[]{:S(2)}) collective-permute-start(bf16[128,256]{1,0:T(8,128)(2,1)S(1)} %get-tuple-element.52), channel_id=1, source_target_pairs={{64,0},{68,4},{72,8},{76,12},{80,16},{84,20},{88,24},{92,28},{96,3... | collective-permute-start | bytes 196616 | tf_op jit(solution)/shard_map/ppermute | solution.py:227
  74.9 15.9 %collective-permute-start.9 = (bf16[128,256]{1,0:T(8,128)(2,1)S(1)}, bf16[128,256]{1,0:T(8,128)(2,1)S(1)}, u32[]{:S(2)}, u32[]{:S(2)}) collective-permute-start(bf16[128,256]{1,0:T(8,128)(2,1)S(1)} %get-tuple-element.54), channel_id=1, source_target_pairs={{256,0},{260,4},{264,8},{268,12},{272,16},{276,20},{280,24},{284,2... | collective-permute-start | bytes 196616 | tf_op jit(solution)/shard_map/ppermute | solution.py:227
  76.9 13.9 %collective-permute-start.10 = (bf16[128,256]{1,0:T(8,128)(2,1)S(1)}, bf16[128,256]{1,0:T(8,128)(2,1)S(1)}, u32[]{:S(2)}, u32[]{:S(2)}) collective-permute-start(bf16[128,256]{1,0:T(8,128)(2,1)S(1)} %get-tuple-element.55), channel_id=1, source_target_pairs={{128,0},{132,4},{136,8},{140,12},{144,16},{148,20},{152,24},{156,2... | collective-permute-start | bytes 196616 | tf_op jit(solution)/shard_map/ppermute | solution.py:227
  78.6 12.1 %collective-permute-start.11 = (bf16[128,256]{1,0:T(8,128)(2,1)S(1)}, bf16[128,256]{1,0:T(8,128)(2,1)S(1)}, u32[]{:S(2)}, u32[]{:S(2)}) collective-permute-start(bf16[128,256]{1,0:T(8,128)(2,1)S(1)} %get-tuple-element.56), channel_id=1, source_target_pairs={{8,0},{12,4},{16,8},{20,12},{24,16},{28,20},{32,24},{36,28},{40,32... | collective-permute-start | bytes 196616 | tf_op jit(solution)/shard_map/ppermute | solution.py:227
  81.7 9.1 %collective-permute-start.12 = (bf16[128,256]{1,0:T(8,128)(2,1)S(1)}, bf16[128,256]{1,0:T(8,128)(2,1)S(1)}, u32[]{:S(2)}, u32[]{:S(2)}) collective-permute-start(bf16[128,256]{1,0:T(8,128)(2,1)S(1)} %get-tuple-element.57), channel_id=1, source_target_pairs={{4,0},{8,4},{12,8},{16,12},{20,16},{24,20},{28,24},{32,28},{36,32}... | collective-permute-start | bytes 196616 | tf_op jit(solution)/shard_map/ppermute | solution.py:227
  87.5 8.2 %collective-permute-start.13 = (bf16[128,256]{1,0:T(8,128)(2,1)S(1)}, bf16[128,256]{1,0:T(8,128)(2,1)S(1)}, u32[]{:S(2)}, u32[]{:S(2)}) collective-permute-start(bf16[128,256]{1,0:T(8,128)(2,1)S(1)} %shard_map.135), channel_id=1, source_target_pairs={{16,0},{20,4},{24,8},{28,12},{32,16},{36,20},{40,24},{44,28},{48,3... | collective-permute-start | bytes 196616 | tf_op jit(solution)/shard_map/ppermute | solution.py:227

commit v4 on v3

--- a/solution.py
+++ b/solution.py
@@ -136,11 +136,13 @@
     terms = jnp.concatenate([att, att * att, scaled, scaled * att], axis=0)
     rows = dot(jnp.ones((8, F), f32), terms, NT, lax.Precision.HIGHEST)
     for r in range(4):
-        sums_ref[r : r + 1, :] = rows[0:1, r * C : (r + 1) * C]
+        for x in range(4):
+            sums_ref[x, r : r + 1, :] = rows[0:1, r * C : (r + 1) * C]
 
 
 def norm_terms(sums_ref, att_ref):
-    sums = jnp.concatenate([sums_ref[...], jnp.zeros((4, C), f32)], axis=0)
+    sums = sums_ref[0] + sums_ref[1] + sums_ref[2] + sums_ref[3]
+    sums = jnp.concatenate([sums, jnp.zeros((4, C), f32)], axis=0)
     cols = jnp.transpose(sums) * (1.0 / WIDE)
     mean, square, mean_scaled, mean_cross = (cols[:, r : r + 1] for r in range(4))
     inv_std = lax.rsqrt(square - mean * mean + norm_eps)
@@ -264,35 +266,18 @@
     packets = [packet] + [fetched[d] for d in DISTANCES]
     att, sums, weights, slopes = call(
         forward_kernel,
-        [((C, F), f32), ((4, C), f32), ((2 * C, 8 * C), bf16), ((2 * C, 8 * C), f32)],
+        [((C, F), f32), ((4, 4, C), f32), ((2 * C, 8 * C), bf16), ((2 * C, 8 * C), f32)],
         1,
     )(group, heads, scaled, lists, table, totals, *packets)
-    sums = lax.psum(sums, "head")
+    sums = lax.all_to_all(sums, "head", 0, 0)
     kept = (heads, weights, slopes)
     narrow, wide = ((C, 2 * F), bf16), ((C, 2 * F), f32)
-    blocks = (5, 4)
-    grads, acc, part16, part8 = call(
+    blocks = (5, 7, 4, 3, 6, 2, 1)
+    grads, acc, *parts = call(
         functools.partial(first_backward, blocks),
-        [((2 * C, F), bf16), ((2 * C, F), f32), narrow, narrow],
+        [((2 * C, F), bf16), ((2 * C, F), f32)] + [narrow] * 7,
     )(att, sums, heads, scaled, weights, slopes, *(packets[b] for b in blocks))
-
-    def more(blocks, acc, outs):
-        return call(functools.partial(next_backward, blocks), [((2 * C, F), f32)] + outs, cost=COST)(
-            grads, acc, *kept, *(packets[b] for b in blocks)
-        )
-
-    relayed = shifted(part8, -4)
-    acc, part64, part32, part2, part1, part4 = more((7, 6, 2, 1, 3), acc, [narrow] * 4 + [wide])
-    returned = [
-        shifted(part16, -16),
-        shifted(part64, -64),
-        shifted(part32, -32),
-        shifted(part2, -2),
-        shifted(part1, -1),
-    ]
-    part4, relayed, returned[0] = lax.optimization_barrier((part4, relayed, returned[0]))
-    (both,) = call(add_kernel, [narrow])(part4, relayed)
-    returned.append(shifted(both, -4))
+    returned = [shifted(part, -DISTANCES[b - 1]) for b, part in zip(blocks, parts)]
     layer_out, grad_query, grad_gate, own = call(
         last_backward, [((C, F), bf16)] * 3 + [((C, 2 * F), f32)]
     )(grads, acc, *kept, packet, att, sums, gate_rows, cotangent, gain)

time: 97 us -> 93.2 us (0.961)
  waiting for transfers between devices: 10.6 us -> 7.04 us
    psum x1 -> x0, blocking collectives: 8.47 us -> none  [per_device(): sums = lax.psum(sums, 'head')]
    all_to_all x0 -> x1, blocking collectives: none -> 8 us  [per_device(): sums = lax.all_to_all(sums, 'head', 0, 0)]
    ppermute x14, waiting for transfers between devices: 10.6 us -> 7.04 us  [shifted(): lax.ppermute(x, 'seq', [(i, i + by) for i in range(count) if 0 <= i + by...]
    pallas_call x8 -> x6, Pallas kernels: 5.04 us -> 5.04 us  [run(): pl.pallas_call(kernel, out_shape=[jax.ShapeDtypeStruct(s, t) for s, t in...]
  transfers between devices with their start and end apart: 15 -> 15, of which waited for: 3 -> 3; matrix products, arithmetic and copies ran while one was open for 0% -> 0% of each run, Pallas kernels for 2% -> 1%
where the time goes in v4:
time: 93.2 us; the launch traced here: 92.5 us
  starting transfers between devices  69.1 us (74%)
  blocking collectives  8 us (9%)
  waiting for transfers between devices  7.04 us (8%)
  Pallas kernels  6.49 us (7%)
  between operations  0.94 us (1%)
    ppermute x14, starting transfers between devices, shifted(): lax.ppermute(x, 'seq', [(i, i + by) for i in range(count) if 0 <= i + by...  64.4 us
    all_to_all x1, blocking collectives, per_device(): sums = lax.all_to_all(sums, 'head', 0, 0)  8 us
    ppermute x14, waiting for transfers between devices, shifted(): lax.ppermute(x, 'seq', [(i, i + by) for i in range(count) if 0 <= i + by...  7.04 us
    pallas_call x6, Pallas kernels, run(): pl.pallas_call(kernel, out_shape=[jax.ShapeDtypeStruct(s, t) for s, t in...  5.04 us
    all_to_all x1, starting transfers between devices, per_device(): totals = lax.all_to_all(totals, 'seq', 0, 0, axis_index_groups=rows)  4.73 us
  transfers between devices with their start and end apart: 15, of which 3 were waited for; matrix products, arithmetic and copies ran while one was open for 0% of the time, Pallas kernels for 1%

profile of v4, /device:TPU:25, one launch (start us, length us, event | category | flops | bytes accessed | tf_op | source)
XLA Modules:
  0.0 92.5 jit_solution(11323192580352744212)
XLA Ops:
  0.6 1.4 %shard_map.129 = (bf16[144,256]{1,0:T(8,128)(2,1)}, f32[32,1,128]{2,1,0:T(1,128)}) custom-call(bf16[128,128]{1,0:T(8,128)(2,1)} %key_ref.1, bf16[128,128]{1,0:T(8,128)(2,1)} %value_ref.1, s32[1,128]{1,0:T(1,128)} %bitcast.7), custom_call_target="tpu_custom_call" | custom-call | tf_op jit(solution)/shard_map/pallas_call | solution.py:246
  2.1 15.4 %collective-permute-start.4 = (bf16[144,256]{1,0:T(8,128)(2,1)}, bf16[144,256]{1,0:T(8,128)(2,1)S(1)}, u32[]{:S(2)}, u32[]{:S(2)}) collective-permute-start(bf16[144,256]{1,0:T(8,128)(2,1)} %get-tuple-element.35.packet_ref.refs_0_.packet), channel_id=1, source_target_pairs={{0,64},{4,68},{8,72},{12,76},{16,80},{20,84},{24,88},{28,92},{32,9... | collective-permute-start | bytes 221192 | tf_op jit(solution)/shard_map/ppermute | solution.py:229
  17.5 4.0 %collective-permute-start.3 = (bf16[144,256]{1,0:T(8,128)(2,1)}, bf16[144,256]{1,0:T(8,128)(2,1)S(1)}, u32[]{:S(2)}, u32[]{:S(2)}) collective-permute-start(bf16[144,256]{1,0:T(8,128)(2,1)} %get-tuple-element.35.packet_ref.refs_0_.packet), channel_id=1, source_target_pairs={{0,32},{4,36},{8,40},{12,44},{16,48},{20,52},{24,56},{28,60},{32,6... | collective-permute-start | bytes 221192 | tf_op jit(solution)/shard_map/ppermute | solution.py:229
  21.6 4.7 %all-to-all-start = ((f32[32,1,128]{2,1,0:T(1,128)}), f32[32,1,128]{2,1,0:T(1,128)S(1)}, u32[]{:S(2)}, u32[]{:S(2)}) async-start(f32[32,1,128]{2,1,0:T(1,128)} %get-tuple-element.34), calls=%async_computation | async-start | bytes 32768 | tf_op jit(solution)/shard_map/all_to_all | solution.py:258
  26.3 4.2 %collective-permute-start.2 = (bf16[144,256]{1,0:T(8,128)(2,1)}, bf16[144,256]{1,0:T(8,128)(2,1)S(1)}, u32[]{:S(2)}, u32[]{:S(2)}) collective-permute-start(bf16[144,256]{1,0:T(8,128)(2,1)} %get-tuple-element.35.packet_ref.refs_0_.packet), channel_id=1, source_target_pairs={{0,16},{4,20},{8,24},{12,28},{16,32},{20,36},{24,40},{28,44},{32,4... | collective-permute-start | bytes 221192 | tf_op jit(solution)/shard_map/ppermute | solution.py:229
  30.5 3.1 %collective-permute-start.1 = (bf16[144,256]{1,0:T(8,128)(2,1)}, bf16[144,256]{1,0:T(8,128)(2,1)S(1)}, u32[]{:S(2)}, u32[]{:S(2)}) collective-permute-start(bf16[144,256]{1,0:T(8,128)(2,1)} %get-tuple-element.35.packet_ref.refs_0_.packet), channel_id=1, source_target_pairs={{0,8},{4,12},{8,16},{12,20},{16,24},{20,28},{24,32},{28,36},{32,40... | collective-permute-start | bytes 221192 | tf_op jit(solution)/shard_map/ppermute | solution.py:229
  33.6 5.1 %collective-permute-start = (bf16[144,256]{1,0:T(8,128)(2,1)}, bf16[144,256]{1,0:T(8,128)(2,1)S(1)}, u32[]{:S(2)}, u32[]{:S(2)}) collective-permute-start(bf16[144,256]{1,0:T(8,128)(2,1)} %get-tuple-element.35.packet_ref.refs_0_.packet), channel_id=1, source_target_pairs={{0,4},{4,8},{8,12},{12,16},{16,20},{20,24},{24,28},{28,32},{32,36}... | collective-permute-start | bytes 221192 | tf_op jit(solution)/shard_map/ppermute | solution.py:229
  38.7 0.0 all-to-all-done.totals_ref
  38.8 0.0 copy-start
  38.8 0.9 copy-done
  39.7 0.0 copy-start.6
  39.7 0.0 copy-start.7
  39.7 0.0 copy-start.1
  39.7 0.0 collective-permute-done.4.refs_5_.refs_0_
  39.7 1.4 %collective-permute-start.6 = (bf16[144,256]{1,0:T(8,128)(2,1)S(1)}, bf16[144,256]{1,0:T(8,128)(2,1)S(1)}, u32[]{:S(2)}, u32[]{:S(2)}) collective-permute-start(bf16[144,256]{1,0:T(8,128)(2,1)S(1)} %shard_map.130), channel_id=1, source_target_pairs={{0,256},{4,260},{8,264},{12,268},{16,272},{20,276},{24,280},{28,28... | collective-permute-start | bytes 221192 | tf_op jit(solution)/shard_map/ppermute | solution.py:229
  41.2 0.0 collective-permute-done.3.refs_4_.refs_2_
  41.2 1.3 %collective-permute-start.5 = (bf16[144,256]{1,0:T(8,128)(2,1)S(1)}, bf16[144,256]{1,0:T(8,128)(2,1)S(1)}, u32[]{:S(2)}, u32[]{:S(2)}) collective-permute-start(bf16[144,256]{1,0:T(8,128)(2,1)S(1)} %shard_map.130), channel_id=1, source_target_pairs={{0,128},{4,132},{8,136},{12,140},{16,144},{20,148},{24,152},{28,15... | collective-permute-start | bytes 221192 | tf_op jit(solution)/shard_map/ppermute | solution.py:229
  42.5 0.0 copy-done.2
  42.5 0.0 copy-done.3
  42.5 0.0 copy-done.4
  42.5 0.0 copy-done.5
  42.5 0.0 copy-done.6
  42.5 0.0 copy-done.7
  42.6 0.0 collective-permute-done.2.refs_3_
  42.6 0.0 collective-permute-done.1.refs_2_.refs_5_
  42.6 0.0 collective-permute-done.refs_1_.refs_6_
  42.6 4.2 %collective-permute-done.6.refs_7_.refs_1_ = bf16[144,256]{1,0:T(8,128)(2,1)S(1)} collective-permute-done((bf16[144,256]{1,0:T(8,128)(2,1)S(1)}, bf16[144,256]{1,0:T(8,128)(2,1)S(1)}, u32[]{:S(2)}, u32[]{:S(2)}) %collective-permute-start.6) | collective-permute-done | bytes 73760 | tf_op jit(solution)/shard_map/ppermute | solution.py:229
  46.8 1.4 %collective-permute-done.5.refs_6_.refs_4_ = bf16[144,256]{1,0:T(8,128)(2,1)S(1)} collective-permute-done((bf16[144,256]{1,0:T(8,128)(2,1)S(1)}, bf16[144,256]{1,0:T(8,128)(2,1)S(1)}, u32[]{:S(2)}, u32[]{:S(2)}) %collective-permute-start.5) | collective-permute-done | bytes 73760 | tf_op jit(solution)/shard_map/ppermute | solution.py:229
  48.2 0.0 copy-done.1
  48.2 1.4 %shard_map.131 = (f32[128,128]{1,0:T(8,128)S(1)}, f32[4,4,128]{2,1,0:T(4,128)S(1)}, bf16[256,1024]{1,0:T(8,128)(2,1)S(1)}, f32[256,1024]{1,0:T(8,128)S(1)}) custom-call(s32[1]{0:T(128)} %bitcast.group_ref, bf16[256,128]{1,0:T(8,128)(2,1)S(1)} %get-tuple-element.30.heads_ref, f32[128,128]{1,0:T(8,128)S(1)} %get-tuple-element.31.scaled_ref, ...), custom_call_target="tpu_custom_call" | custom-call | tf_op jit(solution)/shard_map/pallas_call | solution.py:215
  49.7 8.0 %all_to_all.10.sums_ref = f32[4,4,128]{2,1,0:T(4,128)S(1)} all-to-all(f32[4,4,128]{2,1,0:T(4,128)S(1)} %get-tuple-element.37), channel_id=1, replica_groups=mesh['seq'=128,'head'=4] {'head'}, dimensions={0} | all-to-all | bytes 16384 | tf_op jit(solution)/shard_map/all_to_all | solution.py:272
  57.7 1.7 %shard_map.132 = (bf16[256,128]{1,0:T(8,128)(2,1)S(1)}, f32[256,128]{1,0:T(8,128)S(1)}, bf16[128,256]{1,0:T(8,128)(2,1)S(1)}, bf16[128,256]{1,0:T(8,128)(2,1)S(1...) custom-call(f32[128,128]{1,0:T(8,128)S(1)} %get-tuple-element.36.att, ...), custom_call_target="tpu_custom_call" | custom-call | tf_op jit(solution)/shard_map/pallas_call | solution.py:215
  59.4 9.8 %collective-permute-start.7 = (bf16[128,256]{1,0:T(8,128)(2,1)S(1)}, bf16[128,256]{1,0:T(8,128)(2,1)S(1)}, u32[]{:S(2)}, u32[]{:S(2)}) collective-permute-start(bf16[128,256]{1,0:T(8,128)(2,1)S(1)} %get-tuple-element.45), channel_id=1, source_target_pairs={{64,0},{68,4},{72,8},{76,12},{80,16},{84,20},{88,24},{92,28},{96,3... | collective-permute-start | bytes 196616 | tf_op jit(solution)/shard_map/ppermute | solution.py:229
  69.2 2.0 %collective-permute-start.8 = (bf16[128,256]{1,0:T(8,128)(2,1)S(1)}, bf16[128,256]{1,0:T(8,128)(2,1)S(1)}, u32[]{:S(2)}, u32[]{:S(2)}) collective-permute-start(bf16[128,256]{1,0:T(8,128)(2,1)S(1)} %get-tuple-element.46), channel_id=1, source_target_pairs={{256,0},{260,4},{264,8},{268,12},{272,16},{276,20},{280,24},{284,2... | collective-permute-start | bytes 196616 | tf_op jit(solution)/shard_map/ppermute | solution.py:229
  71.3 5.7 %collective-permute-start.9 = (bf16[128,256]{1,0:T(8,128)(2,1)S(1)}, bf16[128,256]{1,0:T(8,128)(2,1)S(1)}, u32[]{:S(2)}, u32[]{:S(2)}) collective-permute-start(bf16[128,256]{1,0:T(8,128)(2,1)S(1)} %get-tuple-element.47), channel_id=1, source_target_pairs={{32,0},{36,4},{40,8},{44,12},{48,16},{52,20},{56,24},{60,28},{64,3... | collective-permute-start | bytes 196616 | tf_op jit(solution)/shard_map/ppermute | solution.py:229
  76.9 2.6 %collective-permute-start.10 = (bf16[128,256]{1,0:T(8,128)(2,1)S(1)}, bf16[128,256]{1,0:T(8,128)(2,1)S(1)}, u32[]{:S(2)}, u32[]{:S(2)}) collective-permute-start(bf16[128,256]{1,0:T(8,128)(2,1)S(1)} %get-tuple-element.48), channel_id=1, source_target_pairs={{16,0},{20,4},{24,8},{28,12},{32,16},{36,20},{40,24},{44,28},{48,3... | collective-permute-start | bytes 196616 | tf_op jit(solution)/shard_map/ppermute | solution.py:229
  79.5 2.0 %collective-permute-start.11 = (bf16[128,256]{1,0:T(8,128)(2,1)S(1)}, bf16[128,256]{1,0:T(8,128)(2,1)S(1)}, u32[]{:S(2)}, u32[]{:S(2)}) collective-permute-start(bf16[128,256]{1,0:T(8,128)(2,1)S(1)} %get-tuple-element.49), channel_id=1, source_target_pairs={{128,0},{132,4},{136,8},{140,12},{144,16},{148,20},{152,24},{156,2... | collective-permute-start | bytes 196616 | tf_op jit(solution)/shard_map/ppermute | solution.py:229
  81.5 0.0 collective-permute-done.7.refs_0_
  81.6 2.6 %collective-permute-start.12 = (bf16[128,256]{1,0:T(8,128)(2,1)S(1)}, bf16[128,256]{1,0:T(8,128)(2,1)S(1)}, u32[]{:S(2)}, u32[]{:S(2)}) collective-permute-start(bf16[128,256]{1,0:T(8,128)(2,1)S(1)} %get-tuple-element.50), channel_id=1, source_target_pairs={{8,0},{12,4},{16,8},{20,12},{24,16},{28,20},{32,24},{36,28},{40,32... | collective-permute-start | bytes 196616 | tf_op jit(solution)/shard_map/ppermute | solution.py:229
  84.2 0.0 collective-permute-done.8.refs_1_
  84.2 5.1 %collective-permute-start.13 = (bf16[128,256]{1,0:T(8,128)(2,1)S(1)}, bf16[128,256]{1,0:T(8,128)(2,1)S(1)}, u32[]{:S(2)}, u32[]{:S(2)}) collective-permute-start(bf16[128,256]{1,0:T(8,128)(2,1)S(1)} %get-tuple-element.51), channel_id=1, source_target_pairs={{4,0},{8,4},{12,8},{16,12},{20,16},{24,20},{28,24},{32,28},{36,32}... | collective-permute-start | bytes 196616 | tf_op jit(solution)/shard_map/ppermute | solution.py:229
  89.3 1.1 %shard_map.133 = (bf16[128,128]{1,0:T(8,128)(2,1)}, bf16[128,128]{1,0:T(8,128)(2,1)}, bf16[128,128]{1,0:T(8,128)(2,1)}, f32[128,256]{1,0:T(8,128)S(1)}) custom-call(bf16[256,128]{1,0:T(8,128)(2,1)S(1)} %get-tuple-element.40.grads_ref, f32[256,128]{1,0:T(8,128)S(1)} %get-tuple-element.41.before_ref, bf16[256,128]{1,0:T(8,128)(2,1)S(1)} %get-tuple-element.30.heads_ref, ...), custom_call_target="tpu_custom_call" | custom-call | tf_op jit(solution)/shard_map/pallas_call | solution.py:215
  90.4 0.0 collective-permute-done.9.refs_2_
  90.4 0.0 collective-permute-done.10.refs_3_
  90.4 0.0 collective-permute-done.11.refs_4_
  90.4 0.0 collective-permute-done.12.refs_5_
  90.5 1.4 %collective-permute-done.13.refs_6_ = bf16[128,256]{1,0:T(8,128)(2,1)S(1)} collective-permute-done((bf16[128,256]{1,0:T(8,128)(2,1)S(1)}, bf16[128,256]{1,0:T(8,128)(2,1)S(1)}, u32[]{:S(2)}, u32[]{:S(2)}) %collective-permute-start.13) | collective-permute-done | bytes 65568 | tf_op jit(solution)/shard_map/ppermute | solution.py:229
  91.8 0.7 shard_map.134
  (6 shorter events, 0.1 us)
Async XLA Ops:
  2.1 37.6 %collective-permute-start.4 = (bf16[144,256]{1,0:T(8,128)(2,1)}, bf16[144,256]{1,0:T(8,128)(2,1)S(1)}, u32[]{:S(2)}, u32[]{:S(2)}) collective-permute-start(bf16[144,256]{1,0:T(8,128)(2,1)} %get-tuple-element.35.packet_ref.refs_0_.packet), channel_id=1, source_target_pairs={{0,64},{4,68},{8,72},{12,76},{16,80},{20,84},{24,88},{28,92},{32,9... | collective-permute-start | bytes 221192 | tf_op jit(solution)/shard_map/ppermute | solution.py:229
  17.5 23.6 %collective-permute-start.3 = (bf16[144,256]{1,0:T(8,128)(2,1)}, bf16[144,256]{1,0:T(8,128)(2,1)S(1)}, u32[]{:S(2)}, u32[]{:S(2)}) collective-permute-start(bf16[144,256]{1,0:T(8,128)(2,1)} %get-tuple-element.35.packet_ref.refs_0_.packet), channel_id=1, source_target_pairs={{0,32},{4,36},{8,40},{12,44},{16,48},{20,52},{24,56},{28,60},{32,6... | collective-permute-start | bytes 221192 | tf_op jit(solution)/shard_map/ppermute | solution.py:229
  21.6 17.2 %all-to-all-start = ((f32[32,1,128]{2,1,0:T(1,128)}), f32[32,1,128]{2,1,0:T(1,128)S(1)}, u32[]{:S(2)}, u32[]{:S(2)}) async-start(f32[32,1,128]{2,1,0:T(1,128)} %get-tuple-element.34), calls=%async_computation | async-start | bytes 32768 | tf_op jit(solution)/shard_map/all_to_all | solution.py:258
  26.3 16.3 %collective-permute-start.2 = (bf16[144,256]{1,0:T(8,128)(2,1)}, bf16[144,256]{1,0:T(8,128)(2,1)S(1)}, u32[]{:S(2)}, u32[]{:S(2)}) collective-permute-start(bf16[144,256]{1,0:T(8,128)(2,1)} %get-tuple-element.35.packet_ref.refs_0_.packet), channel_id=1, source_target_pairs={{0,16},{4,20},{8,24},{12,28},{16,32},{20,36},{24,40},{28,44},{32,4... | collective-permute-start | bytes 221192 | tf_op jit(solution)/shard_map/ppermute | solution.py:229
  30.5 12.1 %collective-permute-start.1 = (bf16[144,256]{1,0:T(8,128)(2,1)}, bf16[144,256]{1,0:T(8,128)(2,1)S(1)}, u32[]{:S(2)}, u32[]{:S(2)}) collective-permute-start(bf16[144,256]{1,0:T(8,128)(2,1)} %get-tuple-element.35.packet_ref.refs_0_.packet), channel_id=1, source_target_pairs={{0,8},{4,12},{8,16},{12,20},{16,24},{20,28},{24,32},{28,36},{32,40... | collective-permute-start | bytes 221192 | tf_op jit(solution)/shard_map/ppermute | solution.py:229
  33.6 9.0 %collective-permute-start = (bf16[144,256]{1,0:T(8,128)(2,1)}, bf16[144,256]{1,0:T(8,128)(2,1)S(1)}, u32[]{:S(2)}, u32[]{:S(2)}) collective-permute-start(bf16[144,256]{1,0:T(8,128)(2,1)} %get-tuple-element.35.packet_ref.refs_0_.packet), channel_id=1, source_target_pairs={{0,4},{4,8},{8,12},{12,16},{16,20},{20,24},{24,28},{28,32},{32,36}... | collective-permute-start | bytes 221192 | tf_op jit(solution)/shard_map/ppermute | solution.py:229
  38.8 0.9 copy-start
  39.6 2.8 %copy-start.2 = (bf16[128,128]{1,0:T(8,128)(2,1)S(1)}, bf16[128,128]{1,0:T(8,128)(2,1)}, u32[]{:S(2)}) copy-start(bf16[128,128]{1,0:T(8,128)(2,1)} %gate_ref.3) | copy-start | bytes 98308
  39.6 2.8 %copy-start.3 = (bf16[128,128]{1,0:T(8,128)(2,1)S(1)}, bf16[128,128]{1,0:T(8,128)(2,1)}, u32[]{:S(2)}) copy-start(bf16[128,128]{1,0:T(8,128)(2,1)} %cot_ref.3) | copy-start | bytes 98308
  39.6 2.9 %copy-start.4 = (bf16[128,128]{1,0:T(8,128)(2,1)S(1)}, bf16[128,128]{1,0:T(8,128)(2,1)}, u32[]{:S(2)}) copy-start(bf16[128,128]{1,0:T(8,128)(2,1)} %query_ref.1) | copy-start | bytes 98308
  39.7 2.9 %copy-start.5 = (s32[128,8]{0,1:T(8,128)S(1)}, s32[128,8]{0,1:T(8,128)}, u32[]{:S(2)}) copy-start(s32[128,8]{0,1:T(8,128)} %param.15) | copy-start | bytes 12292
  39.7 2.9 %copy-start.6 = (f32[128]{0:T(128)S(1)}, f32[128]{0:T(128)}, u32[]{:S(2)}) copy-start(f32[128]{0:T(128)} %param.17) | copy-start | bytes 1540
  39.7 2.9 %copy-start.7 = (f32[2,16]{1,0:T(2,128)S(1)}, f32[2,16]{1,0:T(2,128)}, u32[]{:S(2)}) copy-start(f32[2,16]{1,0:T(2,128)} %table_ref.1) | copy-start | bytes 388
  39.7 8.5 %copy-start.1 = (bf16[144,256]{1,0:T(8,128)(2,1)S(1)}, bf16[144,256]{1,0:T(8,128)(2,1)}, u32[]{:S(2)}) copy-start(bf16[144,256]{1,0:T(8,128)(2,1)} %get-tuple-element.35.packet_ref.refs_0_.packet) | copy-start | bytes 221188
  39.7 7.1 %collective-permute-start.6 = (bf16[144,256]{1,0:T(8,128)(2,1)S(1)}, bf16[144,256]{1,0:T(8,128)(2,1)S(1)}, u32[]{:S(2)}, u32[]{:S(2)}) collective-permute-start(bf16[144,256]{1,0:T(8,128)(2,1)S(1)} %shard_map.130), channel_id=1, source_target_pairs={{0,256},{4,260},{8,264},{12,268},{16,272},{20,276},{24,280},{28,28... | collective-permute-start | bytes 221192 | tf_op jit(solution)/shard_map/ppermute | solution.py:229
  41.2 7.1 %collective-permute-start.5 = (bf16[144,256]{1,0:T(8,128)(2,1)S(1)}, bf16[144,256]{1,0:T(8,128)(2,1)S(1)}, u32[]{:S(2)}, u32[]{:S(2)}) collective-permute-start(bf16[144,256]{1,0:T(8,128)(2,1)S(1)} %shard_map.130), channel_id=1, source_target_pairs={{0,128},{4,132},{8,136},{12,140},{16,144},{20,148},{24,152},{28,15... | collective-permute-start | bytes 221192 | tf_op jit(solution)/shard_map/ppermute | solution.py:229
  59.4 22.1 %collective-permute-start.7 = (bf16[128,256]{1,0:T(8,128)(2,1)S(1)}, bf16[128,256]{1,0:T(8,128)(2,1)S(1)}, u32[]{:S(2)}, u32[]{:S(2)}) collective-permute-start(bf16[128,256]{1,0:T(8,128)(2,1)S(1)} %get-tuple-element.45), channel_id=1, source_target_pairs={{64,0},{68,4},{72,8},{76,12},{80,16},{84,20},{88,24},{92,28},{96,3... | collective-permute-start | bytes 196616 | tf_op jit(solution)/shard_map/ppermute | solution.py:229
  69.2 14.9 %collective-permute-start.8 = (bf16[128,256]{1,0:T(8,128)(2,1)S(1)}, bf16[128,256]{1,0:T(8,128)(2,1)S(1)}, u32[]{:S(2)}, u32[]{:S(2)}) collective-permute-start(bf16[128,256]{1,0:T(8,128)(2,1)S(1)} %get-tuple-element.46), channel_id=1, source_target_pairs={{256,0},{260,4},{264,8},{268,12},{272,16},{276,20},{280,24},{284,2... | collective-permute-start | bytes 196616 | tf_op jit(solution)/shard_map/ppermute | solution.py:229
  71.3 19.2 %collective-permute-start.9 = (bf16[128,256]{1,0:T(8,128)(2,1)S(1)}, bf16[128,256]{1,0:T(8,128)(2,1)S(1)}, u32[]{:S(2)}, u32[]{:S(2)}) collective-permute-start(bf16[128,256]{1,0:T(8,128)(2,1)S(1)} %get-tuple-element.47), channel_id=1, source_target_pairs={{32,0},{36,4},{40,8},{44,12},{48,16},{52,20},{56,24},{60,28},{64,3... | collective-permute-start | bytes 196616 | tf_op jit(solution)/shard_map/ppermute | solution.py:229
  76.9 13.5 %collective-permute-start.10 = (bf16[128,256]{1,0:T(8,128)(2,1)S(1)}, bf16[128,256]{1,0:T(8,128)(2,1)S(1)}, u32[]{:S(2)}, u32[]{:S(2)}) collective-permute-start(bf16[128,256]{1,0:T(8,128)(2,1)S(1)} %get-tuple-element.48), channel_id=1, source_target_pairs={{16,0},{20,4},{24,8},{28,12},{32,16},{36,20},{40,24},{44,28},{48,3... | collective-permute-start | bytes 196616 | tf_op jit(solution)/shard_map/ppermute | solution.py:229
  79.5 10.9 %collective-permute-start.11 = (bf16[128,256]{1,0:T(8,128)(2,1)S(1)}, bf16[128,256]{1,0:T(8,128)(2,1)S(1)}, u32[]{:S(2)}, u32[]{:S(2)}) collective-permute-start(bf16[128,256]{1,0:T(8,128)(2,1)S(1)} %get-tuple-element.49), channel_id=1, source_target_pairs={{128,0},{132,4},{136,8},{140,12},{144,16},{148,20},{152,24},{156,2... | collective-permute-start | bytes 196616 | tf_op jit(solution)/shard_map/ppermute | solution.py:229
  81.6 8.9 %collective-permute-start.12 = (bf16[128,256]{1,0:T(8,128)(2,1)S(1)}, bf16[128,256]{1,0:T(8,128)(2,1)S(1)}, u32[]{:S(2)}, u32[]{:S(2)}) collective-permute-start(bf16[128,256]{1,0:T(8,128)(2,1)S(1)} %get-tuple-element.50), channel_id=1, source_target_pairs={{8,0},{12,4},{16,8},{20,12},{24,16},{28,20},{32,24},{36,28},{40,32... | collective-permute-start | bytes 196616 | tf_op jit(solution)/shard_map/ppermute | solution.py:229
  84.2 7.7 %collective-permute-start.13 = (bf16[128,256]{1,0:T(8,128)(2,1)S(1)}, bf16[128,256]{1,0:T(8,128)(2,1)S(1)}, u32[]{:S(2)}, u32[]{:S(2)}) collective-permute-start(bf16[128,256]{1,0:T(8,128)(2,1)S(1)} %get-tuple-element.51), channel_id=1, source_target_pairs={{4,0},{8,4},{12,8},{16,12},{20,16},{24,20},{28,24},{32,28},{36,32}... | collective-permute-start | bytes 196616 | tf_op jit(solution)/shard_map/ppermute | solution.py:229

commit v5 on v4

--- a/solution.py
+++ b/solution.py
@@ -17,7 +17,6 @@
 WIDE = 512.0
 f32, bf16, i32 = jnp.float32, jnp.bfloat16, jnp.int32
 VMEM = pl.BlockSpec(memory_space=pltpu.VMEM)
-COST = pl.CostEstimate(flops=8 * 10**8, bytes_accessed=2**20, transcendentals=0)
 PARAMS = pltpu.CompilerParams(vmem_limit_bytes=40 * 1024 * 1024)
 
 
@@ -150,10 +149,6 @@
     return inv_std, (att_ref[...] - mean) * inv_std, mean_scaled, mean_cross
 
 
-def add_kernel(part_ref, received_ref, out_ref):
-    out_ref[...] = (part_ref[...] + received_ref[...].astype(f32)).astype(bf16)
-
-
 def block_grads(b, queries, grads, weights_ref, slopes_ref, packet, out_ref):
     at = slice(b * C, (b + 1) * C)
     grad_weights = dot(grads, packet[:C, F:], NT)
@@ -163,7 +158,7 @@
     return dot(grad_scores, packet[:C, :F], NN)
 
 
-def first_backward(blocks, att_ref, sums_ref, heads_ref, scaled_ref, weights_ref, slopes_ref, *refs):
+def blocks_backward(blocks, att_ref, sums_ref, heads_ref, scaled_ref, weights_ref, slopes_ref, *refs):
     n = len(blocks)
     packets, grads_ref, acc_ref, sent = refs[:n], refs[n], refs[n + 1], refs[n + 2 :]
     inv_std, centered, mean_scaled, mean_cross = norm_terms(sums_ref, att_ref)
@@ -172,15 +167,6 @@
     grads_ref[...] = grads
     queries = heads_ref[...]
     acc = jnp.zeros((2 * C, F), f32)
-    for b, packet, out in zip(blocks, packets, sent):
-        acc = acc + block_grads(b, queries, grads, weights_ref, slopes_ref, packet, out)
-    acc_ref[...] = acc
-
-
-def next_backward(blocks, grads_ref, before_ref, heads_ref, weights_ref, slopes_ref, *refs):
-    n = len(blocks)
-    packets, acc_ref, sent = refs[:n], refs[n], refs[n + 1 :]
-    grads, queries, acc = grads_ref[...], heads_ref[...], before_ref[...]
     for b, packet, out in zip(blocks, packets, sent):
         acc = acc + block_grads(b, queries, grads, weights_ref, slopes_ref, packet, out)
     acc_ref[...] = acc
@@ -209,7 +195,7 @@
     dv_ref[...] = total[:, F:].astype(bf16)
 
 
-def call(kernel, outs, smem=0, cost=None):
+def call(kernel, outs, smem=0):
     def run(*args):
         specs = [pl.BlockSpec(memory_space=pltpu.SMEM)] * smem + [VMEM] * (len(args) - smem)
         return pl.pallas_call(
@@ -218,7 +204,6 @@
             in_specs=specs,
             out_specs=[VMEM] * len(outs),
             compiler_params=PARAMS,
-            cost_estimate=cost,
         )(*args)
 
     return run
@@ -271,10 +256,10 @@
     )(group, heads, scaled, lists, table, totals, *packets)
     sums = lax.all_to_all(sums, "head", 0, 0)
     kept = (heads, weights, slopes)
-    narrow, wide = ((C, 2 * F), bf16), ((C, 2 * F), f32)
-    blocks = (5, 7, 4, 3, 6, 2, 1)
+    narrow = ((C, 2 * F), bf16)
+    blocks = (5, 7, 4, 6, 3, 2, 1)
     grads, acc, *parts = call(
-        functools.partial(first_backward, blocks),
+        functools.partial(blocks_backward, blocks),
         [((2 * C, F), bf16), ((2 * C, F), f32)] + [narrow] * 7,
     )(att, sums, heads, scaled, weights, slopes, *(packets[b] for b in blocks))
     returned = [shifted(part, -DISTANCES[b - 1]) for b, part in zip(blocks, parts)]

time: 93.2 us -> 93.2 us (level)
  no operation moved by 1% of the time
where the time goes in v5:
time: 93.2 us; the launch traced here: 92.5 us
  starting transfers between devices  69.1 us (74%)
  blocking collectives  8 us (9%)
  waiting for transfers between devices  7.04 us (8%)
  Pallas kernels  6.49 us (7%)
  between operations  0.94 us (1%)
    ppermute x14, starting transfers between devices, shifted(): lax.ppermute(x, 'seq', [(i, i + by) for i in range(count) if 0 <= i + by...  64.4 us
    all_to_all x1, blocking collectives, per_device(): sums = lax.all_to_all(sums, 'head', 0, 0)  8 us
    ppermute x14, waiting for transfers between devices, shifted(): lax.ppermute(x, 'seq', [(i, i + by) for i in range(count) if 0 <= i + by...  7.04 us
    pallas_call x6, Pallas kernels, run(): pl.pallas_call(kernel, out_shape=[jax.ShapeDtypeStruct(s, t) for s, t in...  5.05 us
    all_to_all x1, starting transfers between devices, per_device(): totals = lax.all_to_all(totals, 'seq', 0, 0, axis_index_groups=rows)  4.73 us
  transfers between devices with their start and end apart: 15, of which 3 were waited for; matrix products, arithmetic and copies ran while one was open for 0% of the time, Pallas kernels for 1%

profile of v5, /device:TPU:25, one launch (start us, length us, event | category | flops | bytes accessed | tf_op | source)
XLA Modules:
  0.0 92.5 jit_solution(11435039198364834594)
XLA Ops:
  0.6 1.4 %shard_map.129 = (bf16[144,256]{1,0:T(8,128)(2,1)}, f32[32,1,128]{2,1,0:T(1,128)}) custom-call(bf16[128,128]{1,0:T(8,128)(2,1)} %key_ref.1, bf16[128,128]{1,0:T(8,128)(2,1)} %value_ref.1, s32[1,128]{1,0:T(1,128)} %bitcast.7), custom_call_target="tpu_custom_call" | custom-call | tf_op jit(solution)/shard_map/pallas_call | solution.py:231
  2.1 15.4 %collective-permute-start.4 = (bf16[144,256]{1,0:T(8,128)(2,1)}, bf16[144,256]{1,0:T(8,128)(2,1)S(1)}, u32[]{:S(2)}, u32[]{:S(2)}) collective-permute-start(bf16[144,256]{1,0:T(8,128)(2,1)} %get-tuple-element.35.packet_ref.refs_0_.packet), channel_id=1, source_target_pairs={{0,64},{4,68},{8,72},{12,76},{16,80},{20,84},{24,88},{28,92},{32,9... | collective-permute-start | bytes 221192 | tf_op jit(solution)/shard_map/ppermute | solution.py:214
  17.5 4.0 %collective-permute-start.3 = (bf16[144,256]{1,0:T(8,128)(2,1)}, bf16[144,256]{1,0:T(8,128)(2,1)S(1)}, u32[]{:S(2)}, u32[]{:S(2)}) collective-permute-start(bf16[144,256]{1,0:T(8,128)(2,1)} %get-tuple-element.35.packet_ref.refs_0_.packet), channel_id=1, source_target_pairs={{0,32},{4,36},{8,40},{12,44},{16,48},{20,52},{24,56},{28,60},{32,6... | collective-permute-start | bytes 221192 | tf_op jit(solution)/shard_map/ppermute | solution.py:214
  21.6 4.7 %all-to-all-start = ((f32[32,1,128]{2,1,0:T(1,128)}), f32[32,1,128]{2,1,0:T(1,128)S(1)}, u32[]{:S(2)}, u32[]{:S(2)}) async-start(f32[32,1,128]{2,1,0:T(1,128)} %get-tuple-element.34), calls=%async_computation | async-start | bytes 32768 | tf_op jit(solution)/shard_map/all_to_all | solution.py:243
  26.3 4.2 %collective-permute-start.2 = (bf16[144,256]{1,0:T(8,128)(2,1)}, bf16[144,256]{1,0:T(8,128)(2,1)S(1)}, u32[]{:S(2)}, u32[]{:S(2)}) collective-permute-start(bf16[144,256]{1,0:T(8,128)(2,1)} %get-tuple-element.35.packet_ref.refs_0_.packet), channel_id=1, source_target_pairs={{0,16},{4,20},{8,24},{12,28},{16,32},{20,36},{24,40},{28,44},{32,4... | collective-permute-start | bytes 221192 | tf_op jit(solution)/shard_map/ppermute | solution.py:214
  30.5 3.1 %collective-permute-start.1 = (bf16[144,256]{1,0:T(8,128)(2,1)}, bf16[144,256]{1,0:T(8,128)(2,1)S(1)}, u32[]{:S(2)}, u32[]{:S(2)}) collective-permute-start(bf16[144,256]{1,0:T(8,128)(2,1)} %get-tuple-element.35.packet_ref.refs_0_.packet), channel_id=1, source_target_pairs={{0,8},{4,12},{8,16},{12,20},{16,24},{20,28},{24,32},{28,36},{32,40... | collective-permute-start | bytes 221192 | tf_op jit(solution)/shard_map/ppermute | solution.py:214
  33.6 5.1 %collective-permute-start = (bf16[144,256]{1,0:T(8,128)(2,1)}, bf16[144,256]{1,0:T(8,128)(2,1)S(1)}, u32[]{:S(2)}, u32[]{:S(2)}) collective-permute-start(bf16[144,256]{1,0:T(8,128)(2,1)} %get-tuple-element.35.packet_ref.refs_0_.packet), channel_id=1, source_target_pairs={{0,4},{4,8},{8,12},{12,16},{16,20},{20,24},{24,28},{28,32},{32,36}... | collective-permute-start | bytes 221192 | tf_op jit(solution)/shard_map/ppermute | solution.py:214
  38.7 0.0 all-to-all-done.totals_ref
  38.8 0.0 copy-start
  38.8 0.9 copy-done
  39.7 0.0 copy-start.6
  39.7 0.0 copy-start.7
  39.7 0.0 copy-start.1
  39.7 0.0 collective-permute-done.4.refs_5_.refs_0_
  39.7 1.4 %collective-permute-start.6 = (bf16[144,256]{1,0:T(8,128)(2,1)S(1)}, bf16[144,256]{1,0:T(8,128)(2,1)S(1)}, u32[]{:S(2)}, u32[]{:S(2)}) collective-permute-start(bf16[144,256]{1,0:T(8,128)(2,1)S(1)} %shard_map.130), channel_id=1, source_target_pairs={{0,256},{4,260},{8,264},{12,268},{16,272},{20,276},{24,280},{28,28... | collective-permute-start | bytes 221192 | tf_op jit(solution)/shard_map/ppermute | solution.py:214
  41.2 0.0 collective-permute-done.3.refs_4_.refs_2_
  41.2 1.3 %collective-permute-start.5 = (bf16[144,256]{1,0:T(8,128)(2,1)S(1)}, bf16[144,256]{1,0:T(8,128)(2,1)S(1)}, u32[]{:S(2)}, u32[]{:S(2)}) collective-permute-start(bf16[144,256]{1,0:T(8,128)(2,1)S(1)} %shard_map.130), channel_id=1, source_target_pairs={{0,128},{4,132},{8,136},{12,140},{16,144},{20,148},{24,152},{28,15... | collective-permute-start | bytes 221192 | tf_op jit(solution)/shard_map/ppermute | solution.py:214
  42.5 0.0 copy-done.2
  42.5 0.0 copy-done.3
  42.5 0.0 copy-done.4
  42.5 0.0 copy-done.5
  42.5 0.0 copy-done.6
  42.5 0.0 copy-done.7
  42.6 0.0 collective-permute-done.2.refs_3_.refs_4_
  42.6 0.0 collective-permute-done.1.refs_2_.refs_5_
  42.6 0.0 collective-permute-done.refs_1_.refs_6_
  42.6 4.2 %collective-permute-done.6.refs_7_.refs_1_ = bf16[144,256]{1,0:T(8,128)(2,1)S(1)} collective-permute-done((bf16[144,256]{1,0:T(8,128)(2,1)S(1)}, bf16[144,256]{1,0:T(8,128)(2,1)S(1)}, u32[]{:S(2)}, u32[]{:S(2)}) %collective-permute-start.6) | collective-permute-done | bytes 73760 | tf_op jit(solution)/shard_map/ppermute | solution.py:214
  46.8 1.4 %collective-permute-done.5.refs_6_.refs_3_ = bf16[144,256]{1,0:T(8,128)(2,1)S(1)} collective-permute-done((bf16[144,256]{1,0:T(8,128)(2,1)S(1)}, bf16[144,256]{1,0:T(8,128)(2,1)S(1)}, u32[]{:S(2)}, u32[]{:S(2)}) %collective-permute-start.5) | collective-permute-done | bytes 73760 | tf_op jit(solution)/shard_map/ppermute | solution.py:214
  48.2 0.0 copy-done.1
  48.2 1.4 %shard_map.131 = (f32[128,128]{1,0:T(8,128)S(1)}, f32[4,4,128]{2,1,0:T(4,128)S(1)}, bf16[256,1024]{1,0:T(8,128)(2,1)S(1)}, f32[256,1024]{1,0:T(8,128)S(1)}) custom-call(s32[1]{0:T(128)} %bitcast.group_ref, bf16[256,128]{1,0:T(8,128)(2,1)S(1)} %get-tuple-element.30.heads_ref, f32[128,128]{1,0:T(8,128)S(1)} %get-tuple-element.31.scaled_ref, ...), custom_call_target="tpu_custom_call" | custom-call | tf_op jit(solution)/shard_map/pallas_call | solution.py:201
  49.7 8.0 %all_to_all.10.sums_ref = f32[4,4,128]{2,1,0:T(4,128)S(1)} all-to-all(f32[4,4,128]{2,1,0:T(4,128)S(1)} %get-tuple-element.37), channel_id=1, replica_groups=mesh['seq'=128,'head'=4] {'head'}, dimensions={0} | all-to-all | bytes 16384 | tf_op jit(solution)/shard_map/all_to_all | solution.py:257
  57.7 1.7 %shard_map.132 = (bf16[256,128]{1,0:T(8,128)(2,1)S(1)}, f32[256,128]{1,0:T(8,128)S(1)}, bf16[128,256]{1,0:T(8,128)(2,1)S(1)}, bf16[128,256]{1,0:T(8,128)(2,1)S(1...) custom-call(f32[128,128]{1,0:T(8,128)S(1)} %get-tuple-element.36.att, ...), custom_call_target="tpu_custom_call" | custom-call | tf_op jit(solution)/shard_map/pallas_call | solution.py:201
  59.4 9.8 %collective-permute-start.7 = (bf16[128,256]{1,0:T(8,128)(2,1)S(1)}, bf16[128,256]{1,0:T(8,128)(2,1)S(1)}, u32[]{:S(2)}, u32[]{:S(2)}) collective-permute-start(bf16[128,256]{1,0:T(8,128)(2,1)S(1)} %get-tuple-element.45), channel_id=1, source_target_pairs={{64,0},{68,4},{72,8},{76,12},{80,16},{84,20},{88,24},{92,28},{96,3... | collective-permute-start | bytes 196616 | tf_op jit(solution)/shard_map/ppermute | solution.py:214
  69.2 2.0 %collective-permute-start.8 = (bf16[128,256]{1,0:T(8,128)(2,1)S(1)}, bf16[128,256]{1,0:T(8,128)(2,1)S(1)}, u32[]{:S(2)}, u32[]{:S(2)}) collective-permute-start(bf16[128,256]{1,0:T(8,128)(2,1)S(1)} %get-tuple-element.46), channel_id=1, source_target_pairs={{256,0},{260,4},{264,8},{268,12},{272,16},{276,20},{280,24},{284,2... | collective-permute-start | bytes 196616 | tf_op jit(solution)/shard_map/ppermute | solution.py:214
  71.3 5.7 %collective-permute-start.9 = (bf16[128,256]{1,0:T(8,128)(2,1)S(1)}, bf16[128,256]{1,0:T(8,128)(2,1)S(1)}, u32[]{:S(2)}, u32[]{:S(2)}) collective-permute-start(bf16[128,256]{1,0:T(8,128)(2,1)S(1)} %get-tuple-element.47), channel_id=1, source_target_pairs={{32,0},{36,4},{40,8},{44,12},{48,16},{52,20},{56,24},{60,28},{64,3... | collective-permute-start | bytes 196616 | tf_op jit(solution)/shard_map/ppermute | solution.py:214
  76.9 2.2 %collective-permute-start.10 = (bf16[128,256]{1,0:T(8,128)(2,1)S(1)}, bf16[128,256]{1,0:T(8,128)(2,1)S(1)}, u32[]{:S(2)}, u32[]{:S(2)}) collective-permute-start(bf16[128,256]{1,0:T(8,128)(2,1)S(1)} %get-tuple-element.48), channel_id=1, source_target_pairs={{128,0},{132,4},{136,8},{140,12},{144,16},{148,20},{152,24},{156,2... | collective-permute-start | bytes 196616 | tf_op jit(solution)/shard_map/ppermute | solution.py:214
  79.1 2.4 %collective-permute-start.11 = (bf16[128,256]{1,0:T(8,128)(2,1)S(1)}, bf16[128,256]{1,0:T(8,128)(2,1)S(1)}, u32[]{:S(2)}, u32[]{:S(2)}) collective-permute-start(bf16[128,256]{1,0:T(8,128)(2,1)S(1)} %get-tuple-element.49), channel_id=1, source_target_pairs={{16,0},{20,4},{24,8},{28,12},{32,16},{36,20},{40,24},{44,28},{48,3... | collective-permute-start | bytes 196616 | tf_op jit(solution)/shard_map/ppermute | solution.py:214
  81.5 0.0 collective-permute-done.7.refs_0_
  81.5 2.6 %collective-permute-start.12 = (bf16[128,256]{1,0:T(8,128)(2,1)S(1)}, bf16[128,256]{1,0:T(8,128)(2,1)S(1)}, u32[]{:S(2)}, u32[]{:S(2)}) collective-permute-start(bf16[128,256]{1,0:T(8,128)(2,1)S(1)} %get-tuple-element.50), channel_id=1, source_target_pairs={{8,0},{12,4},{16,8},{20,12},{24,16},{28,20},{32,24},{36,28},{40,32... | collective-permute-start | bytes 196616 | tf_op jit(solution)/shard_map/ppermute | solution.py:214
  84.2 0.0 collective-permute-done.8.refs_1_
  84.2 5.1 %collective-permute-start.13 = (bf16[128,256]{1,0:T(8,128)(2,1)S(1)}, bf16[128,256]{1,0:T(8,128)(2,1)S(1)}, u32[]{:S(2)}, u32[]{:S(2)}) collective-permute-start(bf16[128,256]{1,0:T(8,128)(2,1)S(1)} %get-tuple-element.51), channel_id=1, source_target_pairs={{4,0},{8,4},{12,8},{16,12},{20,16},{24,20},{28,24},{32,28},{36,32}... | collective-permute-start | bytes 196616 | tf_op jit(solution)/shard_map/ppermute | solution.py:214
  89.3 1.1 %shard_map.133 = (bf16[128,128]{1,0:T(8,128)(2,1)}, bf16[128,128]{1,0:T(8,128)(2,1)}, bf16[128,128]{1,0:T(8,128)(2,1)}, f32[128,256]{1,0:T(8,128)S(1)}) custom-call(bf16[256,128]{1,0:T(8,128)(2,1)S(1)} %get-tuple-element.40.grads_ref, f32[256,128]{1,0:T(8,128)S(1)} %get-tuple-element.41.before_ref, bf16[256,128]{1,0:T(8,128)(2,1)S(1)} %get-tuple-element.30.heads_ref, ...), custom_call_target="tpu_custom_call" | custom-call | tf_op jit(solution)/shard_map/pallas_call | solution.py:201
  90.4 0.0 collective-permute-done.9.refs_2_
  90.4 0.0 collective-permute-done.10.refs_3_
  90.4 0.0 collective-permute-done.11.refs_4_
  90.4 0.0 collective-permute-done.12.refs_5_
  90.5 1.4 %collective-permute-done.13.refs_6_ = bf16[128,256]{1,0:T(8,128)(2,1)S(1)} collective-permute-done((bf16[128,256]{1,0:T(8,128)(2,1)S(1)}, bf16[128,256]{1,0:T(8,128)(2,1)S(1)}, u32[]{:S(2)}, u32[]{:S(2)}) %collective-permute-start.13) | collective-permute-done | bytes 65568 | tf_op jit(solution)/shard_map/ppermute | solution.py:214
  91.8 0.7 shard_map.134
  (6 shorter events, 0.1 us)
Async XLA Ops:
  2.1 37.6 %collective-permute-start.4 = (bf16[144,256]{1,0:T(8,128)(2,1)}, bf16[144,256]{1,0:T(8,128)(2,1)S(1)}, u32[]{:S(2)}, u32[]{:S(2)}) collective-permute-start(bf16[144,256]{1,0:T(8,128)(2,1)} %get-tuple-element.35.packet_ref.refs_0_.packet), channel_id=1, source_target_pairs={{0,64},{4,68},{8,72},{12,76},{16,80},{20,84},{24,88},{28,92},{32,9... | collective-permute-start | bytes 221192 | tf_op jit(solution)/shard_map/ppermute | solution.py:214
  17.5 23.6 %collective-permute-start.3 = (bf16[144,256]{1,0:T(8,128)(2,1)}, bf16[144,256]{1,0:T(8,128)(2,1)S(1)}, u32[]{:S(2)}, u32[]{:S(2)}) collective-permute-start(bf16[144,256]{1,0:T(8,128)(2,1)} %get-tuple-element.35.packet_ref.refs_0_.packet), channel_id=1, source_target_pairs={{0,32},{4,36},{8,40},{12,44},{16,48},{20,52},{24,56},{28,60},{32,6... | collective-permute-start | bytes 221192 | tf_op jit(solution)/shard_map/ppermute | solution.py:214
  21.6 17.2 %all-to-all-start = ((f32[32,1,128]{2,1,0:T(1,128)}), f32[32,1,128]{2,1,0:T(1,128)S(1)}, u32[]{:S(2)}, u32[]{:S(2)}) async-start(f32[32,1,128]{2,1,0:T(1,128)} %get-tuple-element.34), calls=%async_computation | async-start | bytes 32768 | tf_op jit(solution)/shard_map/all_to_all | solution.py:243
  26.3 16.3 %collective-permute-start.2 = (bf16[144,256]{1,0:T(8,128)(2,1)}, bf16[144,256]{1,0:T(8,128)(2,1)S(1)}, u32[]{:S(2)}, u32[]{:S(2)}) collective-permute-start(bf16[144,256]{1,0:T(8,128)(2,1)} %get-tuple-element.35.packet_ref.refs_0_.packet), channel_id=1, source_target_pairs={{0,16},{4,20},{8,24},{12,28},{16,32},{20,36},{24,40},{28,44},{32,4... | collective-permute-start | bytes 221192 | tf_op jit(solution)/shard_map/ppermute | solution.py:214
  30.5 12.1 %collective-permute-start.1 = (bf16[144,256]{1,0:T(8,128)(2,1)}, bf16[144,256]{1,0:T(8,128)(2,1)S(1)}, u32[]{:S(2)}, u32[]{:S(2)}) collective-permute-start(bf16[144,256]{1,0:T(8,128)(2,1)} %get-tuple-element.35.packet_ref.refs_0_.packet), channel_id=1, source_target_pairs={{0,8},{4,12},{8,16},{12,20},{16,24},{20,28},{24,32},{28,36},{32,40... | collective-permute-start | bytes 221192 | tf_op jit(solution)/shard_map/ppermute | solution.py:214
  33.6 9.0 %collective-permute-start = (bf16[144,256]{1,0:T(8,128)(2,1)}, bf16[144,256]{1,0:T(8,128)(2,1)S(1)}, u32[]{:S(2)}, u32[]{:S(2)}) collective-permute-start(bf16[144,256]{1,0:T(8,128)(2,1)} %get-tuple-element.35.packet_ref.refs_0_.packet), channel_id=1, source_target_pairs={{0,4},{4,8},{8,12},{12,16},{16,20},{20,24},{24,28},{28,32},{32,36}... | collective-permute-start | bytes 221192 | tf_op jit(solution)/shard_map/ppermute | solution.py:214
  38.8 0.9 copy-start
  39.6 2.8 %copy-start.2 = (bf16[128,128]{1,0:T(8,128)(2,1)S(1)}, bf16[128,128]{1,0:T(8,128)(2,1)}, u32[]{:S(2)}) copy-start(bf16[128,128]{1,0:T(8,128)(2,1)} %gate_ref.3) | copy-start | bytes 98308
  39.6 2.8 %copy-start.3 = (bf16[128,128]{1,0:T(8,128)(2,1)S(1)}, bf16[128,128]{1,0:T(8,128)(2,1)}, u32[]{:S(2)}) copy-start(bf16[128,128]{1,0:T(8,128)(2,1)} %cot_ref.3) | copy-start | bytes 98308
  39.6 2.9 %copy-start.4 = (bf16[128,128]{1,0:T(8,128)(2,1)S(1)}, bf16[128,128]{1,0:T(8,128)(2,1)}, u32[]{:S(2)}) copy-start(bf16[128,128]{1,0:T(8,128)(2,1)} %query_ref.1) | copy-start | bytes 98308
  39.7 2.9 %copy-start.5 = (s32[128,8]{0,1:T(8,128)S(1)}, s32[128,8]{0,1:T(8,128)}, u32[]{:S(2)}) copy-start(s32[128,8]{0,1:T(8,128)} %param.15) | copy-start | bytes 12292
  39.7 2.9 %copy-start.6 = (f32[128]{0:T(128)S(1)}, f32[128]{0:T(128)}, u32[]{:S(2)}) copy-start(f32[128]{0:T(128)} %param.17) | copy-start | bytes 1540
  39.7 2.9 %copy-start.7 = (f32[2,16]{1,0:T(2,128)S(1)}, f32[2,16]{1,0:T(2,128)}, u32[]{:S(2)}) copy-start(f32[2,16]{1,0:T(2,128)} %table_ref.1) | copy-start | bytes 388
  39.7 8.5 %copy-start.1 = (bf16[144,256]{1,0:T(8,128)(2,1)S(1)}, bf16[144,256]{1,0:T(8,128)(2,1)}, u32[]{:S(2)}) copy-start(bf16[144,256]{1,0:T(8,128)(2,1)} %get-tuple-element.35.packet_ref.refs_0_.packet) | copy-start | bytes 221188
  39.7 7.1 %collective-permute-start.6 = (bf16[144,256]{1,0:T(8,128)(2,1)S(1)}, bf16[144,256]{1,0:T(8,128)(2,1)S(1)}, u32[]{:S(2)}, u32[]{:S(2)}) collective-permute-start(bf16[144,256]{1,0:T(8,128)(2,1)S(1)} %shard_map.130), channel_id=1, source_target_pairs={{0,256},{4,260},{8,264},{12,268},{16,272},{20,276},{24,280},{28,28... | collective-permute-start | bytes 221192 | tf_op jit(solution)/shard_map/ppermute | solution.py:214
  41.2 7.1 %collective-permute-start.5 = (bf16[144,256]{1,0:T(8,128)(2,1)S(1)}, bf16[144,256]{1,0:T(8,128)(2,1)S(1)}, u32[]{:S(2)}, u32[]{:S(2)}) collective-permute-start(bf16[144,256]{1,0:T(8,128)(2,1)S(1)} %shard_map.130), channel_id=1, source_target_pairs={{0,128},{4,132},{8,136},{12,140},{16,144},{20,148},{24,152},{28,15... | collective-permute-start | bytes 221192 | tf_op jit(solution)/shard_map/ppermute | solution.py:214
  59.4 22.1 %collective-permute-start.7 = (bf16[128,256]{1,0:T(8,128)(2,1)S(1)}, bf16[128,256]{1,0:T(8,128)(2,1)S(1)}, u32[]{:S(2)}, u32[]{:S(2)}) collective-permute-start(bf16[128,256]{1,0:T(8,128)(2,1)S(1)} %get-tuple-element.45), channel_id=1, source_target_pairs={{64,0},{68,4},{72,8},{76,12},{80,16},{84,20},{88,24},{92,28},{96,3... | collective-permute-start | bytes 196616 | tf_op jit(solution)/shard_map/ppermute | solution.py:214
  69.2 14.9 %collective-permute-start.8 = (bf16[128,256]{1,0:T(8,128)(2,1)S(1)}, bf16[128,256]{1,0:T(8,128)(2,1)S(1)}, u32[]{:S(2)}, u32[]{:S(2)}) collective-permute-start(bf16[128,256]{1,0:T(8,128)(2,1)S(1)} %get-tuple-element.46), channel_id=1, source_target_pairs={{256,0},{260,4},{264,8},{268,12},{272,16},{276,20},{280,24},{284,2... | collective-permute-start | bytes 196616 | tf_op jit(solution)/shard_map/ppermute | solution.py:214
  71.3 19.2 %collective-permute-start.9 = (bf16[128,256]{1,0:T(8,128)(2,1)S(1)}, bf16[128,256]{1,0:T(8,128)(2,1)S(1)}, u32[]{:S(2)}, u32[]{:S(2)}) collective-permute-start(bf16[128,256]{1,0:T(8,128)(2,1)S(1)} %get-tuple-element.47), channel_id=1, source_target_pairs={{32,0},{36,4},{40,8},{44,12},{48,16},{52,20},{56,24},{60,28},{64,3... | collective-permute-start | bytes 196616 | tf_op jit(solution)/shard_map/ppermute | solution.py:214
  76.9 13.5 %collective-permute-start.10 = (bf16[128,256]{1,0:T(8,128)(2,1)S(1)}, bf16[128,256]{1,0:T(8,128)(2,1)S(1)}, u32[]{:S(2)}, u32[]{:S(2)}) collective-permute-start(bf16[128,256]{1,0:T(8,128)(2,1)S(1)} %get-tuple-element.48), channel_id=1, source_target_pairs={{128,0},{132,4},{136,8},{140,12},{144,16},{148,20},{152,24},{156,2... | collective-permute-start | bytes 196616 | tf_op jit(solution)/shard_map/ppermute | solution.py:214
  79.1 11.3 %collective-permute-start.11 = (bf16[128,256]{1,0:T(8,128)(2,1)S(1)}, bf16[128,256]{1,0:T(8,128)(2,1)S(1)}, u32[]{:S(2)}, u32[]{:S(2)}) collective-permute-start(bf16[128,256]{1,0:T(8,128)(2,1)S(1)} %get-tuple-element.49), channel_id=1, source_target_pairs={{16,0},{20,4},{24,8},{28,12},{32,16},{36,20},{40,24},{44,28},{48,3... | collective-permute-start | bytes 196616 | tf_op jit(solution)/shard_map/ppermute | solution.py:214
  81.5 8.9 %collective-permute-start.12 = (bf16[128,256]{1,0:T(8,128)(2,1)S(1)}, bf16[128,256]{1,0:T(8,128)(2,1)S(1)}, u32[]{:S(2)}, u32[]{:S(2)}) collective-permute-start(bf16[128,256]{1,0:T(8,128)(2,1)S(1)} %get-tuple-element.50), channel_id=1, source_target_pairs={{8,0},{12,4},{16,8},{20,12},{24,16},{28,20},{32,24},{36,28},{40,32... | collective-permute-start | bytes 196616 | tf_op jit(solution)/shard_map/ppermute | solution.py:214
  84.2 7.7 %collective-permute-start.13 = (bf16[128,256]{1,0:T(8,128)(2,1)S(1)}, bf16[128,256]{1,0:T(8,128)(2,1)S(1)}, u32[]{:S(2)}, u32[]{:S(2)}) collective-permute-start(bf16[128,256]{1,0:T(8,128)(2,1)S(1)} %get-tuple-element.51), channel_id=1, source_target_pairs={{4,0},{8,4},{12,8},{16,12},{20,16},{24,20},{28,24},{32,28},{36,32}... | collective-permute-start | bytes 196616 | tf_op jit(solution)/shard_map/ppermute | solution.py:214

commit v6 on v5

--- a/solution.py
+++ b/solution.py
@@ -75,14 +75,16 @@
 
 
 def prepare_kernel(query_ref, gate_ref, cot_ref, gain_ref, table_ref, lists_ref, *outs):
-    heads_ref, scaled_ref, table_out_ref, lists_out_ref = outs
+    heads_ref, scaled_ref, table_out_ref, lists_out_ref, row_ref = outs
     heads_ref[...] = by_head((query_ref[...].astype(f32) * 0.125).astype(bf16))
-    scaled_ref[...] = cot_ref[...].astype(f32) * gate_ref[...].astype(f32) * gain_ref[...]
+    scaled = cot_ref[...].astype(f32) * gate_ref[...].astype(f32) * gain_ref[...]
+    scaled_ref[...] = scaled
+    row_ref[...] = dot(jnp.ones((8, F), f32), scaled, NT, lax.Precision.HIGHEST)
     table_out_ref[...] = jnp.pad(table_ref[...], ((0, 0), (0, C - 16)))
     lists_out_ref[...] = lists_ref[...]
 
 
-def forward_kernel(group_ref, heads_ref, scaled_ref, lists_ref, table_ref, totals_ref, *refs):
+def forward_kernel(group_ref, heads_ref, scaled_ref, lists_ref, table_ref, row_ref, totals_ref, *refs):
     packets, (att_ref, sums_ref, weights_ref, slopes_ref) = refs[:8], refs[8:]
     group = group_ref[0]
     place = lax.rem(group, ROW)
@@ -132,11 +134,13 @@
     att = from_heads(acc)
     att_ref[...] = att
     scaled = scaled_ref[...]
-    terms = jnp.concatenate([att, att * att, scaled, scaled * att], axis=0)
+    terms = jnp.concatenate([att, att * att, scaled * att], axis=0)
     rows = dot(jnp.ones((8, F), f32), terms, NT, lax.Precision.HIGHEST)
+    parts = [rows[0:1, r * C : (r + 1) * C] for r in range(3)]
+    parts.insert(2, row_ref[0:1, :])
     for r in range(4):
         for x in range(4):
-            sums_ref[x, r : r + 1, :] = rows[0:1, r * C : (r + 1) * C]
+            sums_ref[x, r : r + 1, :] = parts[r]
 
 
 def norm_terms(sums_ref, att_ref):
@@ -244,16 +248,16 @@
     fetched = {d: shifted(packet, d) for d in (16, 8, 4, 2, 1)}
     (row_packet,) = call(row_kernel, [((C + PAD, 2 * F), bf16)])(packet, totals)
     fetched |= {d: shifted(row_packet, d) for d in (64, 32)}
-    heads, scaled, table, lists = call(
+    heads, scaled, table, lists, scaled_row = call(
         prepare_kernel,
-        [((2 * C, F), bf16), ((C, F), f32), ((2, C), f32), ((8, C), i32)],
+        [((2 * C, F), bf16), ((C, F), f32), ((2, C), f32), ((8, C), i32), ((8, C), f32)],
     )(query_rows, gate_rows, cotangent, gain, bias_table, block_lists.T)
     packets = [packet] + [fetched[d] for d in DISTANCES]
     att, sums, weights, slopes = call(
         forward_kernel,
         [((C, F), f32), ((4, 4, C), f32), ((2 * C, 8 * C), bf16), ((2 * C, 8 * C), f32)],
         1,
-    )(group, heads, scaled, lists, table, totals, *packets)
+    )(group, heads, scaled, lists, table, scaled_row, totals, *packets)
     sums = lax.all_to_all(sums, "head", 0, 0)
     kept = (heads, weights, slopes)
     narrow = ((C, 2 * F), bf16)

time: 93.2 us -> 93.2 us (level)
  no operation moved by 1% of the time
where the time goes in v6:
time: 93.2 us; the launch traced here: 92.5 us
  starting transfers between devices  69.1 us (74%)
  blocking collectives  7.99 us (9%)
  waiting for transfers between devices  6.89 us (7%)
  Pallas kernels  6.67 us (7%)
    ppermute x14, starting transfers between devices, shifted(): lax.ppermute(x, 'seq', [(i, i + by) for i in range(count) if 0 <= i + by...  64.4 us
    all_to_all x1, blocking collectives, per_device(): sums = lax.all_to_all(sums, 'head', 0, 0)  7.99 us
    ppermute x14, waiting for transfers between devices, shifted(): lax.ppermute(x, 'seq', [(i, i + by) for i in range(count) if 0 <= i + by...  6.89 us
    pallas_call x6, Pallas kernels, run(): pl.pallas_call(kernel, out_shape=[jax.ShapeDtypeStruct(s, t) for s, t in...  5.23 us
    all_to_all x1, starting transfers between devices, per_device(): totals = lax.all_to_all(totals, 'seq', 0, 0, axis_index_groups=rows)  4.73 us
  transfers between devices with their start and end apart: 15, of which 3 were waited for; matrix products, arithmetic and copies ran while one was open for 0% of the time, Pallas kernels for 1%

profile of v6, /device:TPU:25, one launch (start us, length us, event | category | flops | bytes accessed | tf_op | source)
XLA Modules:
  0.0 92.5 jit_solution(5670042062595261207)
XLA Ops:
  0.6 1.4 %shard_map.129 = (bf16[144,256]{1,0:T(8,128)(2,1)}, f32[32,1,128]{2,1,0:T(1,128)}) custom-call(bf16[128,128]{1,0:T(8,128)(2,1)} %key_ref.1, bf16[128,128]{1,0:T(8,128)(2,1)} %value_ref.1, s32[1,128]{1,0:T(1,128)} %bitcast.7), custom_call_target="tpu_custom_call" | custom-call | tf_op jit(solution)/shard_map/pallas_call | solution.py:235
  2.1 15.4 %collective-permute-start.4 = (bf16[144,256]{1,0:T(8,128)(2,1)}, bf16[144,256]{1,0:T(8,128)(2,1)S(1)}, u32[]{:S(2)}, u32[]{:S(2)}) collective-permute-start(bf16[144,256]{1,0:T(8,128)(2,1)} %get-tuple-element.37.packet_ref.refs_0_.packet), channel_id=1, source_target_pairs={{0,64},{4,68},{8,72},{12,76},{16,80},{20,84},{24,88},{28,92},{32,9... | collective-permute-start | bytes 221192 | tf_op jit(solution)/shard_map/ppermute | solution.py:218
  17.5 4.0 %collective-permute-start.3 = (bf16[144,256]{1,0:T(8,128)(2,1)}, bf16[144,256]{1,0:T(8,128)(2,1)S(1)}, u32[]{:S(2)}, u32[]{:S(2)}) collective-permute-start(bf16[144,256]{1,0:T(8,128)(2,1)} %get-tuple-element.37.packet_ref.refs_0_.packet), channel_id=1, source_target_pairs={{0,32},{4,36},{8,40},{12,44},{16,48},{20,52},{24,56},{28,60},{32,6... | collective-permute-start | bytes 221192 | tf_op jit(solution)/shard_map/ppermute | solution.py:218
  21.6 4.7 %all-to-all-start = ((f32[32,1,128]{2,1,0:T(1,128)}), f32[32,1,128]{2,1,0:T(1,128)S(1)}, u32[]{:S(2)}, u32[]{:S(2)}) async-start(f32[32,1,128]{2,1,0:T(1,128)} %get-tuple-element.36), calls=%async_computation | async-start | bytes 32768 | tf_op jit(solution)/shard_map/all_to_all | solution.py:247
  26.3 4.2 %collective-permute-start.2 = (bf16[144,256]{1,0:T(8,128)(2,1)}, bf16[144,256]{1,0:T(8,128)(2,1)S(1)}, u32[]{:S(2)}, u32[]{:S(2)}) collective-permute-start(bf16[144,256]{1,0:T(8,128)(2,1)} %get-tuple-element.37.packet_ref.refs_0_.packet), channel_id=1, source_target_pairs={{0,16},{4,20},{8,24},{12,28},{16,32},{20,36},{24,40},{28,44},{32,4... | collective-permute-start | bytes 221192 | tf_op jit(solution)/shard_map/ppermute | solution.py:218
  30.5 3.1 %collective-permute-start.1 = (bf16[144,256]{1,0:T(8,128)(2,1)}, bf16[144,256]{1,0:T(8,128)(2,1)S(1)}, u32[]{:S(2)}, u32[]{:S(2)}) collective-permute-start(bf16[144,256]{1,0:T(8,128)(2,1)} %get-tuple-element.37.packet_ref.refs_0_.packet), channel_id=1, source_target_pairs={{0,8},{4,12},{8,16},{12,20},{16,24},{20,28},{24,32},{28,36},{32,40... | collective-permute-start | bytes 221192 | tf_op jit(solution)/shard_map/ppermute | solution.py:218
  33.6 5.1 %collective-permute-start = (bf16[144,256]{1,0:T(8,128)(2,1)}, bf16[144,256]{1,0:T(8,128)(2,1)S(1)}, u32[]{:S(2)}, u32[]{:S(2)}) collective-permute-start(bf16[144,256]{1,0:T(8,128)(2,1)} %get-tuple-element.37.packet_ref.refs_0_.packet), channel_id=1, source_target_pairs={{0,4},{4,8},{8,12},{12,16},{16,20},{20,24},{24,28},{28,32},{32,36}... | collective-permute-start | bytes 221192 | tf_op jit(solution)/shard_map/ppermute | solution.py:218
  38.7 0.0 all-to-all-done.totals_ref
  38.8 0.0 copy-start
  38.8 0.9 copy-done
  39.7 0.0 copy-start.6
  39.7 0.0 copy-start.7
  39.7 0.0 copy-start.1
  39.7 0.0 collective-permute-done.4.refs_5_.refs_0_
  39.7 1.4 %collective-permute-start.6 = (bf16[144,256]{1,0:T(8,128)(2,1)S(1)}, bf16[144,256]{1,0:T(8,128)(2,1)S(1)}, u32[]{:S(2)}, u32[]{:S(2)}) collective-permute-start(bf16[144,256]{1,0:T(8,128)(2,1)S(1)} %shard_map.130), channel_id=1, source_target_pairs={{0,256},{4,260},{8,264},{12,268},{16,272},{20,276},{24,280},{28,28... | collective-permute-start | bytes 221192 | tf_op jit(solution)/shard_map/ppermute | solution.py:218
  41.2 0.0 collective-permute-done.3.refs_4_.refs_2_
  41.2 1.3 %collective-permute-start.5 = (bf16[144,256]{1,0:T(8,128)(2,1)S(1)}, bf16[144,256]{1,0:T(8,128)(2,1)S(1)}, u32[]{:S(2)}, u32[]{:S(2)}) collective-permute-start(bf16[144,256]{1,0:T(8,128)(2,1)S(1)} %shard_map.130), channel_id=1, source_target_pairs={{0,128},{4,132},{8,136},{12,140},{16,144},{20,148},{24,152},{28,15... | collective-permute-start | bytes 221192 | tf_op jit(solution)/shard_map/ppermute | solution.py:218
  42.5 0.0 copy-done.2
  42.5 0.0 copy-done.3
  42.5 0.0 copy-done.4
  42.5 0.0 copy-done.5
  42.5 0.0 copy-done.6
  42.5 0.0 copy-done.7
  42.5 0.2 shard_map.128
  42.7 0.0 collective-permute-done.2.refs_3_.refs_4_
  42.8 0.0 collective-permute-done.1.refs_2_.refs_5_
  42.8 0.0 collective-permute-done.refs_1_.refs_6_
  42.8 4.1 %collective-permute-done.6.refs_7_.refs_1_ = bf16[144,256]{1,0:T(8,128)(2,1)S(1)} collective-permute-done((bf16[144,256]{1,0:T(8,128)(2,1)S(1)}, bf16[144,256]{1,0:T(8,128)(2,1)S(1)}, u32[]{:S(2)}, u32[]{:S(2)}) %collective-permute-start.6) | collective-permute-done | bytes 73760 | tf_op jit(solution)/shard_map/ppermute | solution.py:218
  46.8 1.4 %collective-permute-done.5.refs_6_.refs_3_ = bf16[144,256]{1,0:T(8,128)(2,1)S(1)} collective-permute-done((bf16[144,256]{1,0:T(8,128)(2,1)S(1)}, bf16[144,256]{1,0:T(8,128)(2,1)S(1)}, u32[]{:S(2)}, u32[]{:S(2)}) %collective-permute-start.5) | collective-permute-done | bytes 73760 | tf_op jit(solution)/shard_map/ppermute | solution.py:218
  48.2 1.4 %shard_map.131 = (f32[128,128]{1,0:T(8,128)S(1)}, f32[4,4,128]{2,1,0:T(4,128)S(1)}, bf16[256,1024]{1,0:T(8,128)(2,1)S(1)}, f32[256,1024]{1,0:T(8,128)S(1)}) custom-call(s32[1]{0:T(128)} %bitcast.group_ref, bf16[256,128]{1,0:T(8,128)(2,1)S(1)} %get-tuple-element.31.heads_ref, f32[128,128]{1,0:T(8,128)S(1)} %get-tuple-element.32.scaled_ref, ...), custom_call_target="tpu_custom_call" | custom-call | tf_op jit(solution)/shard_map/pallas_call | solution.py:205
  49.7 8.0 %all_to_all.10.sums_ref = f32[4,4,128]{2,1,0:T(4,128)S(1)} all-to-all(f32[4,4,128]{2,1,0:T(4,128)S(1)} %get-tuple-element.39), channel_id=1, replica_groups=mesh['seq'=128,'head'=4] {'head'}, dimensions={0} | all-to-all | bytes 16384 | tf_op jit(solution)/shard_map/all_to_all | solution.py:261
  57.7 1.7 %shard_map.132 = (bf16[256,128]{1,0:T(8,128)(2,1)S(1)}, f32[256,128]{1,0:T(8,128)S(1)}, bf16[128,256]{1,0:T(8,128)(2,1)S(1)}, bf16[128,256]{1,0:T(8,128)(2,1)S(1...) custom-call(f32[128,128]{1,0:T(8,128)S(1)} %get-tuple-element.38.att, ...), custom_call_target="tpu_custom_call" | custom-call | tf_op jit(solution)/shard_map/pallas_call | solution.py:205
  59.4 9.8 %collective-permute-start.7 = (bf16[128,256]{1,0:T(8,128)(2,1)S(1)}, bf16[128,256]{1,0:T(8,128)(2,1)S(1)}, u32[]{:S(2)}, u32[]{:S(2)}) collective-permute-start(bf16[128,256]{1,0:T(8,128)(2,1)S(1)} %get-tuple-element.47), channel_id=1, source_target_pairs={{64,0},{68,4},{72,8},{76,12},{80,16},{84,20},{88,24},{92,28},{96,3... | collective-permute-start | bytes 196616 | tf_op jit(solution)/shard_map/ppermute | solution.py:218
  69.2 2.0 %collective-permute-start.8 = (bf16[128,256]{1,0:T(8,128)(2,1)S(1)}, bf16[128,256]{1,0:T(8,128)(2,1)S(1)}, u32[]{:S(2)}, u32[]{:S(2)}) collective-permute-start(bf16[128,256]{1,0:T(8,128)(2,1)S(1)} %get-tuple-element.48), channel_id=1, source_target_pairs={{256,0},{260,4},{264,8},{268,12},{272,16},{276,20},{280,24},{284,2... | collective-permute-start | bytes 196616 | tf_op jit(solution)/shard_map/ppermute | solution.py:218
  71.3 5.7 %collective-permute-start.9 = (bf16[128,256]{1,0:T(8,128)(2,1)S(1)}, bf16[128,256]{1,0:T(8,128)(2,1)S(1)}, u32[]{:S(2)}, u32[]{:S(2)}) collective-permute-start(bf16[128,256]{1,0:T(8,128)(2,1)S(1)} %get-tuple-element.49), channel_id=1, source_target_pairs={{32,0},{36,4},{40,8},{44,12},{48,16},{52,20},{56,24},{60,28},{64,3... | collective-permute-start | bytes 196616 | tf_op jit(solution)/shard_map/ppermute | solution.py:218
  76.9 2.2 %collective-permute-start.10 = (bf16[128,256]{1,0:T(8,128)(2,1)S(1)}, bf16[128,256]{1,0:T(8,128)(2,1)S(1)}, u32[]{:S(2)}, u32[]{:S(2)}) collective-permute-start(bf16[128,256]{1,0:T(8,128)(2,1)S(1)} %get-tuple-element.50), channel_id=1, source_target_pairs={{128,0},{132,4},{136,8},{140,12},{144,16},{148,20},{152,24},{156,2... | collective-permute-start | bytes 196616 | tf_op jit(solution)/shard_map/ppermute | solution.py:218
  79.1 2.4 %collective-permute-start.11 = (bf16[128,256]{1,0:T(8,128)(2,1)S(1)}, bf16[128,256]{1,0:T(8,128)(2,1)S(1)}, u32[]{:S(2)}, u32[]{:S(2)}) collective-permute-start(bf16[128,256]{1,0:T(8,128)(2,1)S(1)} %get-tuple-element.51), channel_id=1, source_target_pairs={{16,0},{20,4},{24,8},{28,12},{32,16},{36,20},{40,24},{44,28},{48,3... | collective-permute-start | bytes 196616 | tf_op jit(solution)/shard_map/ppermute | solution.py:218
  81.5 0.0 collective-permute-done.7.refs_0_
  81.5 2.6 %collective-permute-start.12 = (bf16[128,256]{1,0:T(8,128)(2,1)S(1)}, bf16[128,256]{1,0:T(8,128)(2,1)S(1)}, u32[]{:S(2)}, u32[]{:S(2)}) collective-permute-start(bf16[128,256]{1,0:T(8,128)(2,1)S(1)} %get-tuple-element.52), channel_id=1, source_target_pairs={{8,0},{12,4},{16,8},{20,12},{24,16},{28,20},{32,24},{36,28},{40,32... | collective-permute-start | bytes 196616 | tf_op jit(solution)/shard_map/ppermute | solution.py:218
  84.2 0.0 collective-permute-done.8.refs_1_
  84.2 5.1 %collective-permute-start.13 = (bf16[128,256]{1,0:T(8,128)(2,1)S(1)}, bf16[128,256]{1,0:T(8,128)(2,1)S(1)}, u32[]{:S(2)}, u32[]{:S(2)}) collective-permute-start(bf16[128,256]{1,0:T(8,128)(2,1)S(1)} %get-tuple-element.53), channel_id=1, source_target_pairs={{4,0},{8,4},{12,8},{16,12},{20,16},{24,20},{28,24},{32,28},{36,32}... | collective-permute-start | bytes 196616 | tf_op jit(solution)/shard_map/ppermute | solution.py:218
  89.3 1.1 %shard_map.133 = (bf16[128,128]{1,0:T(8,128)(2,1)}, bf16[128,128]{1,0:T(8,128)(2,1)}, bf16[128,128]{1,0:T(8,128)(2,1)}, f32[128,256]{1,0:T(8,128)S(1)}) custom-call(bf16[256,128]{1,0:T(8,128)(2,1)S(1)} %get-tuple-element.42.grads_ref, f32[256,128]{1,0:T(8,128)S(1)} %get-tuple-element.43.before_ref, bf16[256,128]{1,0:T(8,128)(2,1)S(1)} %get-tuple-element.31.heads_ref, ...), custom_call_target="tpu_custom_call" | custom-call | tf_op jit(solution)/shard_map/pallas_call | solution.py:205
  90.4 0.0 collective-permute-done.9.refs_2_
  90.4 0.0 collective-permute-done.10.refs_3_
  90.4 0.0 collective-permute-done.11.refs_4_
  90.4 0.0 collective-permute-done.12.refs_5_
  90.5 1.4 %collective-permute-done.13.refs_6_ = bf16[128,256]{1,0:T(8,128)(2,1)S(1)} collective-permute-done((bf16[128,256]{1,0:T(8,128)(2,1)S(1)}, bf16[128,256]{1,0:T(8,128)(2,1)S(1)}, u32[]{:S(2)}, u32[]{:S(2)}) %collective-permute-start.13) | collective-permute-done | bytes 65568 | tf_op jit(solution)/shard_map/ppermute | solution.py:218
  91.8 0.7 shard_map.134
  (6 shorter events, 0.0 us)
Async XLA Ops:
  2.1 37.6 %collective-permute-start.4 = (bf16[144,256]{1,0:T(8,128)(2,1)}, bf16[144,256]{1,0:T(8,128)(2,1)S(1)}, u32[]{:S(2)}, u32[]{:S(2)}) collective-permute-start(bf16[144,256]{1,0:T(8,128)(2,1)} %get-tuple-element.37.packet_ref.refs_0_.packet), channel_id=1, source_target_pairs={{0,64},{4,68},{8,72},{12,76},{16,80},{20,84},{24,88},{28,92},{32,9... | collective-permute-start | bytes 221192 | tf_op jit(solution)/shard_map/ppermute | solution.py:218
  17.5 23.6 %collective-permute-start.3 = (bf16[144,256]{1,0:T(8,128)(2,1)}, bf16[144,256]{1,0:T(8,128)(2,1)S(1)}, u32[]{:S(2)}, u32[]{:S(2)}) collective-permute-start(bf16[144,256]{1,0:T(8,128)(2,1)} %get-tuple-element.37.packet_ref.refs_0_.packet), channel_id=1, source_target_pairs={{0,32},{4,36},{8,40},{12,44},{16,48},{20,52},{24,56},{28,60},{32,6... | collective-permute-start | bytes 221192 | tf_op jit(solution)/shard_map/ppermute | solution.py:218
  21.6 17.2 %all-to-all-start = ((f32[32,1,128]{2,1,0:T(1,128)}), f32[32,1,128]{2,1,0:T(1,128)S(1)}, u32[]{:S(2)}, u32[]{:S(2)}) async-start(f32[32,1,128]{2,1,0:T(1,128)} %get-tuple-element.36), calls=%async_computation | async-start | bytes 32768 | tf_op jit(solution)/shard_map/all_to_all | solution.py:247
  26.3 16.5 %collective-permute-start.2 = (bf16[144,256]{1,0:T(8,128)(2,1)}, bf16[144,256]{1,0:T(8,128)(2,1)S(1)}, u32[]{:S(2)}, u32[]{:S(2)}) collective-permute-start(bf16[144,256]{1,0:T(8,128)(2,1)} %get-tuple-element.37.packet_ref.refs_0_.packet), channel_id=1, source_target_pairs={{0,16},{4,20},{8,24},{12,28},{16,32},{20,36},{24,40},{28,44},{32,4... | collective-permute-start | bytes 221192 | tf_op jit(solution)/shard_map/ppermute | solution.py:218
  30.5 12.2 %collective-permute-start.1 = (bf16[144,256]{1,0:T(8,128)(2,1)}, bf16[144,256]{1,0:T(8,128)(2,1)S(1)}, u32[]{:S(2)}, u32[]{:S(2)}) collective-permute-start(bf16[144,256]{1,0:T(8,128)(2,1)} %get-tuple-element.37.packet_ref.refs_0_.packet), channel_id=1, source_target_pairs={{0,8},{4,12},{8,16},{12,20},{16,24},{20,28},{24,32},{28,36},{32,40... | collective-permute-start | bytes 221192 | tf_op jit(solution)/shard_map/ppermute | solution.py:218
  33.6 9.2 %collective-permute-start = (bf16[144,256]{1,0:T(8,128)(2,1)}, bf16[144,256]{1,0:T(8,128)(2,1)S(1)}, u32[]{:S(2)}, u32[]{:S(2)}) collective-permute-start(bf16[144,256]{1,0:T(8,128)(2,1)} %get-tuple-element.37.packet_ref.refs_0_.packet), channel_id=1, source_target_pairs={{0,4},{4,8},{8,12},{12,16},{16,20},{20,24},{24,28},{28,32},{32,36}... | collective-permute-start | bytes 221192 | tf_op jit(solution)/shard_map/ppermute | solution.py:218
  38.8 0.9 copy-start
  39.6 2.8 %copy-start.2 = (bf16[128,128]{1,0:T(8,128)(2,1)S(1)}, bf16[128,128]{1,0:T(8,128)(2,1)}, u32[]{:S(2)}) copy-start(bf16[128,128]{1,0:T(8,128)(2,1)} %gate_ref.3) | copy-start | bytes 98308
  39.6 2.8 %copy-start.3 = (bf16[128,128]{1,0:T(8,128)(2,1)S(1)}, bf16[128,128]{1,0:T(8,128)(2,1)}, u32[]{:S(2)}) copy-start(bf16[128,128]{1,0:T(8,128)(2,1)} %cot_ref.3) | copy-start | bytes 98308
  39.6 2.9 %copy-start.4 = (bf16[128,128]{1,0:T(8,128)(2,1)S(1)}, bf16[128,128]{1,0:T(8,128)(2,1)}, u32[]{:S(2)}) copy-start(bf16[128,128]{1,0:T(8,128)(2,1)} %query_ref.1) | copy-start | bytes 98308
  39.7 2.9 %copy-start.5 = (s32[128,8]{0,1:T(8,128)S(1)}, s32[128,8]{0,1:T(8,128)}, u32[]{:S(2)}) copy-start(s32[128,8]{0,1:T(8,128)} %param.15) | copy-start | bytes 12292
  39.7 2.9 %copy-start.6 = (f32[128]{0:T(128)S(1)}, f32[128]{0:T(128)}, u32[]{:S(2)}) copy-start(f32[128]{0:T(128)} %param.17) | copy-start | bytes 1540
  39.7 2.9 %copy-start.7 = (f32[2,16]{1,0:T(2,128)S(1)}, f32[2,16]{1,0:T(2,128)}, u32[]{:S(2)}) copy-start(f32[2,16]{1,0:T(2,128)} %table_ref.1) | copy-start | bytes 388
  39.7 8.5 %copy-start.1 = (bf16[144,256]{1,0:T(8,128)(2,1)S(1)}, bf16[144,256]{1,0:T(8,128)(2,1)}, u32[]{:S(2)}) copy-start(bf16[144,256]{1,0:T(8,128)(2,1)} %get-tuple-element.37.packet_ref.refs_0_.packet) | copy-start | bytes 221188
  39.7 7.1 %collective-permute-start.6 = (bf16[144,256]{1,0:T(8,128)(2,1)S(1)}, bf16[144,256]{1,0:T(8,128)(2,1)S(1)}, u32[]{:S(2)}, u32[]{:S(2)}) collective-permute-start(bf16[144,256]{1,0:T(8,128)(2,1)S(1)} %shard_map.130), channel_id=1, source_target_pairs={{0,256},{4,260},{8,264},{12,268},{16,272},{20,276},{24,280},{28,28... | collective-permute-start | bytes 221192 | tf_op jit(solution)/shard_map/ppermute | solution.py:218
  41.2 7.1 %collective-permute-start.5 = (bf16[144,256]{1,0:T(8,128)(2,1)S(1)}, bf16[144,256]{1,0:T(8,128)(2,1)S(1)}, u32[]{:S(2)}, u32[]{:S(2)}) collective-permute-start(bf16[144,256]{1,0:T(8,128)(2,1)S(1)} %shard_map.130), channel_id=1, source_target_pairs={{0,128},{4,132},{8,136},{12,140},{16,144},{20,148},{24,152},{28,15... | collective-permute-start | bytes 221192 | tf_op jit(solution)/shard_map/ppermute | solution.py:218
  59.4 22.1 %collective-permute-start.7 = (bf16[128,256]{1,0:T(8,128)(2,1)S(1)}, bf16[128,256]{1,0:T(8,128)(2,1)S(1)}, u32[]{:S(2)}, u32[]{:S(2)}) collective-permute-start(bf16[128,256]{1,0:T(8,128)(2,1)S(1)} %get-tuple-element.47), channel_id=1, source_target_pairs={{64,0},{68,4},{72,8},{76,12},{80,16},{84,20},{88,24},{92,28},{96,3... | collective-permute-start | bytes 196616 | tf_op jit(solution)/shard_map/ppermute | solution.py:218
  69.2 14.9 %collective-permute-start.8 = (bf16[128,256]{1,0:T(8,128)(2,1)S(1)}, bf16[128,256]{1,0:T(8,128)(2,1)S(1)}, u32[]{:S(2)}, u32[]{:S(2)}) collective-permute-start(bf16[128,256]{1,0:T(8,128)(2,1)S(1)} %get-tuple-element.48), channel_id=1, source_target_pairs={{256,0},{260,4},{264,8},{268,12},{272,16},{276,20},{280,24},{284,2... | collective-permute-start | bytes 196616 | tf_op jit(solution)/shard_map/ppermute | solution.py:218
  71.3 19.2 %collective-permute-start.9 = (bf16[128,256]{1,0:T(8,128)(2,1)S(1)}, bf16[128,256]{1,0:T(8,128)(2,1)S(1)}, u32[]{:S(2)}, u32[]{:S(2)}) collective-permute-start(bf16[128,256]{1,0:T(8,128)(2,1)S(1)} %get-tuple-element.49), channel_id=1, source_target_pairs={{32,0},{36,4},{40,8},{44,12},{48,16},{52,20},{56,24},{60,28},{64,3... | collective-permute-start | bytes 196616 | tf_op jit(solution)/shard_map/ppermute | solution.py:218
  76.9 13.5 %collective-permute-start.10 = (bf16[128,256]{1,0:T(8,128)(2,1)S(1)}, bf16[128,256]{1,0:T(8,128)(2,1)S(1)}, u32[]{:S(2)}, u32[]{:S(2)}) collective-permute-start(bf16[128,256]{1,0:T(8,128)(2,1)S(1)} %get-tuple-element.50), channel_id=1, source_target_pairs={{128,0},{132,4},{136,8},{140,12},{144,16},{148,20},{152,24},{156,2... | collective-permute-start | bytes 196616 | tf_op jit(solution)/shard_map/ppermute | solution.py:218
  79.1 11.3 %collective-permute-start.11 = (bf16[128,256]{1,0:T(8,128)(2,1)S(1)}, bf16[128,256]{1,0:T(8,128)(2,1)S(1)}, u32[]{:S(2)}, u32[]{:S(2)}) collective-permute-start(bf16[128,256]{1,0:T(8,128)(2,1)S(1)} %get-tuple-element.51), channel_id=1, source_target_pairs={{16,0},{20,4},{24,8},{28,12},{32,16},{36,20},{40,24},{44,28},{48,3... | collective-permute-start | bytes 196616 | tf_op jit(solution)/shard_map/ppermute | solution.py:218
  81.5 8.9 %collective-permute-start.12 = (bf16[128,256]{1,0:T(8,128)(2,1)S(1)}, bf16[128,256]{1,0:T(8,128)(2,1)S(1)}, u32[]{:S(2)}, u32[]{:S(2)}) collective-permute-start(bf16[128,256]{1,0:T(8,128)(2,1)S(1)} %get-tuple-element.52), channel_id=1, source_target_pairs={{8,0},{12,4},{16,8},{20,12},{24,16},{28,20},{32,24},{36,28},{40,32... | collective-permute-start | bytes 196616 | tf_op jit(solution)/shard_map/ppermute | solution.py:218
  84.2 7.7 %collective-permute-start.13 = (bf16[128,256]{1,0:T(8,128)(2,1)S(1)}, bf16[128,256]{1,0:T(8,128)(2,1)S(1)}, u32[]{:S(2)}, u32[]{:S(2)}) collective-permute-start(bf16[128,256]{1,0:T(8,128)(2,1)S(1)} %get-tuple-element.53), channel_id=1, source_target_pairs={{4,0},{8,4},{12,8},{16,12},{20,16},{24,20},{28,24},{32,28},{36,32}... | collective-permute-start | bytes 196616 | tf_op jit(solution)/shard_map/ppermute | solution.py:218

commit v7 on v6

--- a/solution.py
+++ b/solution.py
@@ -85,7 +85,8 @@
 
 
 def forward_kernel(group_ref, heads_ref, scaled_ref, lists_ref, table_ref, row_ref, totals_ref, *refs):
-    packets, (att_ref, sums_ref, weights_ref, slopes_ref) = refs[:8], refs[8:]
+    packets = refs[:6] + (refs[7], refs[6])
+    att_ref, sums_ref, weights_ref, slopes_ref = refs[8:]
     group = group_ref[0]
     place = lax.rem(group, ROW)
     queries = heads_ref[...]
@@ -257,7 +258,7 @@
         forward_kernel,
         [((C, F), f32), ((4, 4, C), f32), ((2 * C, 8 * C), bf16), ((2 * C, 8 * C), f32)],
         1,
-    )(group, heads, scaled, lists, table, scaled_row, totals, *packets)
+    )(group, heads, scaled, lists, table, scaled_row, totals, *packets[:6], packets[7], packets[6])
     sums = lax.all_to_all(sums, "head", 0, 0)
     kept = (heads, weights, slopes)
     narrow = ((C, 2 * F), bf16)

time: 93.2 us -> 92.9 us (level)
  starting transfers between devices: 69.1 us -> 67.5 us
  waiting for transfers between devices: 6.89 us -> 8.24 us
    ppermute x14, starting transfers between devices: 64.4 us -> 62.8 us  [shifted(): lax.ppermute(x, 'seq', [(i, i + by) for i in range(count) if 0 <= i + by...]
    ppermute x14, waiting for transfers between devices: 6.89 us -> 8.24 us  [shifted(): lax.ppermute(x, 'seq', [(i, i + by) for i in range(count) if 0 <= i + by...]
where the time goes in v7:
time: 92.9 us; the launch traced here: 92.3 us
  starting transfers between devices  67.5 us (73%)
  waiting for transfers between devices  8.24 us (9%)
  blocking collectives  7.99 us (9%)
  Pallas kernels  6.67 us (7%)
    ppermute x14, starting transfers between devices, shifted(): lax.ppermute(x, 'seq', [(i, i + by) for i in range(count) if 0 <= i + by...  62.8 us
    ppermute x14, waiting for transfers between devices, shifted(): lax.ppermute(x, 'seq', [(i, i + by) for i in range(count) if 0 <= i + by...  8.24 us
    all_to_all x1, blocking collectives, per_device(): sums = lax.all_to_all(sums, 'head', 0, 0)  7.99 us
    pallas_call x6, Pallas kernels, run(): pl.pallas_call(kernel, out_shape=[jax.ShapeDtypeStruct(s, t) for s, t in...  5.23 us
    all_to_all x1, starting transfers between devices, per_device(): totals = lax.all_to_all(totals, 'seq', 0, 0, axis_index_groups=rows)  4.73 us
  transfers between devices with their start and end apart: 15, of which 3 were waited for; matrix products, arithmetic and copies ran while one was open for 0% of the time, Pallas kernels for 1%

profile of v7, /device:TPU:25, one launch (start us, length us, event | category | flops | bytes accessed | tf_op | source)
XLA Modules:
  0.0 92.3 jit_solution(1532107237938632440)
XLA Ops:
  0.6 1.4 %shard_map.129 = (bf16[144,256]{1,0:T(8,128)(2,1)}, f32[32,1,128]{2,1,0:T(1,128)}) custom-call(bf16[128,128]{1,0:T(8,128)(2,1)} %key_ref.1, bf16[128,128]{1,0:T(8,128)(2,1)} %value_ref.1, s32[1,128]{1,0:T(1,128)} %bitcast.7), custom_call_target="tpu_custom_call" | custom-call | tf_op jit(solution)/shard_map/pallas_call | solution.py:236
  2.1 15.4 %collective-permute-start.4 = (bf16[144,256]{1,0:T(8,128)(2,1)}, bf16[144,256]{1,0:T(8,128)(2,1)S(1)}, u32[]{:S(2)}, u32[]{:S(2)}) collective-permute-start(bf16[144,256]{1,0:T(8,128)(2,1)} %get-tuple-element.37.packet_ref.refs_0_.packet), channel_id=1, source_target_pairs={{0,64},{4,68},{8,72},{12,76},{16,80},{20,84},{24,88},{28,92},{32,9... | collective-permute-start | bytes 221192 | tf_op jit(solution)/shard_map/ppermute | solution.py:219
  17.5 4.0 %collective-permute-start.3 = (bf16[144,256]{1,0:T(8,128)(2,1)}, bf16[144,256]{1,0:T(8,128)(2,1)S(1)}, u32[]{:S(2)}, u32[]{:S(2)}) collective-permute-start(bf16[144,256]{1,0:T(8,128)(2,1)} %get-tuple-element.37.packet_ref.refs_0_.packet), channel_id=1, source_target_pairs={{0,32},{4,36},{8,40},{12,44},{16,48},{20,52},{24,56},{28,60},{32,6... | collective-permute-start | bytes 221192 | tf_op jit(solution)/shard_map/ppermute | solution.py:219
  21.6 4.7 %all-to-all-start = ((f32[32,1,128]{2,1,0:T(1,128)}), f32[32,1,128]{2,1,0:T(1,128)S(1)}, u32[]{:S(2)}, u32[]{:S(2)}) async-start(f32[32,1,128]{2,1,0:T(1,128)} %get-tuple-element.36), calls=%async_computation | async-start | bytes 32768 | tf_op jit(solution)/shard_map/all_to_all | solution.py:248
  26.3 4.2 %collective-permute-start.2 = (bf16[144,256]{1,0:T(8,128)(2,1)}, bf16[144,256]{1,0:T(8,128)(2,1)S(1)}, u32[]{:S(2)}, u32[]{:S(2)}) collective-permute-start(bf16[144,256]{1,0:T(8,128)(2,1)} %get-tuple-element.37.packet_ref.refs_0_.packet), channel_id=1, source_target_pairs={{0,16},{4,20},{8,24},{12,28},{16,32},{20,36},{24,40},{28,44},{32,4... | collective-permute-start | bytes 221192 | tf_op jit(solution)/shard_map/ppermute | solution.py:219
  30.5 3.1 %collective-permute-start.1 = (bf16[144,256]{1,0:T(8,128)(2,1)}, bf16[144,256]{1,0:T(8,128)(2,1)S(1)}, u32[]{:S(2)}, u32[]{:S(2)}) collective-permute-start(bf16[144,256]{1,0:T(8,128)(2,1)} %get-tuple-element.37.packet_ref.refs_0_.packet), channel_id=1, source_target_pairs={{0,8},{4,12},{8,16},{12,20},{16,24},{20,28},{24,32},{28,36},{32,40... | collective-permute-start | bytes 221192 | tf_op jit(solution)/shard_map/ppermute | solution.py:219
  33.6 5.1 %collective-permute-start = (bf16[144,256]{1,0:T(8,128)(2,1)}, bf16[144,256]{1,0:T(8,128)(2,1)S(1)}, u32[]{:S(2)}, u32[]{:S(2)}) collective-permute-start(bf16[144,256]{1,0:T(8,128)(2,1)} %get-tuple-element.37.packet_ref.refs_0_.packet), channel_id=1, source_target_pairs={{0,4},{4,8},{8,12},{12,16},{16,20},{20,24},{24,28},{28,32},{32,36}... | collective-permute-start | bytes 221192 | tf_op jit(solution)/shard_map/ppermute | solution.py:219
  38.7 0.0 all-to-all-done.totals_ref
  38.8 0.0 copy-start
  38.8 0.9 copy-done
  39.7 0.0 copy-start.6
  39.7 0.0 copy-start.7
  39.7 0.0 copy-start.1
  39.7 0.0 collective-permute-done.4.refs_5_.refs_0_
  39.7 1.4 %collective-permute-start.6 = (bf16[144,256]{1,0:T(8,128)(2,1)S(1)}, bf16[144,256]{1,0:T(8,128)(2,1)S(1)}, u32[]{:S(2)}, u32[]{:S(2)}) collective-permute-start(bf16[144,256]{1,0:T(8,128)(2,1)S(1)} %shard_map.130), channel_id=1, source_target_pairs={{0,128},{4,132},{8,136},{12,140},{16,144},{20,148},{24,152},{28,15... | collective-permute-start | bytes 221192 | tf_op jit(solution)/shard_map/ppermute | solution.py:219
  41.2 0.0 collective-permute-done.3.refs_4_.refs_2_
  41.2 1.3 %collective-permute-start.5 = (bf16[144,256]{1,0:T(8,128)(2,1)S(1)}, bf16[144,256]{1,0:T(8,128)(2,1)S(1)}, u32[]{:S(2)}, u32[]{:S(2)}) collective-permute-start(bf16[144,256]{1,0:T(8,128)(2,1)S(1)} %shard_map.130), channel_id=1, source_target_pairs={{0,256},{4,260},{8,264},{12,268},{16,272},{20,276},{24,280},{28,28... | collective-permute-start | bytes 221192 | tf_op jit(solution)/shard_map/ppermute | solution.py:219
  42.5 0.0 copy-done.2
  42.5 0.0 copy-done.3
  42.5 0.0 copy-done.4
  42.5 0.0 copy-done.5
  42.5 0.0 copy-done.6
  42.5 0.2 shard_map.128
  42.7 0.0 collective-permute-done.2.refs_3_.refs_4_
  42.8 0.0 collective-permute-done.1.refs_2_.refs_5_
  42.8 0.0 collective-permute-done.refs_1_.refs_6_
  42.8 4.1 %collective-permute-done.6.refs_7_.refs_3_ = bf16[144,256]{1,0:T(8,128)(2,1)S(1)} collective-permute-done((bf16[144,256]{1,0:T(8,128)(2,1)S(1)}, bf16[144,256]{1,0:T(8,128)(2,1)S(1)}, u32[]{:S(2)}, u32[]{:S(2)}) %collective-permute-start.6) | collective-permute-done | bytes 73760 | tf_op jit(solution)/shard_map/ppermute | solution.py:219
  46.9 2.8 %collective-permute-done.5.refs_6_.refs_1_ = bf16[144,256]{1,0:T(8,128)(2,1)S(1)} collective-permute-done((bf16[144,256]{1,0:T(8,128)(2,1)S(1)}, bf16[144,256]{1,0:T(8,128)(2,1)S(1)}, u32[]{:S(2)}, u32[]{:S(2)}) %collective-permute-start.5) | collective-permute-done | bytes 73760 | tf_op jit(solution)/shard_map/ppermute | solution.py:219
  49.8 0.0 copy-done.1
  49.8 1.4 %shard_map.131 = (f32[128,128]{1,0:T(8,128)S(1)}, f32[4,4,128]{2,1,0:T(4,128)S(1)}, bf16[256,1024]{1,0:T(8,128)(2,1)S(1)}, f32[256,1024]{1,0:T(8,128)S(1)}) custom-call(s32[1]{0:T(128)} %bitcast.group_ref, bf16[256,128]{1,0:T(8,128)(2,1)S(1)} %get-tuple-element.31.heads_ref, f32[128,128]{1,0:T(8,128)S(1)} %get-tuple-element.32.scaled_ref, ...), custom_call_target="tpu_custom_call" | custom-call | tf_op jit(solution)/shard_map/pallas_call | solution.py:206
  51.2 8.0 %all_to_all.10.sums_ref = f32[4,4,128]{2,1,0:T(4,128)S(1)} all-to-all(f32[4,4,128]{2,1,0:T(4,128)S(1)} %get-tuple-element.39), channel_id=1, replica_groups=mesh['seq'=128,'head'=4] {'head'}, dimensions={0} | all-to-all | bytes 16384 | tf_op jit(solution)/shard_map/all_to_all | solution.py:262
  59.2 1.7 %shard_map.132 = (bf16[256,128]{1,0:T(8,128)(2,1)S(1)}, f32[256,128]{1,0:T(8,128)S(1)}, bf16[128,256]{1,0:T(8,128)(2,1)S(1)}, bf16[128,256]{1,0:T(8,128)(2,1)S(1...) custom-call(f32[128,128]{1,0:T(8,128)S(1)} %get-tuple-element.38.att, ...), custom_call_target="tpu_custom_call" | custom-call | tf_op jit(solution)/shard_map/pallas_call | solution.py:206
  60.9 8.8 %collective-permute-start.7 = (bf16[128,256]{1,0:T(8,128)(2,1)S(1)}, bf16[128,256]{1,0:T(8,128)(2,1)S(1)}, u32[]{:S(2)}, u32[]{:S(2)}) collective-permute-start(bf16[128,256]{1,0:T(8,128)(2,1)S(1)} %get-tuple-element.47), channel_id=1, source_target_pairs={{64,0},{68,4},{72,8},{76,12},{80,16},{84,20},{88,24},{92,28},{96,3... | collective-permute-start | bytes 196616 | tf_op jit(solution)/shard_map/ppermute | solution.py:219
  69.8 1.8 %collective-permute-start.8 = (bf16[128,256]{1,0:T(8,128)(2,1)S(1)}, bf16[128,256]{1,0:T(8,128)(2,1)S(1)}, u32[]{:S(2)}, u32[]{:S(2)}) collective-permute-start(bf16[128,256]{1,0:T(8,128)(2,1)S(1)} %get-tuple-element.48), channel_id=1, source_target_pairs={{256,0},{260,4},{264,8},{268,12},{272,16},{276,20},{280,24},{284,2... | collective-permute-start | bytes 196616 | tf_op jit(solution)/shard_map/ppermute | solution.py:219
  71.6 6.0 %collective-permute-start.9 = (bf16[128,256]{1,0:T(8,128)(2,1)S(1)}, bf16[128,256]{1,0:T(8,128)(2,1)S(1)}, u32[]{:S(2)}, u32[]{:S(2)}) collective-permute-start(bf16[128,256]{1,0:T(8,128)(2,1)S(1)} %get-tuple-element.49), channel_id=1, source_target_pairs={{32,0},{36,4},{40,8},{44,12},{48,16},{52,20},{56,24},{60,28},{64,3... | collective-permute-start | bytes 196616 | tf_op jit(solution)/shard_map/ppermute | solution.py:219
  77.5 1.3 %collective-permute-start.10 = (bf16[128,256]{1,0:T(8,128)(2,1)S(1)}, bf16[128,256]{1,0:T(8,128)(2,1)S(1)}, u32[]{:S(2)}, u32[]{:S(2)}) collective-permute-start(bf16[128,256]{1,0:T(8,128)(2,1)S(1)} %get-tuple-element.50), channel_id=1, source_target_pairs={{128,0},{132,4},{136,8},{140,12},{144,16},{148,20},{152,24},{156,2... | collective-permute-start | bytes 196616 | tf_op jit(solution)/shard_map/ppermute | solution.py:219
  78.8 2.9 %collective-permute-start.11 = (bf16[128,256]{1,0:T(8,128)(2,1)S(1)}, bf16[128,256]{1,0:T(8,128)(2,1)S(1)}, u32[]{:S(2)}, u32[]{:S(2)}) collective-permute-start(bf16[128,256]{1,0:T(8,128)(2,1)S(1)} %get-tuple-element.51), channel_id=1, source_target_pairs={{16,0},{20,4},{24,8},{28,12},{32,16},{36,20},{40,24},{44,28},{48,3... | collective-permute-start | bytes 196616 | tf_op jit(solution)/shard_map/ppermute | solution.py:219
  81.8 0.0 collective-permute-done.7.refs_0_
  81.8 2.5 %collective-permute-start.12 = (bf16[128,256]{1,0:T(8,128)(2,1)S(1)}, bf16[128,256]{1,0:T(8,128)(2,1)S(1)}, u32[]{:S(2)}, u32[]{:S(2)}) collective-permute-start(bf16[128,256]{1,0:T(8,128)(2,1)S(1)} %get-tuple-element.52), channel_id=1, source_target_pairs={{8,0},{12,4},{16,8},{20,12},{24,16},{28,20},{32,24},{36,28},{40,32... | collective-permute-start | bytes 196616 | tf_op jit(solution)/shard_map/ppermute | solution.py:219
  84.3 0.0 collective-permute-done.8.refs_1_
  84.3 4.9 %collective-permute-start.13 = (bf16[128,256]{1,0:T(8,128)(2,1)S(1)}, bf16[128,256]{1,0:T(8,128)(2,1)S(1)}, u32[]{:S(2)}, u32[]{:S(2)}) collective-permute-start(bf16[128,256]{1,0:T(8,128)(2,1)S(1)} %get-tuple-element.53), channel_id=1, source_target_pairs={{4,0},{8,4},{12,8},{16,12},{20,16},{24,20},{28,24},{32,28},{36,32}... | collective-permute-start | bytes 196616 | tf_op jit(solution)/shard_map/ppermute | solution.py:219
  89.2 1.1 %shard_map.133 = (bf16[128,128]{1,0:T(8,128)(2,1)}, bf16[128,128]{1,0:T(8,128)(2,1)}, bf16[128,128]{1,0:T(8,128)(2,1)}, f32[128,256]{1,0:T(8,128)S(1)}) custom-call(bf16[256,128]{1,0:T(8,128)(2,1)S(1)} %get-tuple-element.42.grads_ref, f32[256,128]{1,0:T(8,128)S(1)} %get-tuple-element.43.before_ref, bf16[256,128]{1,0:T(8,128)(2,1)S(1)} %get-tuple-element.31.heads_ref, ...), custom_call_target="tpu_custom_call" | custom-call | tf_op jit(solution)/shard_map/pallas_call | solution.py:206
  90.4 0.0 collective-permute-done.9.refs_2_
  90.4 0.0 collective-permute-done.10.refs_3_
  90.4 0.0 collective-permute-done.11.refs_4_
  90.4 0.0 collective-permute-done.12.refs_5_
  90.4 1.2 %collective-permute-done.13.refs_6_ = bf16[128,256]{1,0:T(8,128)(2,1)S(1)} collective-permute-done((bf16[128,256]{1,0:T(8,128)(2,1)S(1)}, bf16[128,256]{1,0:T(8,128)(2,1)S(1)}, u32[]{:S(2)}, u32[]{:S(2)}) %collective-permute-start.13) | collective-permute-done | bytes 65568 | tf_op jit(solution)/shard_map/ppermute | solution.py:219
  91.6 0.7 shard_map.134
  (6 shorter events, 0.0 us)
Async XLA Ops:
  2.1 37.6 %collective-permute-start.4 = (bf16[144,256]{1,0:T(8,128)(2,1)}, bf16[144,256]{1,0:T(8,128)(2,1)S(1)}, u32[]{:S(2)}, u32[]{:S(2)}) collective-permute-start(bf16[144,256]{1,0:T(8,128)(2,1)} %get-tuple-element.37.packet_ref.refs_0_.packet), channel_id=1, source_target_pairs={{0,64},{4,68},{8,72},{12,76},{16,80},{20,84},{24,88},{28,92},{32,9... | collective-permute-start | bytes 221192 | tf_op jit(solution)/shard_map/ppermute | solution.py:219
  17.5 23.6 %collective-permute-start.3 = (bf16[144,256]{1,0:T(8,128)(2,1)}, bf16[144,256]{1,0:T(8,128)(2,1)S(1)}, u32[]{:S(2)}, u32[]{:S(2)}) collective-permute-start(bf16[144,256]{1,0:T(8,128)(2,1)} %get-tuple-element.37.packet_ref.refs_0_.packet), channel_id=1, source_target_pairs={{0,32},{4,36},{8,40},{12,44},{16,48},{20,52},{24,56},{28,60},{32,6... | collective-permute-start | bytes 221192 | tf_op jit(solution)/shard_map/ppermute | solution.py:219
  21.6 17.2 %all-to-all-start = ((f32[32,1,128]{2,1,0:T(1,128)}), f32[32,1,128]{2,1,0:T(1,128)S(1)}, u32[]{:S(2)}, u32[]{:S(2)}) async-start(f32[32,1,128]{2,1,0:T(1,128)} %get-tuple-element.36), calls=%async_computation | async-start | bytes 32768 | tf_op jit(solution)/shard_map/all_to_all | solution.py:248
  26.3 16.5 %collective-permute-start.2 = (bf16[144,256]{1,0:T(8,128)(2,1)}, bf16[144,256]{1,0:T(8,128)(2,1)S(1)}, u32[]{:S(2)}, u32[]{:S(2)}) collective-permute-start(bf16[144,256]{1,0:T(8,128)(2,1)} %get-tuple-element.37.packet_ref.refs_0_.packet), channel_id=1, source_target_pairs={{0,16},{4,20},{8,24},{12,28},{16,32},{20,36},{24,40},{28,44},{32,4... | collective-permute-start | bytes 221192 | tf_op jit(solution)/shard_map/ppermute | solution.py:219
  30.5 12.2 %collective-permute-start.1 = (bf16[144,256]{1,0:T(8,128)(2,1)}, bf16[144,256]{1,0:T(8,128)(2,1)S(1)}, u32[]{:S(2)}, u32[]{:S(2)}) collective-permute-start(bf16[144,256]{1,0:T(8,128)(2,1)} %get-tuple-element.37.packet_ref.refs_0_.packet), channel_id=1, source_target_pairs={{0,8},{4,12},{8,16},{12,20},{16,24},{20,28},{24,32},{28,36},{32,40... | collective-permute-start | bytes 221192 | tf_op jit(solution)/shard_map/ppermute | solution.py:219
  33.6 9.2 %collective-permute-start = (bf16[144,256]{1,0:T(8,128)(2,1)}, bf16[144,256]{1,0:T(8,128)(2,1)S(1)}, u32[]{:S(2)}, u32[]{:S(2)}) collective-permute-start(bf16[144,256]{1,0:T(8,128)(2,1)} %get-tuple-element.37.packet_ref.refs_0_.packet), channel_id=1, source_target_pairs={{0,4},{4,8},{8,12},{12,16},{16,20},{20,24},{24,28},{28,32},{32,36}... | collective-permute-start | bytes 221192 | tf_op jit(solution)/shard_map/ppermute | solution.py:219
  38.8 0.9 copy-start
  39.6 2.8 %copy-start.2 = (bf16[128,128]{1,0:T(8,128)(2,1)S(1)}, bf16[128,128]{1,0:T(8,128)(2,1)}, u32[]{:S(2)}) copy-start(bf16[128,128]{1,0:T(8,128)(2,1)} %gate_ref.3) | copy-start | bytes 98308
  39.6 2.8 %copy-start.3 = (bf16[128,128]{1,0:T(8,128)(2,1)S(1)}, bf16[128,128]{1,0:T(8,128)(2,1)}, u32[]{:S(2)}) copy-start(bf16[128,128]{1,0:T(8,128)(2,1)} %cot_ref.3) | copy-start | bytes 98308
  39.6 2.9 %copy-start.4 = (bf16[128,128]{1,0:T(8,128)(2,1)S(1)}, bf16[128,128]{1,0:T(8,128)(2,1)}, u32[]{:S(2)}) copy-start(bf16[128,128]{1,0:T(8,128)(2,1)} %query_ref.1) | copy-start | bytes 98308
  39.7 2.9 %copy-start.5 = (s32[128,8]{0,1:T(8,128)S(1)}, s32[128,8]{0,1:T(8,128)}, u32[]{:S(2)}) copy-start(s32[128,8]{0,1:T(8,128)} %param.15) | copy-start | bytes 12292
  39.7 2.9 %copy-start.6 = (f32[128]{0:T(128)S(1)}, f32[128]{0:T(128)}, u32[]{:S(2)}) copy-start(f32[128]{0:T(128)} %param.17) | copy-start | bytes 1540
  39.7 2.9 %copy-start.7 = (f32[2,16]{1,0:T(2,128)S(1)}, f32[2,16]{1,0:T(2,128)}, u32[]{:S(2)}) copy-start(f32[2,16]{1,0:T(2,128)} %table_ref.1) | copy-start | bytes 388
  39.7 10.1 %copy-start.1 = (bf16[144,256]{1,0:T(8,128)(2,1)S(1)}, bf16[144,256]{1,0:T(8,128)(2,1)}, u32[]{:S(2)}) copy-start(bf16[144,256]{1,0:T(8,128)(2,1)} %get-tuple-element.37.packet_ref.refs_0_.packet) | copy-start | bytes 221188
  39.7 7.2 %collective-permute-start.6 = (bf16[144,256]{1,0:T(8,128)(2,1)S(1)}, bf16[144,256]{1,0:T(8,128)(2,1)S(1)}, u32[]{:S(2)}, u32[]{:S(2)}) collective-permute-start(bf16[144,256]{1,0:T(8,128)(2,1)S(1)} %shard_map.130), channel_id=1, source_target_pairs={{0,128},{4,132},{8,136},{12,140},{16,144},{20,148},{24,152},{28,15... | collective-permute-start | bytes 221192 | tf_op jit(solution)/shard_map/ppermute | solution.py:219
  41.2 8.6 %collective-permute-start.5 = (bf16[144,256]{1,0:T(8,128)(2,1)S(1)}, bf16[144,256]{1,0:T(8,128)(2,1)S(1)}, u32[]{:S(2)}, u32[]{:S(2)}) collective-permute-start(bf16[144,256]{1,0:T(8,128)(2,1)S(1)} %shard_map.130), channel_id=1, source_target_pairs={{0,256},{4,260},{8,264},{12,268},{16,272},{20,276},{24,280},{28,28... | collective-permute-start | bytes 221192 | tf_op jit(solution)/shard_map/ppermute | solution.py:219
  60.9 20.8 %collective-permute-start.7 = (bf16[128,256]{1,0:T(8,128)(2,1)S(1)}, bf16[128,256]{1,0:T(8,128)(2,1)S(1)}, u32[]{:S(2)}, u32[]{:S(2)}) collective-permute-start(bf16[128,256]{1,0:T(8,128)(2,1)S(1)} %get-tuple-element.47), channel_id=1, source_target_pairs={{64,0},{68,4},{72,8},{76,12},{80,16},{84,20},{88,24},{92,28},{96,3... | collective-permute-start | bytes 196616 | tf_op jit(solution)/shard_map/ppermute | solution.py:219
  69.8 14.5 %collective-permute-start.8 = (bf16[128,256]{1,0:T(8,128)(2,1)S(1)}, bf16[128,256]{1,0:T(8,128)(2,1)S(1)}, u32[]{:S(2)}, u32[]{:S(2)}) collective-permute-start(bf16[128,256]{1,0:T(8,128)(2,1)S(1)} %get-tuple-element.48), channel_id=1, source_target_pairs={{256,0},{260,4},{264,8},{268,12},{272,16},{276,20},{280,24},{284,2... | collective-permute-start | bytes 196616 | tf_op jit(solution)/shard_map/ppermute | solution.py:219
  71.6 18.8 %collective-permute-start.9 = (bf16[128,256]{1,0:T(8,128)(2,1)S(1)}, bf16[128,256]{1,0:T(8,128)(2,1)S(1)}, u32[]{:S(2)}, u32[]{:S(2)}) collective-permute-start(bf16[128,256]{1,0:T(8,128)(2,1)S(1)} %get-tuple-element.49), channel_id=1, source_target_pairs={{32,0},{36,4},{40,8},{44,12},{48,16},{52,20},{56,24},{60,28},{64,3... | collective-permute-start | bytes 196616 | tf_op jit(solution)/shard_map/ppermute | solution.py:219
  77.5 12.8 %collective-permute-start.10 = (bf16[128,256]{1,0:T(8,128)(2,1)S(1)}, bf16[128,256]{1,0:T(8,128)(2,1)S(1)}, u32[]{:S(2)}, u32[]{:S(2)}) collective-permute-start(bf16[128,256]{1,0:T(8,128)(2,1)S(1)} %get-tuple-element.50), channel_id=1, source_target_pairs={{128,0},{132,4},{136,8},{140,12},{144,16},{148,20},{152,24},{156,2... | collective-permute-start | bytes 196616 | tf_op jit(solution)/shard_map/ppermute | solution.py:219
  78.8 11.5 %collective-permute-start.11 = (bf16[128,256]{1,0:T(8,128)(2,1)S(1)}, bf16[128,256]{1,0:T(8,128)(2,1)S(1)}, u32[]{:S(2)}, u32[]{:S(2)}) collective-permute-start(bf16[128,256]{1,0:T(8,128)(2,1)S(1)} %get-tuple-element.51), channel_id=1, source_target_pairs={{16,0},{20,4},{24,8},{28,12},{32,16},{36,20},{40,24},{44,28},{48,3... | collective-permute-start | bytes 196616 | tf_op jit(solution)/shard_map/ppermute | solution.py:219
  81.8 8.6 %collective-permute-start.12 = (bf16[128,256]{1,0:T(8,128)(2,1)S(1)}, bf16[128,256]{1,0:T(8,128)(2,1)S(1)}, u32[]{:S(2)}, u32[]{:S(2)}) collective-permute-start(bf16[128,256]{1,0:T(8,128)(2,1)S(1)} %get-tuple-element.52), channel_id=1, source_target_pairs={{8,0},{12,4},{16,8},{20,12},{24,16},{28,20},{32,24},{36,28},{40,32... | collective-permute-start | bytes 196616 | tf_op jit(solution)/shard_map/ppermute | solution.py:219
  84.3 7.3 %collective-permute-start.13 = (bf16[128,256]{1,0:T(8,128)(2,1)S(1)}, bf16[128,256]{1,0:T(8,128)(2,1)S(1)}, u32[]{:S(2)}, u32[]{:S(2)}) collective-permute-start(bf16[128,256]{1,0:T(8,128)(2,1)S(1)} %get-tuple-element.53), channel_id=1, source_target_pairs={{4,0},{8,4},{12,8},{16,12},{20,16},{24,20},{28,24},{32,28},{36,32}... | collective-permute-start | bytes 196616 | tf_op jit(solution)/shard_map/ppermute | solution.py:219
